TPU v7x, 32 devices: a whole 2x2x4 slice. The times are simulated.
32 devices in a mesh: vel: 4 (over y, core), sx: 4 (over z), sy: 2 (over x).
Axes of the slice: x: 2, y: 2, z: 4, core: 2. Of those that a mesh axis runs over, the one named last changes fastest.
Arguments:
- scaled_population_table: float32 [32, 16, 32768], P('sx', 'sy', 'vel'), may hold values from 0 to 8, as said below
Outputs:
- advanced: float32 [32, 16, 32768], P('sx', 'sy', 'vel')
Inputs may be any that keep to these rules, and one draw needn't show every extreme that they name: `scaled_population_table`: every entry is positive.
All inputs are finite; a program needn't handle non-finite values.
Results may differ from a plain program's by a relative error of at most 0.0003.
Values sent between devices are 32-bit elements; how exact they have to be, the bound alone decides.
No kernel may reach another device: no remote copies, remote signals or barrier semaphores. Data moves between devices by JAX's collectives and lax.ppermute only.
A program may use at most 64 MiB of HBM per device.

v0:
```python
import math

import jax
import jax.numpy as jnp
from jax import lax
from jax.sharding import PartitionSpec as P

KV = 32


vel_bound = 4.5
time_step = 0.25 / 4.5
baseline_collision_interval = 0.25
power_law_index = 0.81
diffusivity_ratio_coefficient = 2.0 / 3.0
highest = lax.Precision.HIGHEST


def extended(array, sides, width):
    for axis, dim in sides:
        peers, length = (lax.axis_size(axis), array.shape[dim])
        up = [(i, (i + 1) % peers) for i in range(peers)]
        down = [(j, i) for i, j in up]
        last = lax.slice_in_dim(array, length - width, length, axis=dim)
        initial = lax.slice_in_dim(array, 0, width, axis=dim)
        before = lax.ppermute(last, axis, up)
        after = lax.ppermute(initial, axis, down)
        array = jnp.concatenate([before, array, after], axis=dim)
    return array


def velocity_table(vel_index):
    levels = (vel_index // (KV * KV), vel_index // KV % KV, vel_index % KV)
    return tuple(
        ((2 * one_level + 1 - KV).astype(jnp.float32) * (vel_bound / KV) for one_level in levels)
    )


def quad_weight():
    return (2.0 * vel_bound / KV) ** 3 * (2.0 * math.pi) ** (-1.5)


def minmod(former, latter):
    return (
        0.5 * (jnp.sign(former) + jnp.sign(latter)) * jnp.minimum(jnp.abs(former), jnp.abs(latter))
    )


def flux_change(padded, velocity, along_axis):
    length = padded.shape[along_axis]
    behind = lax.slice_in_dim(padded, 0, length - 2, axis=along_axis)
    middle = lax.slice_in_dim(padded, 1, length - 1, axis=along_axis)
    ahead_cell = lax.slice_in_dim(padded, 2, length, axis=along_axis)
    slopes = minmod(middle - behind, ahead_cell - middle)
    face_low = lax.slice_in_dim(middle + 0.5 * slopes, 0, length - 3, axis=along_axis)
    face_high = lax.slice_in_dim(middle - 0.5 * slopes, 1, length - 2, axis=along_axis)
    fluxes = jnp.maximum(velocity, 0.0) * face_low + jnp.minimum(velocity, 0.0) * face_high
    return lax.slice_in_dim(fluxes, 1, length - 3, axis=along_axis) - lax.slice_in_dim(
        fluxes, 0, length - 4, axis=along_axis
    )


def surround(field):
    return extended(field, (("sx", 0), ("sy", 1)), 2)


def project(flattened, moment_basis):
    return lax.dot_general(flattened, moment_basis, (((1,), (1,)), ((), ())), precision=highest)


def cell_moment_values(inner_cells, particle_speeds, quadrature_weight):
    cells_x, cells_y, vel_count = inner_cells.shape
    flattened = inner_cells.reshape(cells_x * cells_y, vel_count)
    squares = (
        particle_speeds[0] * particle_speeds[0]
        + particle_speeds[1] * particle_speeds[1]
        + particle_speeds[2] * particle_speeds[2]
    )
    moment_basis = jnp.stack(
        [
            jnp.ones_like(particle_speeds[0]),
            particle_speeds[0],
            particle_speeds[1],
            particle_speeds[2],
            particle_speeds[0] * particle_speeds[0],
            particle_speeds[1] * particle_speeds[1],
            particle_speeds[2] * particle_speeds[2],
            particle_speeds[0] * particle_speeds[1],
            particle_speeds[0] * particle_speeds[2],
            particle_speeds[1] * particle_speeds[2],
            particle_speeds[0] * squares,
            particle_speeds[1] * squares,
            particle_speeds[2] * squares,
        ]
    )
    partial_sums = project(flattened, moment_basis) * quadrature_weight
    integrated_sums_list = lax.psum(partial_sums, "vel").reshape(cells_x, cells_y, 13)
    local_matter_amount = integrated_sums_list[..., 0:1]
    bulk_flow_components = tuple(
        (
            integrated_sums_list[..., column : column + 1] / local_matter_amount
            for column in (1, 2, 3)
        )
    )
    bulk_flow_norm_square = (
        bulk_flow_components[0] * bulk_flow_components[0]
        + bulk_flow_components[1] * bulk_flow_components[1]
        + bulk_flow_components[2] * bulk_flow_components[2]
    )
    energy_sum = (
        integrated_sums_list[..., 4:5]
        + integrated_sums_list[..., 5:6]
        + integrated_sums_list[..., 6:7]
    )
    kinetic_warmth_level = (energy_sum / local_matter_amount - bulk_flow_norm_square) / 3.0
    stress_rows = ((4, 7, 8), (7, 5, 9), (8, 9, 6))
    heat_list = []
    for column in range(3):
        row_cols = stress_rows[column]
        stress_dot = (
            integrated_sums_list[..., row_cols[0] : row_cols[0] + 1] * bulk_flow_components[0]
            + integrated_sums_list[..., row_cols[1] : row_cols[1] + 1] * bulk_flow_components[1]
            + integrated_sums_list[..., row_cols[2] : row_cols[2] + 1] * bulk_flow_components[2]
        )
        heat_list.append(
            0.5
            * (
                integrated_sums_list[..., 10 + column : 11 + column]
                - 2.0 * stress_dot
                - bulk_flow_components[column] * energy_sum
                + 2.0 * local_matter_amount * bulk_flow_components[column] * bulk_flow_norm_square
            )
        )
    energy_current_triple = tuple(heat_list)
    neighbour_displacement_list = [
        particle_speeds[column] - bulk_flow_components[column] for column in range(3)
    ]
    velocity_dispersion_width = (
        neighbour_displacement_list[0] * neighbour_displacement_list[0]
        + neighbour_displacement_list[1] * neighbour_displacement_list[1]
        + neighbour_displacement_list[2] * neighbour_displacement_list[2]
    )
    return (
        local_matter_amount,
        kinetic_warmth_level,
        energy_current_triple,
        neighbour_displacement_list,
        velocity_dispersion_width,
    )


def advance_section(padded, particle_speeds, quadrature_weight):
    inner_cells = padded[2:-2, 2:-2]
    (
        local_matter_amount,
        kinetic_warmth_level,
        energy_current_triple,
        neighbour_displacement_list,
        velocity_dispersion_width,
    ) = cell_moment_values(inner_cells, particle_speeds, quadrature_weight)
    collision_rate_coefficient = (
        local_matter_amount
        * kinetic_warmth_level ** (1.0 - power_law_index)
        / baseline_collision_interval
    )
    gaussian_rest_profile = (
        local_matter_amount
        * kinetic_warmth_level ** (-1.5)
        * jnp.exp(-velocity_dispersion_width / (2.0 * kinetic_warmth_level))
    )
    directional_energy_current = (
        neighbour_displacement_list[0] * energy_current_triple[0]
        + neighbour_displacement_list[1] * energy_current_triple[1]
        + neighbour_displacement_list[2] * energy_current_triple[2]
    )
    shakhov_attractor_profile = gaussian_rest_profile * (
        1.0
        + (1.0 - diffusivity_ratio_coefficient)
        * directional_energy_current
        / (5.0 * local_matter_amount * kinetic_warmth_level * kinetic_warmth_level)
        * (velocity_dispersion_width / kinetic_warmth_level - 5.0)
    )
    transport = flux_change(padded[:, 2:-2], particle_speeds[0], 0) + flux_change(
        padded[2:-2, :], particle_speeds[1], 1
    )
    return inner_cells + time_step * (
        collision_rate_coefficient * (shakhov_attractor_profile - inner_cells) - transport
    )


def local(scaled_population_table):
    vel_count = scaled_population_table.shape[2]
    vel_index = lax.axis_index("vel") * vel_count + jnp.arange(vel_count, dtype=jnp.int32)
    particle_speeds = velocity_table(vel_index)
    quadrature_weight = quad_weight()
    sectioned = advance_section(
        surround(scaled_population_table), particle_speeds, quadrature_weight
    )
    finished = advance_section(surround(sectioned), particle_speeds, quadrature_weight)
    return 0.5 * scaled_population_table + 0.5 * finished


def solution(mesh):
    return jax.shard_map(
        local,
        mesh=mesh,
        in_specs=(P("sx", "sy", "vel"),),
        out_specs=P("sx", "sy", "vel"),
        check_vma=False,
    )
```

profile of v0, /device:TPU:0, one launch (start us, length us, event | category | flops | bytes accessed | tf_op | source)
XLA Modules:
  0.0 173.2 jit_solution(1245936815307578550)
XLA Ops:
  0.0 2.4 %fusion.140 = (f32[2,8,8192]{2,1,0:T(8,128)}, f32[2,8,8192]{2,1,0:T(8,128)}) fusion(f32[8,8,8192]{2,1,0:T(8,128)} %param.1), kind=kLoop, calls=%fused_computation.243 | loop fusion | bytes 2097152 | tf_op jit(solution)/shard_map/slice | solution.py:25
  2.4 3.0 %collective-permute-start = (f32[2,8,8192]{2,1,0:T(8,128)}, f32[2,8,8192]{2,1,0:T(8,128)S(1)}, u32[]{:S(2)}, u32[]{:S(2)}) collective-permute-start(f32[2,8,8192]{2,1,0:T(8,128)} %get-tuple-element.32), channel_id=1, source_target_pairs={{0,2},{2,4},{4,6},{6,0},{1,3},{3,5},{5,7},{7,1},{8,10},{10,12},{12... | collective-permute-start | bytes 1572872 | tf_op jit(solution)/shard_map/ppermute | solution.py:26
  5.4 2.0 %collective-permute-start.1 = (f32[2,8,8192]{2,1,0:T(8,128)}, f32[2,8,8192]{2,1,0:T(8,128)}, u32[]{:S(2)}, u32[]{:S(2)}) collective-permute-start(f32[2,8,8192]{2,1,0:T(8,128)} %get-tuple-element.31), channel_id=1, source_target_pairs={{2,0},{4,2},{6,4},{0,6},{3,1},{5,3},{7,5},{1,7},{10,8},{12,10},{14... | collective-permute-start | bytes 1572872 | tf_op jit(solution)/shard_map/ppermute | solution.py:27
  9.2 1.2 fusion.132
  10.4 1.0 fusion.130
  11.4 1.2 fusion.126
  13.3 2.2 %stack.2 = f32[13,8192]{1,0:T(8,128)S(1)} concatenate(f32[1,8192]{1,0:T(1,128)} %broadcast.1391, f32[1,8192]{1,0:T(1,128)S(1)} %get-tuple-element.51, f32[1,8192]{1,0:T(1,128)S(1)} %get-tuple-element.49, f32[1,8192]{1,0:T(1,128)S(1)} %get-tuple-element.50, f32[1,8192]{1,0:T(1,128)S(1)} %get-tuple-element.59, f32[1,8192]{1,0:T(1,128)} %get-tuple-element.64, ...), dimensions={0} | concatenate | bytes 851968 | tf_op jit(solution)/shard_map/stack | solution.py:79
  15.5 1.7 fusion.61
  17.3 12.1 %psum.14 = f32[8,8,13]{1,0,2:T(8,128)S(1)} all-reduce(f32[8,8,13]{1,0,2:T(8,128)S(1)} %reshape.306), channel_id=1, replica_groups=mesh['vel'=4,'sx'=4,'sy'=2] {'vel'}, use_global_device_ids=true, to_apply=%region_0.1 | all-reduce | flops 832 | bytes 6656 | tf_op jit(solution)/shard_map/psum | solution.py:97
  29.7 0.6 collective-permute-done.1
  30.4 1.1 constant_dynamic-update-slice_fusion
  31.4 0.7 fusion.138
  32.6 1.6 collective-permute-start.3
  35.3 3.0 %fusion.137 = (f32[10,8,8192]{2,1,0:T(8,128)S(1)}, f32[10,8,8192]{2,1,0:T(8,128)S(1)}) fusion(f32[12,8,8192]{2,1,0:T(8,128)S(1)} %constant_dynamic-update-slice_fusion, f32[2,8,8192]{2,1,0:T(8,128)} %collective-permute-done.1, f32[8,8,8192]{2,1,0:T(8,128)S(1)} %copy-done, f32[2,8,8192]{2,1,0:T(8,128)S(1)} %collective-permute-done), kind=kLoop, calls=%fused_computation.240 | loop fusion | flops 8519680 | bytes 11010048 | tf_op jit(solution)/shard_map/slice | solution.py:52
  38.7 20.1 %collective-permute-done.3 = f32[12,2,8192]{2,0,1:T(8,128)S(1)} collective-permute-done((f32[12,2,8192]{2,0,1:T(8,128)S(1)}, f32[12,2,8192]{2,0,1:T(8,128)S(1)}, u32[]{:S(2)}, u32[]{:S(2)}) %collective-permute-start.3) | collective-permute-done | bytes 786464 | tf_op jit(solution)/shard_map/ppermute | solution.py:27
  59.4 20.2 %collective-permute-done.2 = f32[12,2,8192]{2,0,1:T(8,128)S(1)} collective-permute-done((f32[12,2,8192]{2,0,1:T(8,128)S(1)}, f32[12,2,8192]{2,0,1:T(8,128)S(1)}, u32[]{:S(2)}, u32[]{:S(2)}) %collective-permute-start.2) | collective-permute-done | bytes 786464 | tf_op jit(solution)/shard_map/ppermute | solution.py:26
  80.2 5.0 %pad_maximum_fusion.12 = (f32[8,10,8192]{2,1,0:T(8,128)S(1)}, f32[8,10,8192]{2,1,0:T(8,128)S(1)}) fusion(f32[12,2,8192]{2,1,0:T(2,128)S(1)} %copy.36, f32[12,8,8192]{2,1,0:T(8,128)S(1)} %constant_dynamic-update-slice_fusion, f32[12,2,8192]{2,1,0:T(2,128)S(1)} %copy.35), kind=kLoop, calls=%fused_computation.26 | loop fusion | flops 9830400 | bytes 9961472 | tf_op jit(solution)/shard_map/concatenate | solution.py:28
  85.3 1.3 fusion.6
  86.9 3.0 %multiply_add_fusion = f32[8,8,8192]{2,1,0:T(8,128)S(1)} fusion(f32[8,8,8192]{2,1,0:T(8,128)S(1)} %copy-done.1, f32[8,9,8192]{2,1,0:T(8,128)S(1)} %fusion.6, f32[9,8,8192]{2,1,0:T(8,128)S(1)} %fusion.14, f32[8,8]{1,0:T(8,128)S(1)} %get-tuple-element.45, f32[8,8]{1,0:T(8,128)S(1)} %get-tuple-element.42, f32[8,8]{1,0:T(8,128)S(1)} %get-tuple-element.37, ...), kind=kLoop, calls=%fused_computation.106 | loop fusion | flops 16252928 | bytes 12684032 | tf_op jit(solution)/shard_map/add | solution.py:186
  89.9 1.1 fusion.139
  90.9 1.7 fusion.64
  92.7 1.7 collective-permute-start.5
  94.8 11.2 %psum.15 = f32[8,8,13]{1,0,2:T(8,128)S(1)} all-reduce(f32[8,8,13]{1,0,2:T(8,128)S(1)} %reshape.308), channel_id=1, replica_groups=mesh['vel'=4,'sx'=4,'sy'=2] {'vel'}, use_global_device_ids=true, to_apply=%region_1.2 | all-reduce | flops 832 | bytes 6656 | tf_op jit(solution)/shard_map/psum | solution.py:97
  106.1 11.0 %collective-permute-done.5 = f32[2,8,8192]{2,1,0:T(8,128)S(1)} collective-permute-done((f32[2,8,8192]{2,1,0:T(8,128)}, f32[2,8,8192]{2,1,0:T(8,128)S(1)}, u32[]{:S(2)}, u32[]{:S(2)}) %collective-permute-start.5) | collective-permute-done | bytes 524320 | tf_op jit(solution)/shard_map/ppermute | solution.py:27
  117.1 0.7 pad_maximum_fusion.16
  118.3 1.6 collective-permute-start.7
  121.2 1.9 %fusion.136 = (f32[10,8,8192]{2,1,0:T(8,128)S(1)}, f32[10,8,8192]{2,1,0:T(8,128)S(1)}) fusion(f32[12,8,8192]{2,1,0:T(8,128)S(1)} %pad_maximum_fusion.14, f32[2,8,8192]{2,1,0:T(8,128)S(1)} %collective-permute-done.5, f32[8,8,8192]{2,1,0:T(8,128)S(1)} %multiply_add_fusion, f32[2,8,8192]{2,1,0:T(8,128)S(1)} %collective-permute-done.4), kind=kLoop, calls=%fused_computation.239 | loop fusion | flops 8519680 | bytes 11010048 | tf_op jit(solution)/shard_map/slice | solution.py:52
  123.5 20.9 %collective-permute-done.7 = f32[12,2,8192]{2,0,1:T(8,128)S(1)} collective-permute-done((f32[12,2,8192]{2,0,1:T(8,128)S(1)}, f32[12,2,8192]{2,0,1:T(8,128)S(1)}, u32[]{:S(2)}, u32[]{:S(2)}) %collective-permute-start.7) | collective-permute-done | bytes 786464 | tf_op jit(solution)/shard_map/ppermute | solution.py:27
  145.1 17.5 %collective-permute-done.6 = f32[12,2,8192]{2,0,1:T(8,128)S(1)} collective-permute-done((f32[12,2,8192]{2,0,1:T(8,128)S(1)}, f32[12,2,8192]{2,0,1:T(8,128)S(1)}, u32[]{:S(2)}, u32[]{:S(2)}) %collective-permute-start.6) | collective-permute-done | bytes 786464 | tf_op jit(solution)/shard_map/ppermute | solution.py:26
  163.2 4.6 %pad_maximum_fusion.6 = (f32[8,10,8192]{2,1,0:T(8,128)S(1)}, f32[8,10,8192]{2,1,0:T(8,128)S(1)}) fusion(f32[12,2,8192]{2,1,0:T(2,128)S(1)} %copy.42, f32[12,2,8192]{2,1,0:T(2,128)S(1)} %copy.41, f32[2,8,8192]{2,1,0:T(8,128)S(1)} %collective-permute-done.5, f32[8,8,8192]{2,1,0:T(8,128)S(1)} %multiply_add_fusion, f32[2,8,8192]{2,1,0:T(8,128)S(1)} %collective-permute-done.4), kind=kLoop, calls=%fused_computation.13 | loop fusion | flops 13762560 | bytes 9961472 | tf_op jit(solution)/shard_map/concatenate | solution.py:28
  167.8 1.3 fusion.1
  169.4 3.8 %add_multiply_fusion = f32[8,8,8192]{2,1,0:T(8,128)} fusion(f32[8,8,8192]{2,1,0:T(8,128)S(1)} %copy-done.2, f32[8,8,8192]{2,1,0:T(8,128)S(1)} %multiply_add_fusion, f32[8,9,8192]{2,1,0:T(8,128)S(1)} %fusion.1, f32[9,8,8192]{2,1,0:T(8,128)S(1)} %fusion.11, f32[8,8]{1,0:T(8,128)S(1)} %get-tuple-element.43, f32[8,8]{1,0:T(8,128)S(1)} %get-tuple-element.40, ...), kind=kLoop, calls=%fused_computation.105 | loop fusion | flops 17301504 | bytes 14781184 | tf_op jit(solution)/shard_map/add | solution.py:200
  (40 shorter events, 10.3 us)
Async XLA Ops:
  0.0 15.5 %copy-start = (f32[8,8,8192]{2,1,0:T(8,128)S(1)}, f32[8,8,8192]{2,1,0:T(8,128)}, u32[]{:S(2)}) copy-start(f32[8,8,8192]{2,1,0:T(8,128)} %param.1) | copy-start | bytes 6291460
  2.4 27.1 %collective-permute-start = (f32[2,8,8192]{2,1,0:T(8,128)}, f32[2,8,8192]{2,1,0:T(8,128)S(1)}, u32[]{:S(2)}, u32[]{:S(2)}) collective-permute-start(f32[2,8,8192]{2,1,0:T(8,128)} %get-tuple-element.32), channel_id=1, source_target_pairs={{0,2},{2,4},{4,6},{6,0},{1,3},{3,5},{5,7},{7,1},{8,10},{10,12},{12... | collective-permute-start | bytes 1572872 | tf_op jit(solution)/shard_map/ppermute | solution.py:26
  5.4 24.9 %collective-permute-start.1 = (f32[2,8,8192]{2,1,0:T(8,128)}, f32[2,8,8192]{2,1,0:T(8,128)}, u32[]{:S(2)}, u32[]{:S(2)}) collective-permute-start(f32[2,8,8192]{2,1,0:T(8,128)} %get-tuple-element.31), channel_id=1, source_target_pairs={{2,0},{4,2},{6,4},{0,6},{3,1},{5,3},{7,5},{1,7},{10,8},{12,10},{14... | collective-permute-start | bytes 1572872 | tf_op jit(solution)/shard_map/ppermute | solution.py:27
  32.6 26.2 %collective-permute-start.3 = (f32[12,2,8192]{2,0,1:T(8,128)S(1)}, f32[12,2,8192]{2,0,1:T(8,128)S(1)}, u32[]{:S(2)}, u32[]{:S(2)}) collective-permute-start(f32[12,2,8192]{2,0,1:T(8,128)S(1)} %copy.34), channel_id=1, source_target_pairs={{1,0},{0,1},{3,2},{2,3},{5,4},{4,5},{7,6},{6,7},{9,8},{8,9},{11,10... | collective-permute-start | bytes 2359304 | tf_op jit(solution)/shard_map/ppermute | solution.py:27
  34.7 45.0 %collective-permute-start.2 = (f32[12,2,8192]{2,0,1:T(8,128)S(1)}, f32[12,2,8192]{2,0,1:T(8,128)S(1)}, u32[]{:S(2)}, u32[]{:S(2)}) collective-permute-start(f32[12,2,8192]{2,0,1:T(8,128)S(1)} %copy.33), channel_id=1, source_target_pairs={{0,1},{1,0},{2,3},{3,2},{4,5},{5,4},{6,7},{7,6},{8,9},{9,8},{10,11... | collective-permute-start | bytes 2359304 | tf_op jit(solution)/shard_map/ppermute | solution.py:26
  85.3 1.6 copy-start.1
  92.7 24.5 %collective-permute-start.5 = (f32[2,8,8192]{2,1,0:T(8,128)}, f32[2,8,8192]{2,1,0:T(8,128)S(1)}, u32[]{:S(2)}, u32[]{:S(2)}) collective-permute-start(f32[2,8,8192]{2,1,0:T(8,128)} %get-tuple-element.30), channel_id=1, source_target_pairs={{2,0},{4,2},{6,4},{0,6},{3,1},{5,3},{7,5},{1,7},{10,8},{12,10},{14... | collective-permute-start | bytes 1572872 | tf_op jit(solution)/shard_map/ppermute | solution.py:27
  94.4 22.8 %collective-permute-start.4 = (f32[2,8,8192]{2,1,0:T(8,128)}, f32[2,8,8192]{2,1,0:T(8,128)S(1)}, u32[]{:S(2)}, u32[]{:S(2)}) collective-permute-start(f32[2,8,8192]{2,1,0:T(8,128)} %get-tuple-element.29), channel_id=1, source_target_pairs={{0,2},{2,4},{4,6},{6,0},{1,3},{3,5},{5,7},{7,1},{8,10},{10,12},{12... | collective-permute-start | bytes 1572872 | tf_op jit(solution)/shard_map/ppermute | solution.py:26
  118.3 26.2 %collective-permute-start.7 = (f32[12,2,8192]{2,0,1:T(8,128)S(1)}, f32[12,2,8192]{2,0,1:T(8,128)S(1)}, u32[]{:S(2)}, u32[]{:S(2)}) collective-permute-start(f32[12,2,8192]{2,0,1:T(8,128)S(1)} %copy.40), channel_id=1, source_target_pairs={{1,0},{0,1},{3,2},{2,3},{5,4},{4,5},{7,6},{6,7},{9,8},{8,9},{11,10... | collective-permute-start | bytes 2359304 | tf_op jit(solution)/shard_map/ppermute | solution.py:27
  120.3 42.3 %collective-permute-start.6 = (f32[12,2,8192]{2,0,1:T(8,128)S(1)}, f32[12,2,8192]{2,0,1:T(8,128)S(1)}, u32[]{:S(2)}, u32[]{:S(2)}) collective-permute-start(f32[12,2,8192]{2,0,1:T(8,128)S(1)} %copy.39), channel_id=1, source_target_pairs={{0,1},{1,0},{2,3},{3,2},{4,5},{5,4},{6,7},{7,6},{8,9},{9,8},{10,11... | collective-permute-start | bytes 2359304 | tf_op jit(solution)/shard_map/ppermute | solution.py:26
  167.8 1.6 copy-start.2
where the time goes:
time: 174 us; the launch traced here: 173 us
  waiting for transfers between devices  90.5 us (52%)
  other arithmetic  31 us (18%)
  blocking collectives  23.3 us (13%)
  local copies, waits for them, and re-layouts  13.3 us (8%)
  starting transfers between devices  11.4 us (7%)
  matrix products  3.46 us (2%)
    ppermute x4, waiting for transfers between devices, extended(): after = lax.ppermute(initial, axis, down)  52.7 us
    ppermute x4, waiting for transfers between devices, extended(): before = lax.ppermute(last, axis, up)  37.8 us
    psum x2, blocking collectives, cell_moment_values(): lax.psum(partial_sums, 'vel').reshape(cells_x, cells_y, 13)  23.3 us
    concatenate x3, other arithmetic, extended(): array = jnp.concatenate([before, array, after], axis=dim)  9.84 us
    ppermute x4, starting transfers between devices, extended(): after = lax.ppermute(initial, axis, down)  6.85 us
    slice x2, other arithmetic, flux_change(): middle = lax.slice_in_dim(padded, 1, length - 1, axis=along_axis)  4.93 us
    ppermute x4, starting transfers between devices, extended(): before = lax.ppermute(last, axis, up)  4.56 us
    add x1, other arithmetic, local(): return 0.5 * scaled_population_table + 0.5 * finished  3.77 us
  transfers between devices with their start and end apart: 8, of which 6 were waited for; matrix products, arithmetic and copies ran while one was open for 11% of the time, Pallas kernels for 0%

commit v1 on v0

v1 whole, which is shorter than its diff:
```python
import functools
import math

import jax
import jax.numpy as jnp
from jax import lax
from jax.experimental import pallas as pl
from jax.experimental.pallas import tpu as pltpu
from jax.sharding import PartitionSpec as P

KV = 32
CHUNKS = 1
LANES = 128
ROWS = 8

vel_bound = 4.5
time_step = 0.25 / 4.5
collision_interval = 0.25
power_law_index = 0.81
diffusivity_ratio = 2.0 / 3.0
step = vel_bound / KV
weight = (2.0 * vel_bound / KV) ** 3 * (2.0 * math.pi) ** (-1.5)
f32 = jnp.float32

TILES = KV * KV // LANES
HALF = TILES // 2
PER_TILE = LANES // KV
SLOTS = LANES // ROWS


def limited(p, q):
    return jnp.maximum(jnp.minimum(p, jnp.maximum(q, 0.0)), jnp.minimum(q, 0.0))


def lane_index():
    return lax.broadcasted_iota(jnp.int32, (ROWS, LANES), 1)


def component(digit):
    return (2 * digit + 1 - KV).astype(f32) * step


def lane_components(tile):
    lane = lane_index()
    return component(tile * PER_TILE + lane // KV), component(lane % KV)


def changes(cells):
    out = []
    slope = cells[1] - cells[0]
    face = None
    for k in range(1, len(cells) - 1):
        ahead = cells[k + 1] - cells[k]
        new_face = cells[k] + 0.5 * limited(slope, ahead)
        if face is not None:
            out.append(new_face - face)
        slope, face = ahead, new_face
    return out


def send_x(source, tile, flow, primary, secondary):
    last = jnp.where(flow, 7, 0)
    before = jnp.where(flow, 6, 1)
    first = jnp.where(flow, 0, 7)
    row = lambda x: pl.ds(pl.multiple_of(x * ROWS, ROWS), ROWS)
    primary[tile, 0] = source[tile, row(before), :]
    primary[tile, 1] = source[tile, row(last), :]
    secondary[tile] = source[tile, row(first), :]


def send_y(source, pair, low, high, across):
    column = lambda tile, y: source[tile, pl.ds(y, ROWS, stride=ROWS), :]
    across[0, pair, 0] = column(high, 6)
    across[0, pair, 1] = column(high, 7)
    across[0, pair, 2] = column(low, 7)
    across[1, pair, 0] = column(low, 1)
    across[1, pair, 1] = column(low, 0)
    across[1, pair, 2] = column(high, 0)


def flow_of(vel_size, vel_name):
    return lax.axis_index(vel_name) >= vel_size // 2


def pack_kernel(vel_size, levels, table, cells, primary, secondary, across):
    flow = flow_of(vel_size, "vel")

    def one(i, carry):
        level, quarter = i // HALF, i % HALF
        low = level * TILES + quarter
        high = low + HALF
        for tile in (low, high):
            lanes = pl.ds(pl.multiple_of(tile * LANES, LANES), LANES)
            for x in range(ROWS):
                cells[tile, x * ROWS : (x + 1) * ROWS, :] = table[x, :, lanes]
            send_x(cells, tile, flow, primary, secondary)
        send_y(cells, i, low, high, across)
        return carry

    lax.fori_loop(0, levels * HALF, one, 0)


def sums_kernel(levels, all_levels, first_level, cells, *rest):
    sums = rest[-1]
    lane = lane_index()
    base = lax.axis_index("vel") * all_levels + first_level
    speed = [component(base + level) for level in range(levels)]

    def one(x, total):
        acc = [jnp.zeros((ROWS, LANES), f32) for _ in range(13)]
        row = pl.ds(pl.multiple_of(x * ROWS, ROWS), ROWS)
        for tile in range(TILES):
            cb, ce = lane_components(tile)
            m0 = m1 = m2 = m3 = None
            for level in range(levels):
                g = cells[level * TILES + tile, row, :]
                g1 = g * speed[level]
                g2 = g1 * speed[level]
                g3 = g2 * speed[level]
                if level == 0:
                    m0, m1, m2, m3 = g, g1, g2, g3
                else:
                    m0, m1, m2, m3 = m0 + g, m1 + g1, m2 + g2, m3 + g3
            square = cb * cb + ce * ce
            b0 = cb * m0
            e0 = ce * m0
            terms = (
                m0, m1, b0, e0, m2, cb * b0, ce * e0, cb * m1, ce * m1, cb * e0,
                m3 + square * m1, cb * m2 + square * b0, ce * m2 + square * e0,
            )
            acc = [a + t for a, t in zip(acc, terms)]
        for m in range(13):
            total = jnp.where(lane == x * SLOTS + m, jnp.sum(acc[m], axis=1, keepdims=True), total)
        return total

    total = lax.fori_loop(0, ROWS, one, jnp.zeros((ROWS, LANES), f32))
    for other in rest[:-1]:
        total = total + other[...]
    sums[...] = total


def tables(parts, levels, base, scale, tab_b, tab_a, keep):
    sums = parts[0][...]
    for part in parts[1:]:
        sums = sums + part[...]
    sums = sums * weight
    for x in range(ROWS):
        m = [
            jnp.broadcast_to(sums[:, x * SLOTS + i : x * SLOTS + i + 1], (ROWS, LANES))
            for i in range(13)
        ]
        n = m[0]
        inverse = 1.0 / n
        u = [m[i] * inverse for i in (1, 2, 3)]
        uu = u[0] * u[0] + u[1] * u[1] + u[2] * u[2]
        energy = m[4] + m[5] + m[6]
        temp = (energy * inverse - uu) * (1.0 / 3.0)
        rows = ((4, 7, 8), (7, 5, 9), (8, 9, 6))
        q = []
        for i in range(3):
            r = rows[i]
            stress = m[r[0]] * u[0] + m[r[1]] * u[1] + m[r[2]] * u[2]
            q.append(0.5 * (m[10 + i] - 2.0 * stress - u[i] * energy + 2.0 * n * u[i] * uu))
        log_temp = jnp.log(temp)
        rate = n * jnp.exp((1.0 - power_law_index) * log_temp) * (time_step / collision_interval)
        cold = 1.0 / temp
        half_cold = 0.5 * cold
        size = scale * rate * n * (cold * lax.rsqrt(temp))
        lift = (1.0 - diffusivity_ratio) / (5.0 * n * temp * temp)
        keep[x] = scale * (1.0 - rate)
        ql = [part * lift for part in q]
        for tile in range(TILES):
            cb, ce = lane_components(tile)
            db, de = cb - u[1], ce - u[2]
            square = db * db + de * de
            tab_b[x, tile, 0] = size * jnp.exp(-square * half_cold)
            tab_b[x, tile, 1] = db * ql[1] + de * ql[2]
            tab_b[x, tile, 2] = square * cold - 5.0
        for level in range(levels):
            da = component(base + level) - u[0]
            square = da * da
            tab_a[x, level, 0] = jnp.exp(-square * half_cold)
            tab_a[x, level, 1] = da * ql[0]
            tab_a[x, level, 2] = square * cold


def update_kernel(vel_size, levels, all_levels, first_level, parts_count, last, *refs):
    cells, from_x, from_x2, from_y = refs[:4]
    parts = refs[4 : 4 + parts_count]
    refs = refs[4 + parts_count :]
    if last:
        table, out, tab_b, tab_a, keep, side = refs
    else:
        out, primary, secondary, across, tab_b, tab_a, keep, side = refs
    scale = 0.5 if last else 1.0
    flow = flow_of(vel_size, "vel")
    base = lax.axis_index("vel") * all_levels + first_level
    tables(parts, levels, base, scale, tab_b, tab_a, keep)
    lane = lane_index()
    xs = [jnp.where(flow, k, ROWS - 1 - k) for k in range(ROWS)]

    def one(i, carry):
        level, quarter = i // HALF, i % HALF
        a_speed = jnp.abs(component(base + level)) * (time_step * scale)
        b_digit = quarter * PER_TILE + lane // KV
        for sign in (0, 1):
            sub = quarter + sign * HALF
            tile = level * TILES + sub
            b_speed = jnp.abs(component(b_digit + sign * (KV // 2))) * (time_step * scale)
            ys = range(ROWS) if sign else range(ROWS - 1, -1, -1)
            line = [from_y[1 - sign, i, 0], from_y[1 - sign, i, 1]]
            line += [cells[tile, pl.ds(y, ROWS, stride=ROWS), :] for y in ys]
            line += [from_y[sign, i, 2]]
            for y, change in zip(ys, changes(line)):
                side[sign, pl.ds(y, ROWS, stride=ROWS), :] = b_speed * change
            rows = [pl.ds(pl.multiple_of(x * ROWS, ROWS), ROWS) for x in xs]
            line = [from_x[tile, 0], from_x[tile, 1]]
            line += [cells[tile, row, :] for row in rows]
            line += [from_x2[tile]]
            for k, change in enumerate(changes(line)):
                x, row = xs[k], rows[k]
                source = tab_a[x, level, 0] * tab_b[x, sub, 0]
                bend = tab_a[x, level, 1] + tab_b[x, sub, 1]
                wide = tab_a[x, level, 2] + tab_b[x, sub, 2]
                new = line[k + 2] * keep[x] + (source + source * (bend * wide))
                new = new - (a_speed * change + side[sign, row, :])
                if last:
                    lanes = pl.ds(pl.multiple_of(tile * LANES, LANES), LANES)
                    out[x, :, lanes] = 0.5 * table[x, :, lanes] + new
                else:
                    out[tile, row, :] = new
            if not last:
                send_x(out, tile, flow, primary, secondary)
        if not last:
            low = level * TILES + quarter
            send_y(out, i, low, low + HALF, across)
        return carry

    lax.fori_loop(0, levels * HALF, one, 0)


def local(sizes, table):
    vel_size, sx_size, sy_size = sizes
    cells_x, cells_y, count = table.shape
    all_levels = count // (KV * KV)
    chunks = math.gcd(CHUNKS, all_levels)
    levels = all_levels // chunks
    assert cells_x == ROWS and cells_y == ROWS and vel_size % 2 == 0
    assert count == all_levels * KV * KV
    width = count // chunks
    tiles = levels * TILES
    shape = jax.ShapeDtypeStruct
    cells_shape = shape((tiles, ROWS * ROWS, LANES), f32)
    primary_shape = shape((tiles, 2, ROWS, LANES), f32)
    secondary_shape = shape((tiles, ROWS, LANES), f32)
    across_shape = shape((2, levels * HALF, 3, ROWS, LANES), f32)
    sums_shape = shape((ROWS, LANES), f32)
    message_shapes = (cells_shape, primary_shape, secondary_shape, across_shape)
    whole = pl.BlockSpec(memory_space=pltpu.VMEM)
    params = pltpu.CompilerParams(vmem_limit_bytes=40 * 1024 * 1024)
    half = vel_size // 2

    def along_x(array, sign):
        pairs = []
        for v in range(vel_size):
            way = sign if v >= half else -sign
            pairs += [(v * sx_size + i, v * sx_size + (i + way) % sx_size) for i in range(sx_size)]
        return lax.ppermute(array, ("vel", "sx"), pairs)

    def along_y(array):
        if sy_size == 2:
            return lax.ppermute(array, "sy", [(0, 1), (1, 0)])
        up = [(i, (i + 1) % sy_size) for i in range(sy_size)]
        down = [(j, i) for i, j in up]
        return jnp.stack([lax.ppermute(array[0], "sy", up), lax.ppermute(array[1], "sy", down)])

    def exchange(messages):
        primary, secondary, across = messages
        return along_x(primary, 1), along_x(secondary, -1), along_y(across)

    def gathered(sums):
        if vel_size > 4:
            return (lax.psum(sums, "vel"),)
        others = [
            lax.ppermute(sums, "vel", [(i, (i + k) % vel_size) for i in range(vel_size)])
            for k in range(1, vel_size)
        ]
        return (sums, *others)

    def piece(c):
        return pl.BlockSpec((ROWS, ROWS, width), lambda i, c=c: (0, 0, c))

    def pack(c):
        return pl.pallas_call(
            functools.partial(pack_kernel, vel_size, levels),
            grid=(1,),
            out_shape=message_shapes,
            in_specs=[piece(c)],
            out_specs=[whole] * 4,
            compiler_params=params,
            name="pack",
        )(table)

    def sums_of(c, cells, *earlier):
        return pl.pallas_call(
            functools.partial(sums_kernel, levels, all_levels, c * levels),
            out_shape=sums_shape,
            in_specs=[whole] * (1 + len(earlier)),
            out_specs=whole,
            compiler_params=params,
            name="sums",
        )(cells, *earlier)

    scratch = [
        pltpu.VMEM((ROWS, TILES, 3, ROWS, LANES), f32),
        pltpu.VMEM((ROWS, levels, 3, ROWS, LANES), f32),
        pltpu.VMEM((ROWS, ROWS, LANES), f32),
        pltpu.VMEM((2, ROWS * ROWS, LANES), f32),
    ]

    def advance(c, cells, messages, parts):
        return pl.pallas_call(
            functools.partial(
                update_kernel, vel_size, levels, all_levels, c * levels, len(parts), False
            ),
            out_shape=message_shapes,
            in_specs=[whole] * (4 + len(parts)),
            out_specs=[whole] * 4,
            scratch_shapes=scratch,
            compiler_params=params,
            name="advance",
        )(cells, *messages, *parts)

    def finish(c, cells, messages, parts):
        return pl.pallas_call(
            functools.partial(
                update_kernel, vel_size, levels, all_levels, c * levels, len(parts), True
            ),
            grid=(1,),
            out_shape=shape((ROWS, ROWS, width), f32),
            in_specs=[whole] * (4 + len(parts)) + [piece(c)],
            out_specs=whole,
            scratch_shapes=scratch,
            compiler_params=params,
            name="finish",
        )(cells, *messages, *parts, table)

    def all_sums(pieces):
        sums = ()
        for c, cells in enumerate(pieces):
            sums = (sums_of(c, cells, *sums),)
        return gathered(sums[0])

    packed = [pack(c) for c in range(chunks)]
    arrived = [exchange(p[1:]) for p in packed]
    parts = all_sums([p[0] for p in packed])
    staged = [advance(c, packed[c][0], arrived[c], parts) for c in range(chunks)]
    arrived = [exchange(s[1:]) for s in staged]
    parts = all_sums([s[0] for s in staged])
    done = [finish(c, staged[c][0], arrived[c], parts) for c in range(chunks)]
    return done[0] if chunks == 1 else jnp.concatenate(done, axis=2)


def solution(mesh):
    sizes = tuple(mesh.shape[name] for name in ("vel", "sx", "sy"))
    return jax.shard_map(
        functools.partial(local, sizes),
        mesh=mesh,
        in_specs=(P("sx", "sy", "vel"),),
        out_specs=P("sx", "sy", "vel"),
        check_vma=False,
    )
```

time: 174 us -> 54.2 us (0.31)
  waiting for transfers between devices: 90.5 us -> 22.6 us
  other arithmetic: 31 us -> 0 us
  blocking collectives: 23.3 us -> 0 us
  Pallas kernels: 0 us -> 12.9 us
  local copies, waits for them, and re-layouts: 13.3 us -> 1.59 us
  starting transfers between devices: 11.4 us -> 17 us
  matrix products: 3.46 us -> 0 us
    ppermute x8 -> x12, waiting for transfers between devices: 90.5 us -> 22.6 us  [the longest x4 19.6 us: along_x(): return lax.ppermute(array, ('vel', 'sx'), pairs)]
    psum x2 -> x0, blocking collectives: 23.3 us -> none  [cell_moment_values(): lax.psum(partial_sums, 'vel').reshape(cells_x, cells_y, 13)]
    pallas_call x0 -> x5, Pallas kernels: none -> 12.9 us  [the longest x1 5.19 us: finish(): pl.pallas_call(functools.partial(update_kernel, vel_size, levels, all_lev...]
    add x6 -> x0, other arithmetic: 10.2 us -> none  [the longest x1 3.77 us: local(): return 0.5 * scaled_population_table + 0.5 * finished]
    concatenate x3 -> x0, other arithmetic: 9.84 us -> none  [extended(): array = jnp.concatenate([before, array, after], axis=dim)]
    slice x7 -> x0, local copies, waits for them, and re-layouts: 6.01 us -> none  [the longest x3 3.32 us: extended(): initial = lax.slice_in_dim(array, 0, width, axis=dim)]
    slice x3 -> x0, other arithmetic: 5.65 us -> none  [the longest x2 4.93 us: flux_change(): middle = lax.slice_in_dim(padded, 1, length - 1, axis=along_axis)]
    ppermute x8 -> x12, starting transfers between devices: 11.4 us -> 17 us  [the longest x6 7.74 us: gathered(): lax.ppermute(sums, 'vel', [(i, (i + k) % vel_size) for i in range(vel_siz...]
  transfers between devices with their start and end apart: 8 -> 12, of which waited for: 6 -> 5; matrix products, arithmetic and copies ran while one was open for 11% -> 0% of each run, Pallas kernels for 0% -> 6%
where the time goes in v1:
time: 54.2 us; the launch traced here: 54.1 us
  waiting for transfers between devices  22.6 us (42%)
  starting transfers between devices  17 us (31%)
  Pallas kernels  12.9 us (24%)
  local copies, waits for them, and re-layouts  1.59 us (3%)
    ppermute x4, waiting for transfers between devices, along_x(): return lax.ppermute(array, ('vel', 'sx'), pairs)  19.6 us
    ppermute x6, starting transfers between devices, gathered(): lax.ppermute(sums, 'vel', [(i, (i + k) % vel_size) for i in range(vel_siz...  7.74 us
    ppermute x4, starting transfers between devices, along_x(): return lax.ppermute(array, ('vel', 'sx'), pairs)  5.63 us
    pallas_call x1, Pallas kernels, finish(): pl.pallas_call(functools.partial(update_kernel, vel_size, levels, all_lev...  5.19 us
    pallas_call x1, Pallas kernels, advance(): pl.pallas_call(functools.partial(update_kernel, vel_size, levels, all_lev...  3.78 us
    ppermute x2, starting transfers between devices, along_y(): return lax.ppermute(array, 'sy', [(0, 1), (1, 0)])  3.6 us
    pallas_call x2, Pallas kernels, sums_of(): pl.pallas_call(functools.partial(sums_kernel, levels, all_levels, c * lev...  3.06 us
    ppermute x6, waiting for transfers between devices, gathered(): lax.ppermute(sums, 'vel', [(i, (i + k) % vel_size) for i in range(vel_siz...  2.99 us
  transfers between devices with their start and end apart: 12, of which 5 were waited for; matrix products, arithmetic and copies ran while one was open for 0% of the time, Pallas kernels for 6%

profile of v1, /device:TPU:0, one launch (start us, length us, event | category | flops | bytes accessed | tf_op | source)
XLA Modules:
  0.0 54.1 jit_solution(10711069811985016185)
XLA Ops:
  0.0 0.0 copy-start
  0.0 1.6 %copy-done = f32[8,8,8192]{2,1,0:T(8,128)S(1)} copy-done((f32[8,8,8192]{2,1,0:T(8,128)S(1)}, f32[8,8,8192]{2,1,0:T(8,128)}, u32[]{:S(2)}) %copy-start) | copy-done | bytes 2097176
  1.6 0.9 %pack.1 = (f32[64,64,128]{2,1,0:T(8,128)S(1)}, f32[64,2,8,128]{3,2,1,0:T(8,128)S(1)}, f32[64,8,128]{2,1,0:T(8,128)S(1)}, f32[2,32,3,8,128]{4,3,2,1,0:T(8,128)S(1)}) custom-call(f32[8,8,8192]{2,1,0:T(8,128)S(1)} %copy-done), custom_call_target="tpu_custom_call" | custom-call | tf_op jit(solution)/shard_map/pack/pallas_call | solution.py:294
  2.5 3.0 %collective-permute-start.2 = (f32[2,32,3,8,128]{4,3,2,1,0:T(8,128)S(1)}, f32[2,32,3,8,128]{4,3,2,1,0:T(8,128)S(1)}, u32[]{:S(2)}, u32[]{:S(2)}) collective-permute-start(f32[2,32,3,8,128]{4,3,2,1,0:T(8,128)S(1)} %get-tuple-element.16), channel_id=1, source_target_pairs={{0,1},{1,0},{2,3},{3,2},{4,5},{5,4},{6,7},{7,6},{8,9},{9,8},{10,11... | collective-permute-start | bytes 2359304 | tf_op jit(solution)/shard_map/ppermute | solution.py:272
  5.5 3.6 %collective-permute-start = (f32[64,2,8,128]{3,2,1,0:T(8,128)S(1)}, f32[64,2,8,128]{3,2,1,0:T(8,128)S(1)}, u32[]{:S(2)}, u32[]{:S(2)}) collective-permute-start(f32[64,2,8,128]{3,2,1,0:T(8,128)S(1)} %get-tuple-element.14), channel_id=1, source_target_pairs={{0,6},{2,0},{4,2},{6,4},{8,14},{10,8},{12,10},{14,12},{16,18},{18,... | collective-permute-start | bytes 1572872 | tf_op jit(solution)/shard_map/ppermute | solution.py:268
  9.1 0.0 collective-permute-start.1
  9.1 1.5 %sums.2.refs_4_ = f32[8,128]{1,0:T(8,128)S(1)} custom-call(f32[64,64,128]{2,1,0:T(8,128)S(1)} %get-tuple-element.13.cells.refs_0_), custom_call_target="tpu_custom_call" | custom-call | tf_op jit(solution)/shard_map/sums/pallas_call | solution.py:305
  10.7 0.4 collective-permute-start.5
  11.1 1.4 %collective-permute-start.4 = (f32[8,128]{1,0:T(8,128)S(1)}, f32[8,128]{1,0:T(8,128)S(1)}, u32[]{:S(2)}, u32[]{:S(2)}) collective-permute-start(f32[8,128]{1,0:T(8,128)S(1)} %sums.2.refs_4_), channel_id=1, source_target_pairs={{0,16},{8,24},{16,0},{24,8},{1,17},{9,25},{17,1},{25,9},{2,18},{10... | collective-permute-start | bytes 12296 | tf_op jit(solution)/shard_map/ppermute | solution.py:285
  12.5 0.0 collective-permute-done.5.refs_7_
  12.5 1.6 %collective-permute-start.3 = (f32[8,128]{1,0:T(8,128)S(1)}, f32[8,128]{1,0:T(8,128)S(1)}, u32[]{:S(2)}, u32[]{:S(2)}) collective-permute-start(f32[8,128]{1,0:T(8,128)S(1)} %sums.2.refs_4_), channel_id=1, source_target_pairs={{0,8},{8,16},{16,24},{24,0},{1,9},{9,17},{17,25},{25,1},{2,10},{10... | collective-permute-start | bytes 12296 | tf_op jit(solution)/shard_map/ppermute | solution.py:285
  14.1 0.6 %collective-permute-done.4.refs_6_ = f32[8,128]{1,0:T(8,128)S(1)} collective-permute-done((f32[8,128]{1,0:T(8,128)S(1)}, f32[8,128]{1,0:T(8,128)S(1)}, u32[]{:S(2)}, u32[]{:S(2)}) %collective-permute-start.4) | collective-permute-done | bytes 4128 | tf_op jit(solution)/shard_map/ppermute | solution.py:285
  14.7 1.0 %collective-permute-done.3.refs_5_ = f32[8,128]{1,0:T(8,128)S(1)} collective-permute-done((f32[8,128]{1,0:T(8,128)S(1)}, f32[8,128]{1,0:T(8,128)S(1)}, u32[]{:S(2)}, u32[]{:S(2)}) %collective-permute-start.3) | collective-permute-done | bytes 4128 | tf_op jit(solution)/shard_map/ppermute | solution.py:285
  15.7 10.8 %collective-permute-done.1.refs_2_ = f32[64,8,128]{2,1,0:T(8,128)S(1)} collective-permute-done((f32[64,8,128]{2,1,0:T(8,128)S(1)}, f32[64,8,128]{2,1,0:T(8,128)S(1)}, u32[]{:S(2)}, u32[]{:S(2)}) %collective-permute-start.1) | collective-permute-done | bytes 262176 | tf_op jit(solution)/shard_map/ppermute | solution.py:268
  26.5 0.0 collective-permute-done.refs_1_
  26.5 0.0 collective-permute-done.2.refs_3_
  26.6 3.8 %advance.1 = (f32[64,64,128]{2,1,0:T(8,128)S(1)}, f32[64,2,8,128]{3,2,1,0:T(8,128)S(1)}, f32[64,8,128]{2,1,0:T(8,128)S(1)}, f32[2,32,3,8,128]{4,3,2,1,0:T(8,128)S(1)}) custom-call(f32[64,64,128]{2,1,0:T(8,128)S(1)} %get-tuple-element.13.cells.refs_0_, f32[64,2,8,128]{3,2,1,0:T(8,128)S(1)} %collective-permute-done.refs_1_, ...), custom_call_target="tpu_custom_call" | custom-call | tf_op jit(solution)/shard_map/advance/pallas_call | solution.py:322
  30.3 0.6 %collective-permute-start.8 = (f32[2,32,3,8,128]{4,3,2,1,0:T(8,128)S(1)}, f32[2,32,3,8,128]{4,3,2,1,0:T(8,128)S(1)}, u32[]{:S(2)}, u32[]{:S(2)}) collective-permute-start(f32[2,32,3,8,128]{4,3,2,1,0:T(8,128)S(1)} %get-tuple-element.20), channel_id=1, source_target_pairs={{0,1},{1,0},{2,3},{3,2},{4,5},{5,4},{6,7},{7,6},{8,9},{9,8},{10,11... | collective-permute-start | bytes 2359304 | tf_op jit(solution)/shard_map/ppermute | solution.py:272
  30.9 1.7 %collective-permute-start.6 = (f32[64,2,8,128]{3,2,1,0:T(8,128)S(1)}, f32[64,2,8,128]{3,2,1,0:T(8,128)S(1)}, u32[]{:S(2)}, u32[]{:S(2)}) collective-permute-start(f32[64,2,8,128]{3,2,1,0:T(8,128)S(1)} %get-tuple-element.18), channel_id=1, source_target_pairs={{0,6},{2,0},{4,2},{6,4},{8,14},{10,8},{12,10},{14,12},{16,18},{18,... | collective-permute-start | bytes 1572872 | tf_op jit(solution)/shard_map/ppermute | solution.py:268
  32.7 0.3 collective-permute-start.7
  33.0 1.5 %sums.3.refs_4_ = f32[8,128]{1,0:T(8,128)S(1)} custom-call(f32[64,64,128]{2,1,0:T(8,128)S(1)} %get-tuple-element.17.cells.refs_0_), custom_call_target="tpu_custom_call" | custom-call | tf_op jit(solution)/shard_map/sums/pallas_call | solution.py:305
  34.5 0.7 %collective-permute-start.11 = (f32[8,128]{1,0:T(8,128)S(1)}, f32[8,128]{1,0:T(8,128)S(1)}, u32[]{:S(2)}, u32[]{:S(2)}) collective-permute-start(f32[8,128]{1,0:T(8,128)S(1)} %sums.3.refs_4_), channel_id=1, source_target_pairs={{0,24},{8,0},{16,8},{24,16},{1,25},{9,1},{17,9},{25,17},{2,26},{10... | collective-permute-start | bytes 12296 | tf_op jit(solution)/shard_map/ppermute | solution.py:285
  35.2 1.9 %collective-permute-start.10 = (f32[8,128]{1,0:T(8,128)S(1)}, f32[8,128]{1,0:T(8,128)S(1)}, u32[]{:S(2)}, u32[]{:S(2)}) collective-permute-start(f32[8,128]{1,0:T(8,128)S(1)} %sums.3.refs_4_), channel_id=1, source_target_pairs={{0,16},{8,24},{16,0},{24,8},{1,17},{9,25},{17,1},{25,9},{2,18},{10... | collective-permute-start | bytes 12296 | tf_op jit(solution)/shard_map/ppermute | solution.py:285
  37.1 0.0 collective-permute-done.11.refs_7_
  37.1 1.6 %collective-permute-start.9 = (f32[8,128]{1,0:T(8,128)S(1)}, f32[8,128]{1,0:T(8,128)S(1)}, u32[]{:S(2)}, u32[]{:S(2)}) collective-permute-start(f32[8,128]{1,0:T(8,128)S(1)} %sums.3.refs_4_), channel_id=1, source_target_pairs={{0,8},{8,16},{16,24},{24,0},{1,9},{9,17},{17,25},{25,1},{2,10},{10... | collective-permute-start | bytes 12296 | tf_op jit(solution)/shard_map/ppermute | solution.py:285
  38.8 0.0 collective-permute-done.10.refs_6_
  38.8 1.4 %collective-permute-done.9.refs_5_ = f32[8,128]{1,0:T(8,128)S(1)} collective-permute-done((f32[8,128]{1,0:T(8,128)S(1)}, f32[8,128]{1,0:T(8,128)S(1)}, u32[]{:S(2)}, u32[]{:S(2)}) %collective-permute-start.9) | collective-permute-done | bytes 4128 | tf_op jit(solution)/shard_map/ppermute | solution.py:285
  40.2 8.7 %collective-permute-done.7.refs_2_ = f32[64,8,128]{2,1,0:T(8,128)S(1)} collective-permute-done((f32[64,8,128]{2,1,0:T(8,128)S(1)}, f32[64,8,128]{2,1,0:T(8,128)S(1)}, u32[]{:S(2)}, u32[]{:S(2)}) %collective-permute-start.7) | collective-permute-done | bytes 262176 | tf_op jit(solution)/shard_map/ppermute | solution.py:268
  48.9 0.0 collective-permute-done.6.refs_1_
  48.9 0.0 collective-permute-done.8.refs_3_
  48.9 0.0 copy-done.1
  48.9 5.2 %finish.1 = f32[8,8,8192]{2,1,0:T(8,128)} custom-call(f32[64,64,128]{2,1,0:T(8,128)S(1)} %get-tuple-element.17.cells.refs_0_, f32[64,2,8,128]{3,2,1,0:T(8,128)S(1)} %collective-permute-done.6.refs_1_, f32[64,8,128]{2,1,0:T(8,128)S(1)} %collective-permute-done.7.refs_2_, f32[2,32,3,8,128]{4,3,2,1,0:T(8,128)S(1)} %collective-permute-done.8.refs_3_, ...), custom_call_target="tpu_custom_call" | custom-call | tf_op jit(solution)/shard_map/finish/pallas_call | solution.py:335
  (1 shorter events, 0.0 us)
Async XLA Ops:
  0.0 1.6 %copy-start = (f32[8,8,8192]{2,1,0:T(8,128)S(1)}, f32[8,8,8192]{2,1,0:T(8,128)}, u32[]{:S(2)}) copy-start(f32[8,8,8192]{2,1,0:T(8,128)} %refs_8_.1) | copy-start | bytes 6291460
  2.5 24.0 %collective-permute-start.2 = (f32[2,32,3,8,128]{4,3,2,1,0:T(8,128)S(1)}, f32[2,32,3,8,128]{4,3,2,1,0:T(8,128)S(1)}, u32[]{:S(2)}, u32[]{:S(2)}) collective-permute-start(f32[2,32,3,8,128]{4,3,2,1,0:T(8,128)S(1)} %get-tuple-element.16), channel_id=1, source_target_pairs={{0,1},{1,0},{2,3},{3,2},{4,5},{5,4},{6,7},{7,6},{8,9},{9,8},{10,11... | collective-permute-start | bytes 2359304 | tf_op jit(solution)/shard_map/ppermute | solution.py:272
  5.5 21.0 %collective-permute-start = (f32[64,2,8,128]{3,2,1,0:T(8,128)S(1)}, f32[64,2,8,128]{3,2,1,0:T(8,128)S(1)}, u32[]{:S(2)}, u32[]{:S(2)}) collective-permute-start(f32[64,2,8,128]{3,2,1,0:T(8,128)S(1)} %get-tuple-element.14), channel_id=1, source_target_pairs={{0,6},{2,0},{4,2},{6,4},{8,14},{10,8},{12,10},{14,12},{16,18},{18,... | collective-permute-start | bytes 1572872 | tf_op jit(solution)/shard_map/ppermute | solution.py:268
  9.1 17.4 %collective-permute-start.1 = (f32[64,8,128]{2,1,0:T(8,128)S(1)}, f32[64,8,128]{2,1,0:T(8,128)S(1)}, u32[]{:S(2)}, u32[]{:S(2)}) collective-permute-start(f32[64,8,128]{2,1,0:T(8,128)S(1)} %get-tuple-element.15), channel_id=1, source_target_pairs={{0,2},{2,4},{4,6},{6,0},{8,10},{10,12},{12,14},{14,8},{16,22},{18,... | collective-permute-start | bytes 786440 | tf_op jit(solution)/shard_map/ppermute | solution.py:268
  10.7 38.3 %copy-start.1 = (f32[8,8,8192]{2,1,0:T(8,128)S(1)}, f32[8,8,8192]{2,1,0:T(8,128)}, u32[]{:S(2)}) copy-start(f32[8,8,8192]{2,1,0:T(8,128)} %refs_8_.1) | copy-start | bytes 6291460
  10.7 1.9 %collective-permute-start.5 = (f32[8,128]{1,0:T(8,128)S(1)}, f32[8,128]{1,0:T(8,128)S(1)}, u32[]{:S(2)}, u32[]{:S(2)}) collective-permute-start(f32[8,128]{1,0:T(8,128)S(1)} %sums.2.refs_4_), channel_id=1, source_target_pairs={{0,24},{8,0},{16,8},{24,16},{1,25},{9,1},{17,9},{25,17},{2,26},{10... | collective-permute-start | bytes 12296 | tf_op jit(solution)/shard_map/ppermute | solution.py:285
  11.1 3.6 %collective-permute-start.4 = (f32[8,128]{1,0:T(8,128)S(1)}, f32[8,128]{1,0:T(8,128)S(1)}, u32[]{:S(2)}, u32[]{:S(2)}) collective-permute-start(f32[8,128]{1,0:T(8,128)S(1)} %sums.2.refs_4_), channel_id=1, source_target_pairs={{0,16},{8,24},{16,0},{24,8},{1,17},{9,25},{17,1},{25,9},{2,18},{10... | collective-permute-start | bytes 12296 | tf_op jit(solution)/shard_map/ppermute | solution.py:285
  12.5 3.2 %collective-permute-start.3 = (f32[8,128]{1,0:T(8,128)S(1)}, f32[8,128]{1,0:T(8,128)S(1)}, u32[]{:S(2)}, u32[]{:S(2)}) collective-permute-start(f32[8,128]{1,0:T(8,128)S(1)} %sums.2.refs_4_), channel_id=1, source_target_pairs={{0,8},{8,16},{16,24},{24,0},{1,9},{9,17},{17,25},{25,1},{2,10},{10... | collective-permute-start | bytes 12296 | tf_op jit(solution)/shard_map/ppermute | solution.py:285
  30.3 18.6 %collective-permute-start.8 = (f32[2,32,3,8,128]{4,3,2,1,0:T(8,128)S(1)}, f32[2,32,3,8,128]{4,3,2,1,0:T(8,128)S(1)}, u32[]{:S(2)}, u32[]{:S(2)}) collective-permute-start(f32[2,32,3,8,128]{4,3,2,1,0:T(8,128)S(1)} %get-tuple-element.20), channel_id=1, source_target_pairs={{0,1},{1,0},{2,3},{3,2},{4,5},{5,4},{6,7},{7,6},{8,9},{9,8},{10,11... | collective-permute-start | bytes 2359304 | tf_op jit(solution)/shard_map/ppermute | solution.py:272
  30.9 18.0 %collective-permute-start.6 = (f32[64,2,8,128]{3,2,1,0:T(8,128)S(1)}, f32[64,2,8,128]{3,2,1,0:T(8,128)S(1)}, u32[]{:S(2)}, u32[]{:S(2)}) collective-permute-start(f32[64,2,8,128]{3,2,1,0:T(8,128)S(1)} %get-tuple-element.18), channel_id=1, source_target_pairs={{0,6},{2,0},{4,2},{6,4},{8,14},{10,8},{12,10},{14,12},{16,18},{18,... | collective-permute-start | bytes 1572872 | tf_op jit(solution)/shard_map/ppermute | solution.py:268
  32.7 16.2 %collective-permute-start.7 = (f32[64,8,128]{2,1,0:T(8,128)S(1)}, f32[64,8,128]{2,1,0:T(8,128)S(1)}, u32[]{:S(2)}, u32[]{:S(2)}) collective-permute-start(f32[64,8,128]{2,1,0:T(8,128)S(1)} %get-tuple-element.19), channel_id=1, source_target_pairs={{0,2},{2,4},{4,6},{6,0},{8,10},{10,12},{12,14},{14,8},{16,22},{18,... | collective-permute-start | bytes 786440 | tf_op jit(solution)/shard_map/ppermute | solution.py:268
  34.5 2.7 %collective-permute-start.11 = (f32[8,128]{1,0:T(8,128)S(1)}, f32[8,128]{1,0:T(8,128)S(1)}, u32[]{:S(2)}, u32[]{:S(2)}) collective-permute-start(f32[8,128]{1,0:T(8,128)S(1)} %sums.3.refs_4_), channel_id=1, source_target_pairs={{0,24},{8,0},{16,8},{24,16},{1,25},{9,1},{17,9},{25,17},{2,26},{10... | collective-permute-start | bytes 12296 | tf_op jit(solution)/shard_map/ppermute | solution.py:285
  35.2 3.6 %collective-permute-start.10 = (f32[8,128]{1,0:T(8,128)S(1)}, f32[8,128]{1,0:T(8,128)S(1)}, u32[]{:S(2)}, u32[]{:S(2)}) collective-permute-start(f32[8,128]{1,0:T(8,128)S(1)} %sums.3.refs_4_), channel_id=1, source_target_pairs={{0,16},{8,24},{16,0},{24,8},{1,17},{9,25},{17,1},{25,9},{2,18},{10... | collective-permute-start | bytes 12296 | tf_op jit(solution)/shard_map/ppermute | solution.py:285
  37.1 3.0 %collective-permute-start.9 = (f32[8,128]{1,0:T(8,128)S(1)}, f32[8,128]{1,0:T(8,128)S(1)}, u32[]{:S(2)}, u32[]{:S(2)}) collective-permute-start(f32[8,128]{1,0:T(8,128)S(1)} %sums.3.refs_4_), channel_id=1, source_target_pairs={{0,8},{8,16},{16,24},{24,0},{1,9},{9,17},{17,25},{25,1},{2,10},{10... | collective-permute-start | bytes 12296 | tf_op jit(solution)/shard_map/ppermute | solution.py:285

commit v2 on v1

v2 whole, which is shorter than its diff:
```python
import functools
import math

import jax
import jax.numpy as jnp
from jax import lax
from jax.experimental import pallas as pl
from jax.experimental.pallas import tpu as pltpu
from jax.sharding import PartitionSpec as P

KV = 32
LANES = 128
ROWS = 8

vel_bound = 4.5
time_step = 0.25 / 4.5
collision_interval = 0.25
power_law_index = 0.81
diffusivity_ratio = 2.0 / 3.0
step = vel_bound / KV
weight = (2.0 * vel_bound / KV) ** 3 * (2.0 * math.pi) ** (-1.5)
f32 = jnp.float32

TILES = KV * KV // LANES
HALF = TILES // 2
PER_TILE = LANES // KV
SLOTS = LANES // ROWS


def limited(p, q):
    return jnp.maximum(jnp.minimum(p, jnp.maximum(q, 0.0)), jnp.minimum(q, 0.0))


def lane_index():
    return lax.broadcasted_iota(jnp.int32, (ROWS, LANES), 1)


def component(digit):
    return (2 * digit + 1 - KV).astype(f32) * step


def lane_components(tile):
    lane = lane_index()
    return component(tile * PER_TILE + lane // KV), component(lane % KV)


def flow_of(vel_size):
    return lax.axis_index("vel") >= vel_size // 2


def order_of(flow):
    return [jnp.where(flow, k, ROWS - 1 - k) for k in range(ROWS)]


def row_of(x):
    return pl.ds(pl.multiple_of(x * ROWS, ROWS), ROWS)


def column_of(y):
    return pl.ds(y, ROWS, stride=ROWS)


def lanes_of(tile):
    return pl.ds(pl.multiple_of(tile * LANES, LANES), LANES)


def columns_in_order(sign):
    return range(ROWS) if sign else range(ROWS - 1, -1, -1)


def inner_changes(cells):
    slopes = [cells[k + 1] - cells[k] for k in range(ROWS - 1)]
    faces = [cells[k] + 0.5 * limited(slopes[k - 1], slopes[k]) for k in range(1, ROWS - 1)]
    middle = [faces[k] - faces[k - 1] for k in range(1, ROWS - 2)]
    return [faces[0], *middle, -faces[-1]]


def outer_changes(far, near, p0, p1, p6, p7, ahead):
    slope = p0 - near
    entry = near + 0.5 * limited(near - far, slope)
    first = p0 + 0.5 * limited(slope, p1 - p0)
    leave = p7 + 0.5 * limited(p7 - p6, ahead - p7)
    return first - entry, -first, leave


def pack_x_kernel(vel_size, table, primary, secondary, sems):
    flow = flow_of(vel_size)
    xs = order_of(flow)
    copies = [
        pltpu.make_async_copy(table.at[xs[6]], primary.at[0], sems.at[0]),
        pltpu.make_async_copy(table.at[xs[7]], primary.at[1], sems.at[1]),
        pltpu.make_async_copy(table.at[xs[0]], secondary.at[0], sems.at[2]),
    ]
    for copy in copies:
        copy.start()
    for copy in copies:
        copy.wait()


def send_y(source, pair, low, high, up, down):
    up[pair, 0] = source[high, column_of(6), :]
    up[pair, 1] = source[high, column_of(7), :]
    up[pair, 2] = source[low, column_of(7), :]
    down[pair, 0] = source[low, column_of(1), :]
    down[pair, 1] = source[low, column_of(0), :]
    down[pair, 2] = source[high, column_of(0), :]


def pack_y_kernel(levels, table, cells, up, down, held, sems):
    width = TILES * LANES

    def copy(level):
        lanes = pl.ds(pl.multiple_of(level * width, width), width)
        return pltpu.make_async_copy(table.at[:, :, lanes], held.at[level], sems.at[level])

    for level in range(levels):
        copy(level).start()

    def one(level, carry):
        copy(level).wait()
        for quarter in range(HALF):
            low = level * TILES + quarter
            high = low + HALF
            for tile, sub in ((low, quarter), (high, quarter + HALF)):
                for x in range(ROWS):
                    cells[tile, x * ROWS : (x + 1) * ROWS, :] = held[
                        level, x, :, sub * LANES : (sub + 1) * LANES
                    ]
            send_y(cells, level * HALF + quarter, low, high, up, down)
        return carry

    lax.fori_loop(0, levels, one, 0)


def sums_kernel(levels, cells, sums):
    lane = lane_index()
    base = lax.axis_index("vel") * levels
    speed = [component(base + level) for level in range(levels)]

    def one(x, total):
        acc = [jnp.zeros((ROWS, LANES), f32) for _ in range(13)]
        row = row_of(x)
        for tile in range(TILES):
            cb, ce = lane_components(tile)
            m0 = m1 = m2 = m3 = None
            for level in range(levels):
                g = cells[level * TILES + tile, row, :]
                g1 = g * speed[level]
                g2 = g1 * speed[level]
                g3 = g2 * speed[level]
                if level == 0:
                    m0, m1, m2, m3 = g, g1, g2, g3
                else:
                    m0, m1, m2, m3 = m0 + g, m1 + g1, m2 + g2, m3 + g3
            square = cb * cb + ce * ce
            b0 = cb * m0
            e0 = ce * m0
            terms = (
                m0, m1, b0, e0, m2, cb * b0, ce * e0, cb * m1, ce * m1, cb * e0,
                m3 + square * m1, cb * m2 + square * b0, ce * m2 + square * e0,
            )
            acc = [a + t for a, t in zip(acc, terms)]
        for m in range(13):
            total = jnp.where(lane == x * SLOTS + m, jnp.sum(acc[m], axis=1, keepdims=True), total)
        return total

    sums[...] = lax.fori_loop(0, ROWS, one, jnp.zeros((ROWS, LANES), f32))


def tables(parts, levels, base, scale, tab_b, tab_a, keep):
    sums = parts[0][...]
    for part in parts[1:]:
        sums = sums + part[...]
    sums = sums * weight
    for x in range(ROWS):
        m = [
            jnp.broadcast_to(sums[:, x * SLOTS + i : x * SLOTS + i + 1], (ROWS, LANES))
            for i in range(13)
        ]
        n = m[0]
        inverse = 1.0 / n
        u = [m[i] * inverse for i in (1, 2, 3)]
        uu = u[0] * u[0] + u[1] * u[1] + u[2] * u[2]
        energy = m[4] + m[5] + m[6]
        temp = (energy * inverse - uu) * (1.0 / 3.0)
        rows = ((4, 7, 8), (7, 5, 9), (8, 9, 6))
        q = []
        for i in range(3):
            r = rows[i]
            stress = m[r[0]] * u[0] + m[r[1]] * u[1] + m[r[2]] * u[2]
            q.append(0.5 * (m[10 + i] - 2.0 * stress - u[i] * energy + 2.0 * n * u[i] * uu))
        log_temp = jnp.log(temp)
        rate = n * jnp.exp((1.0 - power_law_index) * log_temp) * (time_step / collision_interval)
        cold = 1.0 / temp
        half_cold = 0.5 * cold
        size = scale * rate * n * (cold * lax.rsqrt(temp))
        lift = (1.0 - diffusivity_ratio) / (5.0 * n * temp * temp)
        keep[x] = scale * (1.0 - rate)
        ql = [part * lift for part in q]
        for tile in range(TILES):
            cb, ce = lane_components(tile)
            db, de = cb - u[1], ce - u[2]
            square = db * db + de * de
            tab_b[x, tile, 0] = size * jnp.exp(-square * half_cold)
            tab_b[x, tile, 1] = db * ql[1] + de * ql[2]
            tab_b[x, tile, 2] = square * cold - 5.0
        for level in range(levels):
            da = component(base + level) - u[0]
            square = da * da
            tab_a[x, level, 0] = jnp.exp(-square * half_cold)
            tab_a[x, level, 1] = da * ql[0]
            tab_a[x, level, 2] = square * cold


def speeds(base, level, quarter, sign, scale):
    b_digit = quarter * PER_TILE + lane_index() // KV + sign * (KV // 2)
    a_speed = jnp.abs(component(base + level)) * (time_step * scale)
    return a_speed, jnp.abs(component(b_digit)) * (time_step * scale)


def local_kernel(vel_size, levels, last, *refs):
    cells, parts, first, (out, tab_b, tab_a, keep, side) = refs[0], refs[1:2], refs[2:-5], refs[-5:]
    scale = 0.5 if last else 1.0
    base = lax.axis_index("vel") * levels
    tables(parts, levels, base, scale, tab_b, tab_a, keep)
    xs = order_of(flow_of(vel_size))
    rows = [row_of(x) for x in xs]
    for sign in (0, 1):
        side[sign] = jnp.zeros((ROWS * ROWS, LANES), f32)

    def one(i, carry):
        level, quarter = i // HALF, i % HALF
        for sign in (0, 1):
            sub = quarter + sign * HALF
            tile = level * TILES + sub
            a_speed, b_speed = speeds(base, level, quarter, sign, scale)
            ys = columns_in_order(sign)
            line = [cells[tile, column_of(y), :] for y in ys]
            for k, change in enumerate(inner_changes(line)):
                side[sign, column_of(ys[k + 1]), :] = b_speed * change
            line = [cells[tile, row, :] for row in rows]
            changes = inner_changes(line)
            for k in range(ROWS):
                x, row = xs[k], rows[k]
                source = tab_a[x, level, 0] * tab_b[x, sub, 0]
                bend = tab_a[x, level, 1] + tab_b[x, sub, 1]
                wide = tab_a[x, level, 2] + tab_b[x, sub, 2]
                new = line[k] * keep[x] + (source + source * (bend * wide))
                moved = side[sign, row, :]
                if k > 0:
                    moved = moved + a_speed * changes[k - 1]
                new = new - moved
                if last:
                    new = 0.5 * first[0][tile, row, :] + new
                out[tile, row, :] = new
        return carry

    lax.fori_loop(0, levels * HALF, one, 0)


def edge_changes(cells, tile, i, sign, rows, speed, from_x, up, down):
    a_speed, b_speed = speed
    mine, other = (up, down) if sign else (down, up)
    ys = columns_in_order(sign)
    line = [cells[tile, column_of(ys[k]), :] for k in (0, 1, 6, 7)]
    across = outer_changes(mine[i, 0], mine[i, 1], *line, other[i, 2])
    line = [cells[tile, rows[k], :] for k in (0, 1, 6, 7)]
    far, near, ahead = from_x(tile)
    along = outer_changes(far, near, *line, ahead)
    return [a_speed * c for c in along], [b_speed * c for c in across]


EDGE = (0, 1, ROWS - 1)
GROUP = 1


def correct_kernel(vel_size, levels, partial, cells, from_x1, from_x2, from_up, from_down, *refs):
    out, primary, secondary, up, down = refs
    base = lax.axis_index("vel") * levels
    xs = order_of(flow_of(vel_size))
    rows = [row_of(x) for x in xs]

    def from_x(tile):
        lanes = lanes_of(tile)
        return from_x1[0, :, lanes], from_x1[1, :, lanes], from_x2[0, :, lanes]

    def one(level, carry):
        for group in range(0, HALF, GROUP):
            changes = []
            for quarter in range(group, group + GROUP):
                for sign in (0, 1):
                    tile = level * TILES + quarter + sign * HALF
                    along, across = edge_changes(
                        cells, tile, level * HALF + quarter, sign, rows,
                        speeds(base, level, quarter, sign, 1.0), from_x, from_up, from_down,
                    )
                    changes.append((tile, columns_in_order(sign), along, across))
            old = [[out[t, column_of(ys[k]), :] for k in EDGE] for t, ys, _, _ in changes]
            for (t, ys, _, across), before in zip(changes, old):
                for k, value, change in zip(EDGE, before, across):
                    out[t, column_of(ys[k]), :] = value - change
            old = [[out[t, rows[k], :] for k in EDGE] for t, _, _, _ in changes]
            for (t, _, along, _), before in zip(changes, old):
                new = [value - change for value, change in zip(before, along)]
                for k, value in zip(EDGE, new):
                    out[t, rows[k], :] = value
                secondary[t] = new[0]
                primary[t, 1] = new[2]
            for t, _, _, _ in changes:
                primary[t, 0] = out[t, rows[6], :]
            for quarter in range(group, group + GROUP):
                low = level * TILES + quarter
                send_y(out, level * HALF + quarter, low, low + HALF, up, down)
        return carry

    lax.fori_loop(0, levels, one, 0)


def finish_kernel(vel_size, levels, partial, cells, from_x1, from_x2, from_up, from_down, *refs):
    result, held, side, sems = refs
    base = lax.axis_index("vel") * levels
    xs = order_of(flow_of(vel_size))
    rows = [row_of(x) for x in xs]
    width = TILES * LANES
    for sub in range(TILES):
        side[sub] = jnp.zeros((ROWS * ROWS, LANES), f32)

    def from_x(tile):
        return from_x1[tile, 0], from_x1[tile, 1], from_x2[tile]

    def copy(level):
        lanes = pl.ds(pl.multiple_of(level * width, width), width)
        return pltpu.make_async_copy(held.at[level], result.at[:, :, lanes], sems.at[level])

    def one(level, carry):
        for quarter in range(HALF):
            for sign in (0, 1):
                sub = quarter + sign * HALF
                tile = level * TILES + sub
                ys = columns_in_order(sign)
                along, across = edge_changes(
                    cells, tile, level * HALF + quarter, sign, rows,
                    speeds(base, level, quarter, sign, 0.5), from_x, from_up, from_down,
                )
                for k, change in zip(EDGE, across):
                    side[sub, column_of(ys[k]), :] = change
                extra = dict(zip(EDGE, along))
                for k in range(ROWS):
                    new = partial[tile, rows[k], :] - side[sub, rows[k], :]
                    if k in extra:
                        new = new - extra[k]
                    held[level, xs[k], :, sub * LANES : (sub + 1) * LANES] = new
        copy(level).start()
        return carry

    lax.fori_loop(0, levels, one, 0)
    for level in range(levels):
        copy(level).wait()


def local(sizes, table):
    vel_size, sx_size, sy_size = sizes
    cells_x, cells_y, count = table.shape
    levels = count // (KV * KV)
    assert cells_x == ROWS and cells_y == ROWS and vel_size % 2 == 0
    assert count == levels * KV * KV
    tiles = levels * TILES
    shape = lambda *dims: jax.ShapeDtypeStruct(dims, f32)
    cells_shape = shape(tiles, ROWS * ROWS, LANES)
    across_shape = shape(levels * HALF, 3, ROWS, LANES)
    whole = pl.BlockSpec(memory_space=pltpu.VMEM)
    outside = pl.BlockSpec(memory_space=pltpu.HBM)
    half = vel_size // 2

    def call(kernel, name, ins, outs, *args, scratch=(), aliases={}, static=(), room=16):
        specs = [outside if a is table else whole for a in args]
        return pl.pallas_call(
            functools.partial(kernel, *static),
            out_shape=outs,
            in_specs=specs,
            out_specs=ins,
            scratch_shapes=list(scratch),
            input_output_aliases=aliases,
            compiler_params=pltpu.CompilerParams(vmem_limit_bytes=room * 1024 * 1024),
            name=name,
        )(*args)

    def along_x(array, sign):
        pairs = []
        for v in range(vel_size):
            way = sign if v >= half else -sign
            pairs += [(v * sx_size + i, v * sx_size + (i + way) % sx_size) for i in range(sx_size)]
        return lax.ppermute(array, ("vel", "sx"), pairs)

    def along_y(array, way):
        return lax.ppermute(array, "sy", [(i, (i + way) % sy_size) for i in range(sy_size)])

    def exchange(primary, secondary, up, down):
        return along_x(primary, 1), along_x(secondary, -1), along_y(up, 1), along_y(down, -1)

    def gathered(sums):
        if vel_size & (vel_size - 1):
            return lax.psum(sums, "vel")
        d = 1
        while d < vel_size:
            sums = sums + lax.ppermute(sums, "vel", [(i, i ^ d) for i in range(vel_size)])
            d *= 2
        return sums

    def sums_of(cells):
        return gathered(
            call(sums_kernel, "sums", whole, shape(ROWS, LANES), cells, static=(levels,))
        )

    table_scratch = [
        pltpu.VMEM((ROWS, TILES, 3, ROWS, LANES), f32),
        pltpu.VMEM((ROWS, levels, 3, ROWS, LANES), f32),
        pltpu.VMEM((ROWS, ROWS, LANES), f32),
        pltpu.VMEM((2, ROWS * ROWS, LANES), f32),
    ]
    held = pltpu.VMEM((levels, ROWS, ROWS, TILES * LANES), f32)

    primary, secondary = call(
        pack_x_kernel, "pack_x", [whole] * 2,
        (shape(2, ROWS, count), shape(1, ROWS, count)),
        table, scratch=[pltpu.SemaphoreType.DMA((3,))], static=(vel_size,),
    )
    cells, up, down = call(
        pack_y_kernel, "pack_y", [whole] * 3, (cells_shape, across_shape, across_shape),
        table, scratch=[held, pltpu.SemaphoreType.DMA((levels,))], static=(levels,),
    )
    arrived = exchange(primary, secondary, up, down)
    partial = call(
        local_kernel, "local", whole, cells_shape, cells, sums_of(cells),
        scratch=table_scratch, static=(vel_size, levels, False),
    )
    sectioned, *messages = call(
        correct_kernel, "correct", [whole] * 5,
        (cells_shape, shape(tiles, 2, ROWS, LANES), shape(tiles, ROWS, LANES), across_shape, across_shape),
        partial, cells, *arrived, static=(vel_size, levels), aliases={0: 0},
    )
    arrived = exchange(*messages)
    partial = call(
        local_kernel, "local", whole, cells_shape, sectioned, sums_of(sectioned), cells,
        scratch=table_scratch, static=(vel_size, levels, True),
    )
    return call(
        finish_kernel, "finish", outside, shape(*table.shape), partial, sectioned, *arrived,
        scratch=[
            held,
            pltpu.VMEM((TILES, ROWS * ROWS, LANES), f32),
            pltpu.SemaphoreType.DMA((levels,)),
        ],
        static=(vel_size, levels),
    )


def solution(mesh):
    sizes = tuple(mesh.shape[name] for name in ("vel", "sx", "sy"))
    return jax.shard_map(
        functools.partial(local, sizes),
        mesh=mesh,
        in_specs=(P("sx", "sy", "vel"),),
        out_specs=P("sx", "sy", "vel"),
        check_vma=False,
    )
```

time: 54.2 us -> 50.3 us (0.928)
  starting transfers between devices: 17 us -> 14.4 us
  waiting for transfers between devices: 22.6 us -> 21.2 us
    ppermute x4, waiting for transfers between devices: 19.6 us -> 11.6 us  [along_x(): return lax.ppermute(array, ('vel', 'sx'), pairs)]
    ppermute x8, waiting for transfers between devices: 2.99 us -> 9.57 us  [the longest x4 6.5 us: gathered(): lax.ppermute(sums, 'vel', [(i, i ^ d) for i in range(vel_size)])]
    ppermute x8, starting transfers between devices: 11.3 us -> 7.21 us  [the longest x4 4.12 us: along_y(): lax.ppermute(array, 'sy', [(i, (i + way) % sy_size) for i in range(sy_siz...]
    ppermute x4, starting transfers between devices: 5.63 us -> 7.18 us  [along_x(): return lax.ppermute(array, ('vel', 'sx'), pairs)]
    pallas_call x5 -> x8, Pallas kernels: 12.9 us -> 12.9 us  [call(): pl.pallas_call(functools.partial(kernel, *static), out_shape=outs, in_spe...]
    unnamed x4 -> x2, local copies, waits for them, and re-layouts: 1.59 us -> 1.59 us
  transfers between devices with their start and end apart: 12 -> 12, of which waited for: 5 -> 8; matrix products, arithmetic and copies ran while one was open for 0% -> 0% of each run, Pallas kernels for 6% -> 20%
where the time goes in v2:
time: 50.3 us; the launch traced here: 50.1 us
  waiting for transfers between devices  21.2 us (42%)
  starting transfers between devices  14.4 us (29%)
  Pallas kernels  12.9 us (26%)
  local copies, waits for them, and re-layouts  1.59 us (3%)
    pallas_call x8, Pallas kernels, call(): pl.pallas_call(functools.partial(kernel, *static), out_shape=outs, in_spe...  12.9 us
    ppermute x4, waiting for transfers between devices, along_x(): return lax.ppermute(array, ('vel', 'sx'), pairs)  11.6 us
    ppermute x4, starting transfers between devices, along_x(): return lax.ppermute(array, ('vel', 'sx'), pairs)  7.18 us
    ppermute x4, waiting for transfers between devices, gathered(): lax.ppermute(sums, 'vel', [(i, i ^ d) for i in range(vel_size)])  6.5 us
    ppermute x4, starting transfers between devices, along_y(): lax.ppermute(array, 'sy', [(i, (i + way) % sy_size) for i in range(sy_siz...  4.12 us
    ppermute x4, starting transfers between devices, gathered(): lax.ppermute(sums, 'vel', [(i, i ^ d) for i in range(vel_size)])  3.1 us
    ppermute x4, waiting for transfers between devices, along_y(): lax.ppermute(array, 'sy', [(i, (i + way) % sy_size) for i in range(sy_siz...  3.06 us
    unnamed x2, local copies, waits for them, and re-layouts  1.59 us
  transfers between devices with their start and end apart: 12, of which 8 were waited for; matrix products, arithmetic and copies ran while one was open for 0% of the time, Pallas kernels for 20%

profile of v2, /device:TPU:0, one launch (start us, length us, event | category | flops | bytes accessed | tf_op | source)
XLA Modules:
  0.0 50.1 jit_solution(5396783724235132616)
XLA Ops:
  0.0 1.6 %copy-done = f32[8,8,8192]{2,1,0:T(8,128)S(1)} copy-done((f32[8,8,8192]{2,1,0:T(8,128)S(1)}, f32[8,8,8192]{2,1,0:T(8,128)}, u32[]{:S(2)}) %copy-start) | copy-done | bytes 2097176
  1.6 0.1 pack_x.1
  1.7 5.1 %collective-permute-start.2 = (f32[2,8,8192]{2,1,0:T(8,128)S(1)}, f32[2,8,8192]{2,1,0:T(8,128)S(1)}, u32[]{:S(2)}, u32[]{:S(2)}) collective-permute-start(f32[2,8,8192]{2,1,0:T(8,128)S(1)} %get-tuple-element.16), channel_id=1, source_target_pairs={{0,6},{2,0},{4,2},{6,4},{8,14},{10,8},{12,10},{14,12},{16,18},{18,... | collective-permute-start | bytes 1572872 | tf_op jit(solution)/shard_map/ppermute | solution.py:393
  6.8 0.6 %pack_y.1 = (f32[64,64,128]{2,1,0:T(8,128)S(1)}, f32[32,3,8,128]{3,2,1,0:T(8,128)S(1)}, f32[32,3,8,128]{3,2,1,0:T(8,128)S(1)}) custom-call(f32[8,8,8192]{2,1,0:T(8,128)S(1)} %copy-done), custom_call_target="tpu_custom_call" | custom-call | tf_op jit(solution)/shard_map/pack_y/pallas_call | solution.py:377
  7.3 1.6 %collective-permute-start.4 = (f32[32,3,8,128]{3,2,1,0:T(8,128)S(1)}, f32[32,3,8,128]{3,2,1,0:T(8,128)S(1)}, u32[]{:S(2)}, u32[]{:S(2)}) collective-permute-start(f32[32,3,8,128]{3,2,1,0:T(8,128)S(1)} %get-tuple-element.18), channel_id=1, source_target_pairs={{0,1},{1,0},{2,3},{3,2},{4,5},{5,4},{6,7},{7,6},{8,9},{9,8},{10,11... | collective-permute-start | bytes 1179656 | tf_op jit(solution)/shard_map/ppermute | solution.py:396
  8.9 0.5 %collective-permute-start.5 = (f32[32,3,8,128]{3,2,1,0:T(8,128)S(1)}, f32[32,3,8,128]{3,2,1,0:T(8,128)S(1)}, u32[]{:S(2)}, u32[]{:S(2)}) collective-permute-start(f32[32,3,8,128]{3,2,1,0:T(8,128)S(1)} %get-tuple-element.19), channel_id=1, source_target_pairs={{0,1},{1,0},{2,3},{3,2},{4,5},{5,4},{6,7},{7,6},{8,9},{9,8},{10,11... | collective-permute-start | bytes 1179656 | tf_op jit(solution)/shard_map/ppermute | solution.py:396
  9.4 0.0 collective-permute-start.3
  9.4 1.5 %sums.2 = f32[8,128]{1,0:T(8,128)S(1)} custom-call(f32[64,64,128]{2,1,0:T(8,128)S(1)} %get-tuple-element.15.cells.refs_0_.refs_2_), custom_call_target="tpu_custom_call" | custom-call | tf_op jit(solution)/shard_map/sums/pallas_call | solution.py:377
  11.0 0.0 collective-permute-start
  11.0 1.2 %collective-permute-done = f32[8,128]{1,0:T(8,128)S(1)} collective-permute-done((f32[8,128]{1,0:T(8,128)S(1)}, f32[8,128]{1,0:T(8,128)S(1)}, u32[]{:S(2)}, u32[]{:S(2)}) %collective-permute-start) | collective-permute-done | bytes 4128 | tf_op jit(solution)/shard_map/ppermute | solution.py:406
  12.2 1.7 %collective-permute-start.1 = (f32[8,128]{1,0:T(8,128)S(1)}, f32[8,128]{1,0:T(8,128)S(1)}, u32[]{:S(2)}, u32[]{:S(2)}) collective-permute-start(f32[8,128]{1,0:T(8,128)S(1)} %add.12), channel_id=1, source_target_pairs={{0,16},{8,24},{16,0},{24,8},{1,17},{9,25},{17,1},{25,9},{2,18},{10... | collective-permute-start | bytes 12296 | tf_op jit(solution)/shard_map/ppermute | solution.py:406
  13.9 1.9 %collective-permute-done.1 = f32[8,128]{1,0:T(8,128)S(1)} collective-permute-done((f32[8,128]{1,0:T(8,128)S(1)}, f32[8,128]{1,0:T(8,128)S(1)}, u32[]{:S(2)}, u32[]{:S(2)}) %collective-permute-start.1) | collective-permute-done | bytes 4128 | tf_op jit(solution)/shard_map/ppermute | solution.py:406
  15.8 3.0 %local.2.partial = f32[64,64,128]{2,1,0:T(8,128)S(1)} custom-call(f32[64,64,128]{2,1,0:T(8,128)S(1)} %get-tuple-element.15.cells.refs_0_.refs_2_, f32[8,128]{1,0:T(8,128)S(1)} %add.13.refs_1_), custom_call_target="tpu_custom_call" | custom-call | tf_op jit(solution)/shard_map/local/pallas_call | solution.py:377
  18.7 5.7 %collective-permute-done.3.from_x2 = f32[1,8,8192]{2,1,0:T(8,128)S(1)} collective-permute-done((f32[1,8,8192]{2,1,0:T(8,128)S(1)}, f32[1,8,8192]{2,1,0:T(8,128)S(1)}, u32[]{:S(2)}, u32[]{:S(2)}) %collective-permute-start.3) | collective-permute-done | bytes 262176 | tf_op jit(solution)/shard_map/ppermute | solution.py:393
  24.5 0.0 collective-permute-done.4.from_up
  24.5 1.9 %collective-permute-done.5.from_down = f32[32,3,8,128]{3,2,1,0:T(8,128)S(1)} collective-permute-done((f32[32,3,8,128]{3,2,1,0:T(8,128)S(1)}, f32[32,3,8,128]{3,2,1,0:T(8,128)S(1)}, u32[]{:S(2)}, u32[]{:S(2)}) %collective-permute-start.5) | collective-permute-done | bytes 393248 | tf_op jit(solution)/shard_map/ppermute | solution.py:396
  26.4 0.0 collective-permute-done.2.from_x1
  26.4 1.1 %correct.1 = (f32[64,64,128]{2,1,0:T(8,128)S(1)}, f32[64,2,8,128]{3,2,1,0:T(8,128)S(1)}, f32[64,8,128]{2,1,0:T(8,128)S(1)}, f32[32,3,8,128]{3,2,1,0:T(8,128)S(1)}, f32[32,3,8,128]{3,2,1,0:T(8,128)S(1)}) custom-call(f32[64,64,128]{2,1,0:T(8,128)S(1)} %local.2.partial, ...), custom_call_target="tpu_custom_call", output_to_operand_aliasing={{0}: (0, {})} | custom-call | tf_op jit(solution)/shard_map/correct/pallas_call | solution.py:377
  27.5 1.5 %collective-permute-start.8 = (f32[64,2,8,128]{3,2,1,0:T(8,128)S(1)}, f32[64,2,8,128]{3,2,1,0:T(8,128)S(1)}, u32[]{:S(2)}, u32[]{:S(2)}) collective-permute-start(f32[64,2,8,128]{3,2,1,0:T(8,128)S(1)} %get-tuple-element.21), channel_id=1, source_target_pairs={{0,6},{2,0},{4,2},{6,4},{8,14},{10,8},{12,10},{14,12},{16,18},{18,... | collective-permute-start | bytes 1572872 | tf_op jit(solution)/shard_map/ppermute | solution.py:393
  29.1 1.5 %collective-permute-start.10 = (f32[32,3,8,128]{3,2,1,0:T(8,128)S(1)}, f32[32,3,8,128]{3,2,1,0:T(8,128)S(1)}, u32[]{:S(2)}, u32[]{:S(2)}) collective-permute-start(f32[32,3,8,128]{3,2,1,0:T(8,128)S(1)} %get-tuple-element.23), channel_id=1, source_target_pairs={{0,1},{1,0},{2,3},{3,2},{4,5},{5,4},{6,7},{7,6},{8,9},{9,8},{10,11... | collective-permute-start | bytes 1179656 | tf_op jit(solution)/shard_map/ppermute | solution.py:396
  30.6 0.5 %collective-permute-start.11 = (f32[32,3,8,128]{3,2,1,0:T(8,128)S(1)}, f32[32,3,8,128]{3,2,1,0:T(8,128)S(1)}, u32[]{:S(2)}, u32[]{:S(2)}) collective-permute-start(f32[32,3,8,128]{3,2,1,0:T(8,128)S(1)} %get-tuple-element.24), channel_id=1, source_target_pairs={{0,1},{1,0},{2,3},{3,2},{4,5},{5,4},{6,7},{7,6},{8,9},{9,8},{10,11... | collective-permute-start | bytes 1179656 | tf_op jit(solution)/shard_map/ppermute | solution.py:396
  31.1 0.5 %collective-permute-start.9 = (f32[64,8,128]{2,1,0:T(8,128)S(1)}, f32[64,8,128]{2,1,0:T(8,128)S(1)}, u32[]{:S(2)}, u32[]{:S(2)}) collective-permute-start(f32[64,8,128]{2,1,0:T(8,128)S(1)} %get-tuple-element.22), channel_id=1, source_target_pairs={{0,2},{2,4},{4,6},{6,0},{8,10},{10,12},{12,14},{14,8},{16,22},{18,... | collective-permute-start | bytes 786440 | tf_op jit(solution)/shard_map/ppermute | solution.py:393
  31.6 1.5 %sums.3 = f32[8,128]{1,0:T(8,128)S(1)} custom-call(f32[64,64,128]{2,1,0:T(8,128)S(1)} %get-tuple-element.20.cells.refs_0_), custom_call_target="tpu_custom_call" | custom-call | tf_op jit(solution)/shard_map/sums/pallas_call | solution.py:377
  33.2 0.0 collective-permute-start.6
  33.2 1.2 %collective-permute-done.6 = f32[8,128]{1,0:T(8,128)S(1)} collective-permute-done((f32[8,128]{1,0:T(8,128)S(1)}, f32[8,128]{1,0:T(8,128)S(1)}, u32[]{:S(2)}, u32[]{:S(2)}) %collective-permute-start.6) | collective-permute-done | bytes 4128 | tf_op jit(solution)/shard_map/ppermute | solution.py:406
  34.4 1.3 %collective-permute-start.7 = (f32[8,128]{1,0:T(8,128)S(1)}, f32[8,128]{1,0:T(8,128)S(1)}, u32[]{:S(2)}, u32[]{:S(2)}) collective-permute-start(f32[8,128]{1,0:T(8,128)S(1)} %add.14), channel_id=1, source_target_pairs={{0,16},{8,24},{16,0},{24,8},{1,17},{9,25},{17,1},{25,9},{2,18},{10... | collective-permute-start | bytes 12296 | tf_op jit(solution)/shard_map/ppermute | solution.py:406
  35.6 2.3 %collective-permute-done.7 = f32[8,128]{1,0:T(8,128)S(1)} collective-permute-done((f32[8,128]{1,0:T(8,128)S(1)}, f32[8,128]{1,0:T(8,128)S(1)}, u32[]{:S(2)}, u32[]{:S(2)}) %collective-permute-start.7) | collective-permute-done | bytes 4128 | tf_op jit(solution)/shard_map/ppermute | solution.py:406
  38.0 3.2 %local.3.partial = f32[64,64,128]{2,1,0:T(8,128)S(1)} custom-call(f32[64,64,128]{2,1,0:T(8,128)S(1)} %get-tuple-element.20.cells.refs_0_, f32[8,128]{1,0:T(8,128)S(1)} %add.15.refs_1_, f32[64,64,128]{2,1,0:T(8,128)S(1)} %get-tuple-element.15.cells.refs_0_.refs_2_), custom_call_target="tpu_custom_call" | custom-call | tf_op jit(solution)/shard_map/local/pallas_call | solution.py:377
  41.2 5.9 %collective-permute-done.9.from_x2 = f32[64,8,128]{2,1,0:T(8,128)S(1)} collective-permute-done((f32[64,8,128]{2,1,0:T(8,128)S(1)}, f32[64,8,128]{2,1,0:T(8,128)S(1)}, u32[]{:S(2)}, u32[]{:S(2)}) %collective-permute-start.9) | collective-permute-done | bytes 262176 | tf_op jit(solution)/shard_map/ppermute | solution.py:393
  47.1 0.0 collective-permute-done.10.from_up
  47.1 1.1 %collective-permute-done.11.from_down = f32[32,3,8,128]{3,2,1,0:T(8,128)S(1)} collective-permute-done((f32[32,3,8,128]{3,2,1,0:T(8,128)S(1)}, f32[32,3,8,128]{3,2,1,0:T(8,128)S(1)}, u32[]{:S(2)}, u32[]{:S(2)}) %collective-permute-start.11) | collective-permute-done | bytes 393248 | tf_op jit(solution)/shard_map/ppermute | solution.py:396
  48.2 1.9 %finish.1 = f32[8,8,8192]{2,1,0:T(8,128)} custom-call(f32[64,64,128]{2,1,0:T(8,128)S(1)} %local.3.partial, f32[64,64,128]{2,1,0:T(8,128)S(1)} %get-tuple-element.20.cells.refs_0_, f32[64,2,8,128]{3,2,1,0:T(8,128)S(1)} %collective-permute-done.8.from_x1, f32[64,8,128]{2,1,0:T(8,128)S(1)} %collective-permute-done.9.from_x2, ...), custom_call_target="tpu_custom_call" | custom-call | tf_op jit(solution)/shard_map/finish/pallas_call | solution.py:377
  (6 shorter events, 0.0 us)
Async XLA Ops:
  0.0 1.6 %copy-start = (f32[8,8,8192]{2,1,0:T(8,128)S(1)}, f32[8,8,8192]{2,1,0:T(8,128)}, u32[]{:S(2)}) copy-start(f32[8,8,8192]{2,1,0:T(8,128)} %table.3) | copy-start | bytes 6291460
  1.7 24.7 %collective-permute-start.2 = (f32[2,8,8192]{2,1,0:T(8,128)S(1)}, f32[2,8,8192]{2,1,0:T(8,128)S(1)}, u32[]{:S(2)}, u32[]{:S(2)}) collective-permute-start(f32[2,8,8192]{2,1,0:T(8,128)S(1)} %get-tuple-element.16), channel_id=1, source_target_pairs={{0,6},{2,0},{4,2},{6,4},{8,14},{10,8},{12,10},{14,12},{16,18},{18,... | collective-permute-start | bytes 1572872 | tf_op jit(solution)/shard_map/ppermute | solution.py:393
  7.3 17.1 %collective-permute-start.4 = (f32[32,3,8,128]{3,2,1,0:T(8,128)S(1)}, f32[32,3,8,128]{3,2,1,0:T(8,128)S(1)}, u32[]{:S(2)}, u32[]{:S(2)}) collective-permute-start(f32[32,3,8,128]{3,2,1,0:T(8,128)S(1)} %get-tuple-element.18), channel_id=1, source_target_pairs={{0,1},{1,0},{2,3},{3,2},{4,5},{5,4},{6,7},{7,6},{8,9},{9,8},{10,11... | collective-permute-start | bytes 1179656 | tf_op jit(solution)/shard_map/ppermute | solution.py:396
  8.9 17.5 %collective-permute-start.5 = (f32[32,3,8,128]{3,2,1,0:T(8,128)S(1)}, f32[32,3,8,128]{3,2,1,0:T(8,128)S(1)}, u32[]{:S(2)}, u32[]{:S(2)}) collective-permute-start(f32[32,3,8,128]{3,2,1,0:T(8,128)S(1)} %get-tuple-element.19), channel_id=1, source_target_pairs={{0,1},{1,0},{2,3},{3,2},{4,5},{5,4},{6,7},{7,6},{8,9},{9,8},{10,11... | collective-permute-start | bytes 1179656 | tf_op jit(solution)/shard_map/ppermute | solution.py:396
  9.4 15.1 %collective-permute-start.3 = (f32[1,8,8192]{2,1,0:T(8,128)S(1)}, f32[1,8,8192]{2,1,0:T(8,128)S(1)}, u32[]{:S(2)}, u32[]{:S(2)}) collective-permute-start(f32[1,8,8192]{2,1,0:T(8,128)S(1)} %get-tuple-element.17), channel_id=1, source_target_pairs={{0,2},{2,4},{4,6},{6,0},{8,10},{10,12},{12,14},{14,8},{16,22},{18,... | collective-permute-start | bytes 786440 | tf_op jit(solution)/shard_map/ppermute | solution.py:393
  11.0 1.2 %collective-permute-start = (f32[8,128]{1,0:T(8,128)S(1)}, f32[8,128]{1,0:T(8,128)S(1)}, u32[]{:S(2)}, u32[]{:S(2)}) collective-permute-start(f32[8,128]{1,0:T(8,128)S(1)} %sums.2), channel_id=1, source_target_pairs={{0,8},{8,0},{16,24},{24,16},{1,9},{9,1},{17,25},{25,17},{2,10},{10... | collective-permute-start | bytes 12296 | tf_op jit(solution)/shard_map/ppermute | solution.py:406
  12.2 3.6 %collective-permute-start.1 = (f32[8,128]{1,0:T(8,128)S(1)}, f32[8,128]{1,0:T(8,128)S(1)}, u32[]{:S(2)}, u32[]{:S(2)}) collective-permute-start(f32[8,128]{1,0:T(8,128)S(1)} %add.12), channel_id=1, source_target_pairs={{0,16},{8,24},{16,0},{24,8},{1,17},{9,25},{17,1},{25,9},{2,18},{10... | collective-permute-start | bytes 12296 | tf_op jit(solution)/shard_map/ppermute | solution.py:406
  27.5 20.7 %collective-permute-start.8 = (f32[64,2,8,128]{3,2,1,0:T(8,128)S(1)}, f32[64,2,8,128]{3,2,1,0:T(8,128)S(1)}, u32[]{:S(2)}, u32[]{:S(2)}) collective-permute-start(f32[64,2,8,128]{3,2,1,0:T(8,128)S(1)} %get-tuple-element.21), channel_id=1, source_target_pairs={{0,6},{2,0},{4,2},{6,4},{8,14},{10,8},{12,10},{14,12},{16,18},{18,... | collective-permute-start | bytes 1572872 | tf_op jit(solution)/shard_map/ppermute | solution.py:393
  29.1 18.0 %collective-permute-start.10 = (f32[32,3,8,128]{3,2,1,0:T(8,128)S(1)}, f32[32,3,8,128]{3,2,1,0:T(8,128)S(1)}, u32[]{:S(2)}, u32[]{:S(2)}) collective-permute-start(f32[32,3,8,128]{3,2,1,0:T(8,128)S(1)} %get-tuple-element.23), channel_id=1, source_target_pairs={{0,1},{1,0},{2,3},{3,2},{4,5},{5,4},{6,7},{7,6},{8,9},{9,8},{10,11... | collective-permute-start | bytes 1179656 | tf_op jit(solution)/shard_map/ppermute | solution.py:396
  30.6 17.6 %collective-permute-start.11 = (f32[32,3,8,128]{3,2,1,0:T(8,128)S(1)}, f32[32,3,8,128]{3,2,1,0:T(8,128)S(1)}, u32[]{:S(2)}, u32[]{:S(2)}) collective-permute-start(f32[32,3,8,128]{3,2,1,0:T(8,128)S(1)} %get-tuple-element.24), channel_id=1, source_target_pairs={{0,1},{1,0},{2,3},{3,2},{4,5},{5,4},{6,7},{7,6},{8,9},{9,8},{10,11... | collective-permute-start | bytes 1179656 | tf_op jit(solution)/shard_map/ppermute | solution.py:396
  31.1 16.0 %collective-permute-start.9 = (f32[64,8,128]{2,1,0:T(8,128)S(1)}, f32[64,8,128]{2,1,0:T(8,128)S(1)}, u32[]{:S(2)}, u32[]{:S(2)}) collective-permute-start(f32[64,8,128]{2,1,0:T(8,128)S(1)} %get-tuple-element.22), channel_id=1, source_target_pairs={{0,2},{2,4},{4,6},{6,0},{8,10},{10,12},{12,14},{14,8},{16,22},{18,... | collective-permute-start | bytes 786440 | tf_op jit(solution)/shard_map/ppermute | solution.py:393
  33.2 1.2 %collective-permute-start.6 = (f32[8,128]{1,0:T(8,128)S(1)}, f32[8,128]{1,0:T(8,128)S(1)}, u32[]{:S(2)}, u32[]{:S(2)}) collective-permute-start(f32[8,128]{1,0:T(8,128)S(1)} %sums.3), channel_id=1, source_target_pairs={{0,8},{8,0},{16,24},{24,16},{1,9},{9,1},{17,25},{25,17},{2,10},{10... | collective-permute-start | bytes 12296 | tf_op jit(solution)/shard_map/ppermute | solution.py:406
  34.4 3.6 %collective-permute-start.7 = (f32[8,128]{1,0:T(8,128)S(1)}, f32[8,128]{1,0:T(8,128)S(1)}, u32[]{:S(2)}, u32[]{:S(2)}) collective-permute-start(f32[8,128]{1,0:T(8,128)S(1)} %add.14), channel_id=1, source_target_pairs={{0,16},{8,24},{16,0},{24,8},{1,17},{9,25},{17,1},{25,9},{2,18},{10... | collective-permute-start | bytes 12296 | tf_op jit(solution)/shard_map/ppermute | solution.py:406

commit v3 on v2

--- a/solution.py
+++ b/solution.py
@@ -9,6 +9,8 @@
 from jax.sharding import PartitionSpec as P
 
 KV = 32
+SPLIT = (1, 2)
+PARTED = ()
 LANES = 128
 ROWS = 8
 
@@ -83,30 +85,20 @@
     return first - entry, -first, leave
 
 
-def pack_x_kernel(vel_size, table, primary, secondary, sems):
-    flow = flow_of(vel_size)
-    xs = order_of(flow)
-    copies = [
-        pltpu.make_async_copy(table.at[xs[6]], primary.at[0], sems.at[0]),
-        pltpu.make_async_copy(table.at[xs[7]], primary.at[1], sems.at[1]),
-        pltpu.make_async_copy(table.at[xs[0]], secondary.at[0], sems.at[2]),
-    ]
-    for copy in copies:
-        copy.start()
-    for copy in copies:
-        copy.wait()
-
-
-def send_y(source, pair, low, high, up, down):
-    up[pair, 0] = source[high, column_of(6), :]
-    up[pair, 1] = source[high, column_of(7), :]
-    up[pair, 2] = source[low, column_of(7), :]
-    down[pair, 0] = source[low, column_of(1), :]
-    down[pair, 1] = source[low, column_of(0), :]
-    down[pair, 2] = source[high, column_of(0), :]
-
-
-def pack_y_kernel(levels, table, cells, up, down, held, sems):
+def send_y(source, pair, low, high, across):
+    across[0][pair, 0] = source[high, column_of(6), :]
+    across[0][pair, 1] = source[high, column_of(7), :]
+    across[0][pair, 2] = source[low, column_of(7), :]
+    across[1][pair, 0] = source[low, column_of(1), :]
+    across[1][pair, 1] = source[low, column_of(0), :]
+    across[1][pair, 2] = source[high, column_of(0), :]
+
+
+def pack_kernel(vel_size, levels, bounds, table, cells, *refs):
+    chunks = len(bounds)
+    across, primary, secondary = refs[:chunks], refs[chunks : 2 * chunks], refs[2 * chunks]
+    held, sems = refs[-2], refs[-1]
+    rows = [row_of(x) for x in order_of(flow_of(vel_size))]
     width = TILES * LANES
 
     def copy(level):
@@ -115,24 +107,33 @@
 
     for level in range(levels):
         copy(level).start()
-
-    def one(level, carry):
-        copy(level).wait()
-        for quarter in range(HALF):
-            low = level * TILES + quarter
-            high = low + HALF
-            for tile, sub in ((low, quarter), (high, quarter + HALF)):
-                for x in range(ROWS):
-                    cells[tile, x * ROWS : (x + 1) * ROWS, :] = held[
-                        level, x, :, sub * LANES : (sub + 1) * LANES
-                    ]
-            send_y(cells, level * HALF + quarter, low, high, up, down)
-        return carry
-
-    lax.fori_loop(0, levels, one, 0)
-
-
-def sums_kernel(levels, cells, sums):
+    for c, (begin, end) in enumerate(bounds):
+
+        def one(level, carry, c=c, begin=begin):
+            copy(level).wait()
+            for quarter in range(HALF):
+                low = level * TILES + quarter
+                high = low + HALF
+                for tile, sub in ((low, quarter), (high, quarter + HALF)):
+                    for x in range(ROWS):
+                        cells[tile, x * ROWS : (x + 1) * ROWS, :] = held[
+                            level, x, :, sub * LANES : (sub + 1) * LANES
+                        ]
+                    primary[c][tile - begin * TILES, 0] = cells[tile, rows[6], :]
+                    primary[c][tile - begin * TILES, 1] = cells[tile, rows[7], :]
+                    secondary[tile] = cells[tile, rows[0], :]
+                send_y(cells, (level - begin) * HALF + quarter, low, high, halves(across[c : c + 1]))
+            return carry
+
+        lax.fori_loop(begin, end, one, 0)
+
+
+def halves(refs):
+    return refs if len(refs) == 2 else [refs[0].at[0], refs[0].at[1]]
+
+
+def sums_kernel(levels, cells, *refs):
+    sums = refs[-1]
     lane = lane_index()
     base = lax.axis_index("vel") * levels
     speed = [component(base + level) for level in range(levels)]
@@ -168,9 +169,11 @@
 
 
 def tables(parts, levels, base, scale, tab_b, tab_a, keep):
-    sums = parts[0][...]
-    for part in parts[1:]:
-        sums = sums + part[...]
+    sums = None
+    for part in parts:
+        for i in range(part.shape[0] // ROWS):
+            more = part[i * ROWS : (i + 1) * ROWS, :]
+            sums = more if sums is None else sums + more
     sums = sums * weight
     for x in range(ROWS):
         m = [
@@ -258,12 +261,12 @@
     lax.fori_loop(0, levels * HALF, one, 0)
 
 
-def edge_changes(cells, tile, i, sign, rows, speed, from_x, up, down):
+def edge_changes(cells, tile, i, sign, rows, speed, from_x, from_y):
     a_speed, b_speed = speed
-    mine, other = (up, down) if sign else (down, up)
+    mine, other = 1 - sign, sign
     ys = columns_in_order(sign)
     line = [cells[tile, column_of(ys[k]), :] for k in (0, 1, 6, 7)]
-    across = outer_changes(mine[i, 0], mine[i, 1], *line, other[i, 2])
+    across = outer_changes(from_y[mine][i, 0], from_y[mine][i, 1], *line, from_y[other][i, 2])
     line = [cells[tile, rows[k], :] for k in (0, 1, 6, 7)]
     far, near, ahead = from_x(tile)
     along = outer_changes(far, near, *line, ahead)
@@ -274,15 +277,17 @@
 GROUP = 1
 
 
-def correct_kernel(vel_size, levels, partial, cells, from_x1, from_x2, from_up, from_down, *refs):
-    out, primary, secondary, up, down = refs
+def correct_kernel(vel_size, levels, start, stop, parted, partial, cells, from_x1, from_x2, from_y, *refs):
+    across = halves(refs[-1 - parted :])
+    out, primary, secondary = refs[-4 - parted : -1 - parted]
+    from_y = halves([from_y])
     base = lax.axis_index("vel") * levels
     xs = order_of(flow_of(vel_size))
     rows = [row_of(x) for x in xs]
 
     def from_x(tile):
-        lanes = lanes_of(tile)
-        return from_x1[0, :, lanes], from_x1[1, :, lanes], from_x2[0, :, lanes]
+        here = tile - start * TILES
+        return from_x1[here, 0], from_x1[here, 1], from_x2[tile]
 
     def one(level, carry):
         for group in range(0, HALF, GROUP):
@@ -290,34 +295,36 @@
             for quarter in range(group, group + GROUP):
                 for sign in (0, 1):
                     tile = level * TILES + quarter + sign * HALF
-                    along, across = edge_changes(
-                        cells, tile, level * HALF + quarter, sign, rows,
-                        speeds(base, level, quarter, sign, 1.0), from_x, from_up, from_down,
+                    along, sides = edge_changes(
+                        cells, tile, (level - start) * HALF + quarter, sign, rows,
+                        speeds(base, level, quarter, sign, 1.0), from_x, from_y,
                     )
-                    changes.append((tile, columns_in_order(sign), along, across))
+                    changes.append((tile, columns_in_order(sign), along, sides))
             old = [[out[t, column_of(ys[k]), :] for k in EDGE] for t, ys, _, _ in changes]
-            for (t, ys, _, across), before in zip(changes, old):
-                for k, value, change in zip(EDGE, before, across):
+            for (t, ys, _, sides), before in zip(changes, old):
+                for k, value, change in zip(EDGE, before, sides):
                     out[t, column_of(ys[k]), :] = value - change
             old = [[out[t, rows[k], :] for k in EDGE] for t, _, _, _ in changes]
             for (t, _, along, _), before in zip(changes, old):
+                mine = t - start * TILES
                 new = [value - change for value, change in zip(before, along)]
                 for k, value in zip(EDGE, new):
                     out[t, rows[k], :] = value
                 secondary[t] = new[0]
-                primary[t, 1] = new[2]
+                primary[mine, 1] = new[2]
             for t, _, _, _ in changes:
-                primary[t, 0] = out[t, rows[6], :]
+                primary[t - start * TILES, 0] = out[t, rows[6], :]
             for quarter in range(group, group + GROUP):
                 low = level * TILES + quarter
-                send_y(out, level * HALF + quarter, low, low + HALF, up, down)
+                send_y(out, (level - start) * HALF + quarter, low, low + HALF, across)
         return carry
 
-    lax.fori_loop(0, levels, one, 0)
-
-
-def finish_kernel(vel_size, levels, partial, cells, from_x1, from_x2, from_up, from_down, *refs):
-    result, held, side, sems = refs
+    lax.fori_loop(start, stop, one, 0)
+
+
+def finish_kernel(vel_size, levels, start, stop, parted, partial, cells, from_x1, from_x2, *refs):
+    from_y = halves(refs[: 1 + parted])
+    result, held, side, sems = refs[-4:]
     base = lax.axis_index("vel") * levels
     xs = order_of(flow_of(vel_size))
     rows = [row_of(x) for x in xs]
@@ -326,11 +333,13 @@
         side[sub] = jnp.zeros((ROWS * ROWS, LANES), f32)
 
     def from_x(tile):
-        return from_x1[tile, 0], from_x1[tile, 1], from_x2[tile]
+        here = tile - start * TILES
+        return from_x1[here, 0], from_x1[here, 1], from_x2[tile]
 
     def copy(level):
         lanes = pl.ds(pl.multiple_of(level * width, width), width)
-        return pltpu.make_async_copy(held.at[level], result.at[:, :, lanes], sems.at[level])
+        here = level - start
+        return pltpu.make_async_copy(held.at[here], result.at[:, :, lanes], sems.at[here])
 
     def one(level, carry):
         for quarter in range(HALF):
@@ -339,8 +348,8 @@
                 tile = level * TILES + sub
                 ys = columns_in_order(sign)
                 along, across = edge_changes(
-                    cells, tile, level * HALF + quarter, sign, rows,
-                    speeds(base, level, quarter, sign, 0.5), from_x, from_up, from_down,
+                    cells, tile, (level - start) * HALF + quarter, sign, rows,
+                    speeds(base, level, quarter, sign, 0.5), from_x, from_y,
                 )
                 for k, change in zip(EDGE, across):
                     side[sub, column_of(ys[k]), :] = change
@@ -349,12 +358,12 @@
                     new = partial[tile, rows[k], :] - side[sub, rows[k], :]
                     if k in extra:
                         new = new - extra[k]
-                    held[level, xs[k], :, sub * LANES : (sub + 1) * LANES] = new
+                    held[level - start, xs[k], :, sub * LANES : (sub + 1) * LANES] = new
         copy(level).start()
         return carry
 
-    lax.fori_loop(0, levels, one, 0)
-    for level in range(levels):
+    lax.fori_loop(start, stop, one, 0)
+    for level in range(start, stop):
         copy(level).wait()
 
 
@@ -364,16 +373,21 @@
     levels = count // (KV * KV)
     assert cells_x == ROWS and cells_y == ROWS and vel_size % 2 == 0
     assert count == levels * KV * KV
+    first_part = levels * SPLIT[0] // SPLIT[1]
+    bounds = [(0, first_part), (first_part, levels)] if 0 < first_part < levels else [(0, levels)]
+    chunks = len(bounds)
     tiles = levels * TILES
     shape = lambda *dims: jax.ShapeDtypeStruct(dims, f32)
     cells_shape = shape(tiles, ROWS * ROWS, LANES)
-    across_shape = shape(levels * HALF, 3, ROWS, LANES)
+    across_shape = [shape(2, (b - a) * HALF, 3, ROWS, LANES) for a, b in bounds]
+    primary_shape = [shape((b - a) * TILES, 2, ROWS, LANES) for a, b in bounds]
+    secondary_shape = shape(tiles, ROWS, LANES)
     whole = pl.BlockSpec(memory_space=pltpu.VMEM)
     outside = pl.BlockSpec(memory_space=pltpu.HBM)
     half = vel_size // 2
 
-    def call(kernel, name, ins, outs, *args, scratch=(), aliases={}, static=(), room=16):
-        specs = [outside if a is table else whole for a in args]
+    def call(kernel, name, ins, outs, *args, scratch=(), aliases={}, static=()):
+        specs = [outside if a.shape == table.shape else whole for a in args]
         return pl.pallas_call(
             functools.partial(kernel, *static),
             out_shape=outs,
@@ -381,7 +395,7 @@
             out_specs=ins,
             scratch_shapes=list(scratch),
             input_output_aliases=aliases,
-            compiler_params=pltpu.CompilerParams(vmem_limit_bytes=room * 1024 * 1024),
+            compiler_params=pltpu.CompilerParams(vmem_limit_bytes=16 * 1024 * 1024),
             name=name,
         )(*args)
 
@@ -392,13 +406,27 @@
             pairs += [(v * sx_size + i, v * sx_size + (i + way) % sx_size) for i in range(sx_size)]
         return lax.ppermute(array, ("vel", "sx"), pairs)
 
-    def along_y(array, way):
-        return lax.ppermute(array, "sy", [(i, (i + way) % sy_size) for i in range(sy_size)])
-
-    def exchange(primary, secondary, up, down):
-        return along_x(primary, 1), along_x(secondary, -1), along_y(up, 1), along_y(down, -1)
-
-    def gathered(sums):
+    def along_y(arrays):
+        ways = [[(i, (i + way) % sy_size) for i in range(sy_size)] for way in (1, -1)]
+        if len(arrays) == 2:
+            return tuple(lax.ppermute(a, "sy", way) for a, way in zip(arrays, ways))
+        if sy_size == 2:
+            return (lax.ppermute(arrays[0], "sy", ways[0]),)
+        return (jnp.stack([lax.ppermute(arrays[0][i], "sy", ways[i]) for i in (0, 1)]),)
+
+    def exchange(primary, secondary, across):
+        behind = along_x(secondary, -1)
+        return [(along_x(p, 1), behind, *along_y(a)) for p, a in zip(primary, across)]
+
+    def sums_of(cells, *after):
+        return call(sums_kernel, "sums", whole, shape(ROWS, LANES), cells, *after, static=(levels,))
+
+    def first_sums(sums):
+        if vel_size > 4:
+            return lax.psum(sums, "vel")
+        return lax.all_gather(sums, "vel", axis=0, tiled=True)
+
+    def second_sums(sums):
         if vel_size & (vel_size - 1):
             return lax.psum(sums, "vel")
         d = 1
@@ -407,52 +435,62 @@
             d *= 2
         return sums
 
-    def sums_of(cells):
-        return gathered(
-            call(sums_kernel, "sums", whole, shape(ROWS, LANES), cells, static=(levels,))
-        )
-
     table_scratch = [
         pltpu.VMEM((ROWS, TILES, 3, ROWS, LANES), f32),
         pltpu.VMEM((ROWS, levels, 3, ROWS, LANES), f32),
         pltpu.VMEM((ROWS, ROWS, LANES), f32),
         pltpu.VMEM((2, ROWS * ROWS, LANES), f32),
     ]
-    held = pltpu.VMEM((levels, ROWS, ROWS, TILES * LANES), f32)
-
-    primary, secondary = call(
-        pack_x_kernel, "pack_x", [whole] * 2,
-        (shape(2, ROWS, count), shape(1, ROWS, count)),
-        table, scratch=[pltpu.SemaphoreType.DMA((3,))], static=(vel_size,),
+    held = lambda count: pltpu.VMEM((count, ROWS, ROWS, TILES * LANES), f32)
+    copies = lambda count: pltpu.SemaphoreType.DMA((count,))
+
+    cells, *messages, secondary = call(
+        pack_kernel, "pack", [whole] * (2 * chunks + 2),
+        [cells_shape] + across_shape + primary_shape + [secondary_shape],
+        table, scratch=[held(levels), copies(levels)], static=(vel_size, levels, bounds),
     )
-    cells, up, down = call(
-        pack_y_kernel, "pack_y", [whole] * 3, (cells_shape, across_shape, across_shape),
-        table, scratch=[held, pltpu.SemaphoreType.DMA((levels,))], static=(levels,),
-    )
-    arrived = exchange(primary, secondary, up, down)
-    partial = call(
-        local_kernel, "local", whole, cells_shape, cells, sums_of(cells),
+    arrived = exchange(messages[chunks:], secondary, [(m,) for m in messages[:chunks]])
+    sectioned = call(
+        local_kernel, "local", whole, cells_shape, cells, first_sums(sums_of(cells)),
         scratch=table_scratch, static=(vel_size, levels, False),
     )
-    sectioned, *messages = call(
-        correct_kernel, "correct", [whole] * 5,
-        (cells_shape, shape(tiles, 2, ROWS, LANES), shape(tiles, ROWS, LANES), across_shape, across_shape),
-        partial, cells, *arrived, static=(vel_size, levels), aliases={0: 0},
-    )
-    arrived = exchange(*messages)
+    primary, across, partly = [], [], ()
+    for c, (begin, end) in enumerate(bounds):
+        parted = int(c in PARTED)
+        one_way = shape((end - begin) * HALF, 3, ROWS, LANES)
+        sectioned, first, secondary, *sides = call(
+            correct_kernel, "correct", [whole] * (4 + parted),
+            [cells_shape, primary_shape[c], secondary_shape]
+            + ([one_way] * 2 if parted else [across_shape[c]]),
+            sectioned, cells, *arrived[c], *partly,
+            static=(vel_size, levels, begin, end, parted),
+            aliases={0: 0, 5: 2} if partly else {0: 0},
+        )
+        partly = (secondary,)
+        primary.append(first)
+        across.append(sides)
+    arrived = exchange(primary, secondary, across)
+    sums = first_sums(sums_of(sectioned))
     partial = call(
-        local_kernel, "local", whole, cells_shape, sectioned, sums_of(sectioned), cells,
+        local_kernel, "local", whole, cells_shape, sectioned, sums, cells,
         scratch=table_scratch, static=(vel_size, levels, True),
     )
-    return call(
-        finish_kernel, "finish", outside, shape(*table.shape), partial, sectioned, *arrived,
-        scratch=[
-            held,
-            pltpu.VMEM((TILES, ROWS * ROWS, LANES), f32),
-            pltpu.SemaphoreType.DMA((levels,)),
-        ],
-        static=(vel_size, levels),
-    )
+    result = ()
+    for c, (begin, end) in enumerate(bounds):
+        result = (
+            call(
+                finish_kernel, "finish", outside, shape(*table.shape),
+                partial, sectioned, *arrived[c], *result,
+                scratch=[
+                    held(end - begin),
+                    pltpu.VMEM((TILES, ROWS * ROWS, LANES), f32),
+                    copies(end - begin),
+                ],
+                static=(vel_size, levels, begin, end, int(c in PARTED)),
+                aliases={2 + len(arrived[c]): 0} if result else {},
+            ),
+        )
+    return result[0]
 
 
 def solution(mesh):

time: 50.3 us -> 47.6 us (0.946)
  waiting for transfers between devices: 21.2 us -> 0.71 us
  blocking collectives: 0 us -> 10.3 us
  starting transfers between devices: 14.4 us -> 20.4 us
  Pallas kernels: 12.9 us -> 13.8 us
    ppermute x4 -> x6, waiting for transfers between devices: 11.6 us -> 0.7 us  [along_x(): return lax.ppermute(array, ('vel', 'sx'), pairs)]
    all_gather x0 -> x2, blocking collectives: none -> 10.3 us  [first_sums(): return lax.all_gather(sums, 'vel', axis=0, tiled=True)]
    ppermute x8 -> x4, waiting for transfers between devices: 9.57 us -> 0.01 us  [along_y(): return (lax.ppermute(arrays[0], 'sy', ways[0]),)]
    ppermute x4 -> x6, starting transfers between devices: 7.18 us -> 14.2 us  [along_x(): return lax.ppermute(array, ('vel', 'sx'), pairs)]
    ppermute x8 -> x4, starting transfers between devices: 7.21 us -> 6.19 us  [along_y(): return (lax.ppermute(arrays[0], 'sy', ways[0]),)]
    pallas_call x8 -> x9, Pallas kernels: 12.9 us -> 13.8 us  [call(): pl.pallas_call(functools.partial(kernel, *static), out_shape=outs, in_spe...]
  transfers between devices with their start and end apart: 12 -> 10, of which waited for: 8 -> 1; matrix products, arithmetic and copies ran while one was open for 0% -> 0% of each run, Pallas kernels for 20% -> 25%
where the time goes in v3:
time: 47.6 us; the launch traced here: 47 us
  starting transfers between devices  20.4 us (43%)
  Pallas kernels  13.8 us (29%)
  blocking collectives  10.3 us (22%)
  local copies, waits for them, and re-layouts  1.59 us (3%)
  waiting for transfers between devices  0.71 us (1%)
    ppermute x6, starting transfers between devices, along_x(): return lax.ppermute(array, ('vel', 'sx'), pairs)  14.2 us
    pallas_call x9, Pallas kernels, call(): pl.pallas_call(functools.partial(kernel, *static), out_shape=outs, in_spe...  13.8 us
    all_gather x2, blocking collectives, first_sums(): return lax.all_gather(sums, 'vel', axis=0, tiled=True)  10.3 us
    ppermute x4, starting transfers between devices, along_y(): return (lax.ppermute(arrays[0], 'sy', ways[0]),)  6.19 us
    unnamed x2, local copies, waits for them, and re-layouts  1.59 us
  transfers between devices with their start and end apart: 10, of which 1 were waited for; matrix products, arithmetic and copies ran while one was open for 0% of the time, Pallas kernels for 25%

profile of v3, /device:TPU:0, one launch (start us, length us, event | category | flops | bytes accessed | tf_op | source)
XLA Modules:
  0.0 47.0 jit_solution(3112916736948900218)
XLA Ops:
  0.0 1.6 %copy-done = f32[8,8,8192]{2,1,0:T(8,128)S(1)} copy-done((f32[8,8,8192]{2,1,0:T(8,128)S(1)}, f32[8,8,8192]{2,1,0:T(8,128)}, u32[]{:S(2)}) %copy-start) | copy-done | bytes 2097176
  1.6 0.8 %pack.1 = (f32[64,64,128]{2,1,0:T(8,128)S(1)}, f32[2,16,3,8,128]{4,3,2,1,0:T(8,128)S(1)}, f32[2,16,3,8,128]{4,3,2,1,0:T(8,128)S(1)}, f32[32,2,8,128]{3,2,1,0:T(8...) custom-call(f32[8,8,8192]{2,1,0:T(8,128)S(1)} %copy-done), custom_call_target="tpu_custom_call" | custom-call | tf_op jit(solution)/shard_map/pack/pallas_call | solution.py:391
  2.4 3.0 %collective-permute-start.2 = (f32[2,16,3,8,128]{4,3,2,1,0:T(8,128)S(1)}, f32[2,16,3,8,128]{4,3,2,1,0:T(8,128)S(1)}, u32[]{:S(2)}, u32[]{:S(2)}) collective-permute-start(f32[2,16,3,8,128]{4,3,2,1,0:T(8,128)S(1)} %get-tuple-element.22), channel_id=1, source_target_pairs={{0,1},{1,0},{2,3},{3,2},{4,5},{5,4},{6,7},{7,6},{8,9},{9,8},{10,11... | collective-permute-start | bytes 1179656 | tf_op jit(solution)/shard_map/ppermute | solution.py:414
  5.5 0.1 collective-permute-start.4
  5.5 4.1 %collective-permute-start = (f32[32,2,8,128]{3,2,1,0:T(8,128)S(1)}, f32[32,2,8,128]{3,2,1,0:T(8,128)S(1)}, u32[]{:S(2)}, u32[]{:S(2)}) collective-permute-start(f32[32,2,8,128]{3,2,1,0:T(8,128)S(1)} %get-tuple-element.20), channel_id=1, source_target_pairs={{0,6},{2,0},{4,2},{6,4},{8,14},{10,8},{12,10},{14,12},{16,18},{18,... | collective-permute-start | bytes 786440 | tf_op jit(solution)/shard_map/ppermute | solution.py:407
  9.6 0.0 collective-permute-start.1
  9.6 3.8 %collective-permute-start.3 = (f32[32,2,8,128]{3,2,1,0:T(8,128)S(1)}, f32[32,2,8,128]{3,2,1,0:T(8,128)S(1)}, u32[]{:S(2)}, u32[]{:S(2)}) collective-permute-start(f32[32,2,8,128]{3,2,1,0:T(8,128)S(1)} %get-tuple-element.24), channel_id=1, source_target_pairs={{0,6},{2,0},{4,2},{6,4},{8,14},{10,8},{12,10},{14,12},{16,18},{18,... | collective-permute-start | bytes 786440 | tf_op jit(solution)/shard_map/ppermute | solution.py:407
  13.4 1.5 %sums.2 = f32[8,128]{1,0:T(8,128)S(1)} custom-call(f32[64,64,128]{2,1,0:T(8,128)S(1)} %get-tuple-element.19.cells.refs_0_.refs_2_), custom_call_target="tpu_custom_call" | custom-call | tf_op jit(solution)/shard_map/sums/pallas_call | solution.py:391
  14.9 5.2 %all_gather.6.refs_1_ = f32[32,128]{1,0:T(8,128)S(1)} all-gather(f32[8,128]{1,0:T(8,128)S(1)} %sums.2), channel_id=1, replica_groups=mesh['vel'=4,'sx'=4,'sy'=2] {'vel'}, dimensions={0}, use_global_device_ids=true | all-gather | bytes 20480 | tf_op jit(solution)/shard_map/all_gather | solution.py:427
  20.1 3.0 %local.2.partial = f32[64,64,128]{2,1,0:T(8,128)S(1)} custom-call(f32[64,64,128]{2,1,0:T(8,128)S(1)} %get-tuple-element.19.cells.refs_0_.refs_2_, f32[32,128]{1,0:T(8,128)S(1)} %all_gather.6.refs_1_), custom_call_target="tpu_custom_call" | custom-call | tf_op jit(solution)/shard_map/local/pallas_call | solution.py:391
  23.1 0.0 collective-permute-done.from_x1
  23.1 0.0 collective-permute-done.1.from_x2
  23.1 0.0 collective-permute-done.2.from_y
  23.1 0.6 %correct.2 = (f32[64,64,128]{2,1,0:T(8,128)S(1)}, f32[32,2,8,128]{3,2,1,0:T(8,128)S(1)}, f32[64,8,128]{2,1,0:T(8,128)S(1)}, f32[2,16,3,8,128]{4,3,2,1,0:T(8,128)S(1)}) custom-call(f32[64,64,128]{2,1,0:T(8,128)S(1)} %local.2.partial, f32[64,64,128]{2,1,0:T(8,128)S(1)} %get-tuple-element.19.cells.refs_0_.refs_2_, ...), custom_call_target="tpu_custom_call", output_to_operand_aliasing={{0}: (0, {})} | custom-call | tf_op jit(solution)/shard_map/correct/pallas_call | solution.py:391
  23.7 1.6 %collective-permute-start.9 = (f32[2,16,3,8,128]{4,3,2,1,0:T(8,128)S(1)}, f32[2,16,3,8,128]{4,3,2,1,0:T(8,128)S(1)}, u32[]{:S(2)}, u32[]{:S(2)}) collective-permute-start(f32[2,16,3,8,128]{4,3,2,1,0:T(8,128)S(1)} %get-tuple-element.32), channel_id=1, source_target_pairs={{0,1},{1,0},{2,3},{3,2},{4,5},{5,4},{6,7},{7,6},{8,9},{9,8},{10,11... | collective-permute-start | bytes 1179656 | tf_op jit(solution)/shard_map/ppermute | solution.py:414
  25.2 0.6 %collective-permute-done.3.from_x1 = f32[32,2,8,128]{3,2,1,0:T(8,128)S(1)} collective-permute-done((f32[32,2,8,128]{3,2,1,0:T(8,128)S(1)}, f32[32,2,8,128]{3,2,1,0:T(8,128)S(1)}, u32[]{:S(2)}, u32[]{:S(2)}) %collective-permute-start.3) | collective-permute-done | bytes 262176 | tf_op jit(solution)/shard_map/ppermute | solution.py:407
  25.9 0.0 collective-permute-done.4.from_y
  25.9 0.6 %correct.3 = (f32[64,64,128]{2,1,0:T(8,128)S(1)}, f32[32,2,8,128]{3,2,1,0:T(8,128)S(1)}, f32[64,8,128]{2,1,0:T(8,128)S(1)}, f32[2,16,3,8,128]{4,3,2,1,0:T(8,128)S(1)}) custom-call(f32[64,64,128]{2,1,0:T(8,128)S(1)} %get-tuple-element.23.partial, ...), custom_call_target="tpu_custom_call", output_to_operand_aliasing={{0}: (0, {}), {2}: (5, {})} | custom-call | tf_op jit(solution)/shard_map/correct/pallas_call | solution.py:391
  26.4 1.6 %collective-permute-start.7 = (f32[2,16,3,8,128]{4,3,2,1,0:T(8,128)S(1)}, f32[2,16,3,8,128]{4,3,2,1,0:T(8,128)S(1)}, u32[]{:S(2)}, u32[]{:S(2)}) collective-permute-start(f32[2,16,3,8,128]{4,3,2,1,0:T(8,128)S(1)} %get-tuple-element.30), channel_id=1, source_target_pairs={{0,1},{1,0},{2,3},{3,2},{4,5},{5,4},{6,7},{7,6},{8,9},{9,8},{10,11... | collective-permute-start | bytes 1179656 | tf_op jit(solution)/shard_map/ppermute | solution.py:414
  28.0 0.4 collective-permute-start.6
  28.4 3.9 %collective-permute-start.8 = (f32[32,2,8,128]{3,2,1,0:T(8,128)S(1)}, f32[32,2,8,128]{3,2,1,0:T(8,128)S(1)}, u32[]{:S(2)}, u32[]{:S(2)}) collective-permute-start(f32[32,2,8,128]{3,2,1,0:T(8,128)S(1)} %get-tuple-element.31), channel_id=1, source_target_pairs={{0,6},{2,0},{4,2},{6,4},{8,14},{10,8},{12,10},{14,12},{16,18},{18,... | collective-permute-start | bytes 786440 | tf_op jit(solution)/shard_map/ppermute | solution.py:407
  32.3 2.0 %collective-permute-start.5 = (f32[32,2,8,128]{3,2,1,0:T(8,128)S(1)}, f32[32,2,8,128]{3,2,1,0:T(8,128)S(1)}, u32[]{:S(2)}, u32[]{:S(2)}) collective-permute-start(f32[32,2,8,128]{3,2,1,0:T(8,128)S(1)} %get-tuple-element.28), channel_id=1, source_target_pairs={{0,6},{2,0},{4,2},{6,4},{8,14},{10,8},{12,10},{14,12},{16,18},{18,... | collective-permute-start | bytes 786440 | tf_op jit(solution)/shard_map/ppermute | solution.py:407
  34.3 1.5 %sums.3 = f32[8,128]{1,0:T(8,128)S(1)} custom-call(f32[64,64,128]{2,1,0:T(8,128)S(1)} %get-tuple-element.27.cells.refs_0_), custom_call_target="tpu_custom_call" | custom-call | tf_op jit(solution)/shard_map/sums/pallas_call | solution.py:391
  35.8 5.2 %all_gather.7.refs_1_ = f32[32,128]{1,0:T(8,128)S(1)} all-gather(f32[8,128]{1,0:T(8,128)S(1)} %sums.3), channel_id=1, replica_groups=mesh['vel'=4,'sx'=4,'sy'=2] {'vel'}, dimensions={0}, use_global_device_ids=true | all-gather | bytes 20480 | tf_op jit(solution)/shard_map/all_gather | solution.py:427
  41.0 3.2 %local.3.partial = f32[64,64,128]{2,1,0:T(8,128)S(1)} custom-call(f32[64,64,128]{2,1,0:T(8,128)S(1)} %get-tuple-element.27.cells.refs_0_, f32[32,128]{1,0:T(8,128)S(1)} %all_gather.7.refs_1_, f32[64,64,128]{2,1,0:T(8,128)S(1)} %get-tuple-element.19.cells.refs_0_.refs_2_), custom_call_target="tpu_custom_call" | custom-call | tf_op jit(solution)/shard_map/local/pallas_call | solution.py:391
  44.2 0.0 collective-permute-done.6.from_x2
  44.2 0.0 collective-permute-done.8.from_x1
  44.2 0.0 collective-permute-done.9.refs_0_
  44.3 1.3 %finish.2.refs_1_ = f32[8,8,8192]{2,1,0:T(8,128)} custom-call(f32[64,64,128]{2,1,0:T(8,128)S(1)} %local.3.partial, f32[64,64,128]{2,1,0:T(8,128)S(1)} %get-tuple-element.27.cells.refs_0_, f32[32,2,8,128]{3,2,1,0:T(8,128)S(1)} %collective-permute-done.8.from_x1, f32[64,8,128]{2,1,0:T(8,128)S(1)} %collective-permute-done.6.from_x2, ...), custom_call_target="tpu_custom_call" | custom-call | tf_op jit(solution)/shard_map/finish/pallas_call | solution.py:391
  45.6 0.0 collective-permute-done.5.from_x1
  45.6 0.0 collective-permute-done.7.refs_0_
  45.6 1.3 %finish.3 = f32[8,8,8192]{2,1,0:T(8,128)} custom-call(f32[64,64,128]{2,1,0:T(8,128)S(1)} %local.3.partial, f32[64,64,128]{2,1,0:T(8,128)S(1)} %get-tuple-element.27.cells.refs_0_, f32[32,2,8,128]{3,2,1,0:T(8,128)S(1)} %collective-permute-done.5.from_x1, f32[64,8,128]{2,1,0:T(8,128)S(1)} %collective-permute-done.6.from_x2, ...), custom_call_target="tpu_custom_call", output_to_operand_aliasing={{}: (5, {})} | custom-call | tf_op jit(solution)/shard_map/finish/pallas_call | solution.py:391
  (1 shorter events, 0.0 us)
Async XLA Ops:
  0.0 1.6 %copy-start = (f32[8,8,8192]{2,1,0:T(8,128)S(1)}, f32[8,8,8192]{2,1,0:T(8,128)}, u32[]{:S(2)}) copy-start(f32[8,8,8192]{2,1,0:T(8,128)} %table.1) | copy-start | bytes 6291460
  2.4 20.7 %collective-permute-start.2 = (f32[2,16,3,8,128]{4,3,2,1,0:T(8,128)S(1)}, f32[2,16,3,8,128]{4,3,2,1,0:T(8,128)S(1)}, u32[]{:S(2)}, u32[]{:S(2)}) collective-permute-start(f32[2,16,3,8,128]{4,3,2,1,0:T(8,128)S(1)} %get-tuple-element.22), channel_id=1, source_target_pairs={{0,1},{1,0},{2,3},{3,2},{4,5},{5,4},{6,7},{7,6},{8,9},{9,8},{10,11... | collective-permute-start | bytes 1179656 | tf_op jit(solution)/shard_map/ppermute | solution.py:414
  5.5 20.4 %collective-permute-start.4 = (f32[2,16,3,8,128]{4,3,2,1,0:T(8,128)S(1)}, f32[2,16,3,8,128]{4,3,2,1,0:T(8,128)S(1)}, u32[]{:S(2)}, u32[]{:S(2)}) collective-permute-start(f32[2,16,3,8,128]{4,3,2,1,0:T(8,128)S(1)} %get-tuple-element.25), channel_id=1, source_target_pairs={{0,1},{1,0},{2,3},{3,2},{4,5},{5,4},{6,7},{7,6},{8,9},{9,8},{10,11... | collective-permute-start | bytes 1179656 | tf_op jit(solution)/shard_map/ppermute | solution.py:414
  5.5 17.6 %collective-permute-start = (f32[32,2,8,128]{3,2,1,0:T(8,128)S(1)}, f32[32,2,8,128]{3,2,1,0:T(8,128)S(1)}, u32[]{:S(2)}, u32[]{:S(2)}) collective-permute-start(f32[32,2,8,128]{3,2,1,0:T(8,128)S(1)} %get-tuple-element.20), channel_id=1, source_target_pairs={{0,6},{2,0},{4,2},{6,4},{8,14},{10,8},{12,10},{14,12},{16,18},{18,... | collective-permute-start | bytes 786440 | tf_op jit(solution)/shard_map/ppermute | solution.py:407
  9.6 13.5 %collective-permute-start.1 = (f32[64,8,128]{2,1,0:T(8,128)S(1)}, f32[64,8,128]{2,1,0:T(8,128)S(1)}, u32[]{:S(2)}, u32[]{:S(2)}) collective-permute-start(f32[64,8,128]{2,1,0:T(8,128)S(1)} %get-tuple-element.21), channel_id=1, source_target_pairs={{0,2},{2,4},{4,6},{6,0},{8,10},{10,12},{12,14},{14,8},{16,22},{18,... | collective-permute-start | bytes 786440 | tf_op jit(solution)/shard_map/ppermute | solution.py:407
  9.6 16.3 %collective-permute-start.3 = (f32[32,2,8,128]{3,2,1,0:T(8,128)S(1)}, f32[32,2,8,128]{3,2,1,0:T(8,128)S(1)}, u32[]{:S(2)}, u32[]{:S(2)}) collective-permute-start(f32[32,2,8,128]{3,2,1,0:T(8,128)S(1)} %get-tuple-element.24), channel_id=1, source_target_pairs={{0,6},{2,0},{4,2},{6,4},{8,14},{10,8},{12,10},{14,12},{16,18},{18,... | collective-permute-start | bytes 786440 | tf_op jit(solution)/shard_map/ppermute | solution.py:407
  23.7 20.6 %collective-permute-start.9 = (f32[2,16,3,8,128]{4,3,2,1,0:T(8,128)S(1)}, f32[2,16,3,8,128]{4,3,2,1,0:T(8,128)S(1)}, u32[]{:S(2)}, u32[]{:S(2)}) collective-permute-start(f32[2,16,3,8,128]{4,3,2,1,0:T(8,128)S(1)} %get-tuple-element.32), channel_id=1, source_target_pairs={{0,1},{1,0},{2,3},{3,2},{4,5},{5,4},{6,7},{7,6},{8,9},{9,8},{10,11... | collective-permute-start | bytes 1179656 | tf_op jit(solution)/shard_map/ppermute | solution.py:414
  26.4 19.2 %collective-permute-start.7 = (f32[2,16,3,8,128]{4,3,2,1,0:T(8,128)S(1)}, f32[2,16,3,8,128]{4,3,2,1,0:T(8,128)S(1)}, u32[]{:S(2)}, u32[]{:S(2)}) collective-permute-start(f32[2,16,3,8,128]{4,3,2,1,0:T(8,128)S(1)} %get-tuple-element.30), channel_id=1, source_target_pairs={{0,1},{1,0},{2,3},{3,2},{4,5},{5,4},{6,7},{7,6},{8,9},{9,8},{10,11... | collective-permute-start | bytes 1179656 | tf_op jit(solution)/shard_map/ppermute | solution.py:414
  28.0 16.2 %collective-permute-start.6 = (f32[64,8,128]{2,1,0:T(8,128)S(1)}, f32[64,8,128]{2,1,0:T(8,128)S(1)}, u32[]{:S(2)}, u32[]{:S(2)}) collective-permute-start(f32[64,8,128]{2,1,0:T(8,128)S(1)} %get-tuple-element.29), channel_id=1, source_target_pairs={{0,2},{2,4},{4,6},{6,0},{8,10},{10,12},{12,14},{14,8},{16,22},{18,... | collective-permute-start | bytes 786440 | tf_op jit(solution)/shard_map/ppermute | solution.py:407
  28.4 15.8 %collective-permute-start.8 = (f32[32,2,8,128]{3,2,1,0:T(8,128)S(1)}, f32[32,2,8,128]{3,2,1,0:T(8,128)S(1)}, u32[]{:S(2)}, u32[]{:S(2)}) collective-permute-start(f32[32,2,8,128]{3,2,1,0:T(8,128)S(1)} %get-tuple-element.31), channel_id=1, source_target_pairs={{0,6},{2,0},{4,2},{6,4},{8,14},{10,8},{12,10},{14,12},{16,18},{18,... | collective-permute-start | bytes 786440 | tf_op jit(solution)/shard_map/ppermute | solution.py:407
  32.3 13.4 %collective-permute-start.5 = (f32[32,2,8,128]{3,2,1,0:T(8,128)S(1)}, f32[32,2,8,128]{3,2,1,0:T(8,128)S(1)}, u32[]{:S(2)}, u32[]{:S(2)}) collective-permute-start(f32[32,2,8,128]{3,2,1,0:T(8,128)S(1)} %get-tuple-element.28), channel_id=1, source_target_pairs={{0,6},{2,0},{4,2},{6,4},{8,14},{10,8},{12,10},{14,12},{16,18},{18,... | collective-permute-start | bytes 786440 | tf_op jit(solution)/shard_map/ppermute | solution.py:407

commit v4 on v3

--- a/solution.py
+++ b/solution.py
@@ -9,7 +9,7 @@
 from jax.sharding import PartitionSpec as P
 
 KV = 32
-SPLIT = (1, 2)
+SPLIT = (5, 8)
 PARTED = ()
 LANES = 128
 ROWS = 8
@@ -447,7 +447,7 @@
     cells, *messages, secondary = call(
         pack_kernel, "pack", [whole] * (2 * chunks + 2),
         [cells_shape] + across_shape + primary_shape + [secondary_shape],
-        table, scratch=[held(levels), copies(levels)], static=(vel_size, levels, bounds),
+        pltpu.with_memory_space_constraint(table, pltpu.HBM), scratch=[held(levels), copies(levels)], static=(vel_size, levels, bounds),
     )
     arrived = exchange(messages[chunks:], secondary, [(m,) for m in messages[:chunks]])
     sectioned = call(

time: 47.6 us -> 45.4 us (0.954)
  starting transfers between devices: 20.4 us -> 16.9 us
  waiting for transfers between devices: 0.71 us -> 3.26 us
  local copies, waits for them, and re-layouts: 1.59 us -> 0 us
  Pallas kernels: 13.8 us -> 14.6 us
    ppermute x6, starting transfers between devices: 14.2 us -> 11.3 us  [along_x(): return lax.ppermute(array, ('vel', 'sx'), pairs)]
    ppermute x6, waiting for transfers between devices: 0.7 us -> 3.25 us  [along_x(): return lax.ppermute(array, ('vel', 'sx'), pairs)]
    unnamed x2 -> x0, local copies, waits for them, and re-layouts: 1.59 us -> none
    pallas_call x9, Pallas kernels: 13.8 us -> 14.6 us  [call(): pl.pallas_call(functools.partial(kernel, *static), out_shape=outs, in_spe...]
    ppermute x4, starting transfers between devices: 6.19 us -> 5.68 us  [along_y(): return (lax.ppermute(arrays[0], 'sy', ways[0]),)]
  transfers between devices with their start and end apart: 10 -> 10, of which waited for: 1 -> 4; matrix products, arithmetic and copies ran while one was open for 0% -> 0% of each run, Pallas kernels for 25% -> 26%
where the time goes in v4:
time: 45.4 us; the launch traced here: 45.2 us
  starting transfers between devices  16.9 us (37%)
  Pallas kernels  14.6 us (32%)
  blocking collectives  10.3 us (23%)
  waiting for transfers between devices  3.26 us (7%)
    pallas_call x9, Pallas kernels, call(): pl.pallas_call(functools.partial(kernel, *static), out_shape=outs, in_spe...  14.6 us
    ppermute x6, starting transfers between devices, along_x(): return lax.ppermute(array, ('vel', 'sx'), pairs)  11.3 us
    all_gather x2, blocking collectives, first_sums(): return lax.all_gather(sums, 'vel', axis=0, tiled=True)  10.3 us
    ppermute x4, starting transfers between devices, along_y(): return (lax.ppermute(arrays[0], 'sy', ways[0]),)  5.68 us
    ppermute x6, waiting for transfers between devices, along_x(): return lax.ppermute(array, ('vel', 'sx'), pairs)  3.25 us
  transfers between devices with their start and end apart: 10, of which 4 were waited for; matrix products, arithmetic and copies ran while one was open for 0% of the time, Pallas kernels for 26%

profile of v4, /device:TPU:0, one launch (start us, length us, event | category | flops | bytes accessed | tf_op | source)
XLA Modules:
  0.0 45.2 jit_solution(7872630798311114621)
XLA Ops:
  0.0 1.6 %pack.1 = (f32[64,64,128]{2,1,0:T(8,128)S(1)}, f32[2,20,3,8,128]{4,3,2,1,0:T(8,128)S(1)}, f32[2,12,3,8,128]{4,3,2,1,0:T(8,128)S(1)}, f32[40,2,8,128]{3,2,1,0:T(8...) custom-call(f32[8,8,8192]{2,1,0:T(8,128)} %table.1), custom_call_target="tpu_custom_call" | custom-call | tf_op jit(solution)/shard_map/pack/pallas_call | solution.py:391
  1.7 3.0 %collective-permute-start.2 = (f32[2,20,3,8,128]{4,3,2,1,0:T(8,128)S(1)}, f32[2,20,3,8,128]{4,3,2,1,0:T(8,128)S(1)}, u32[]{:S(2)}, u32[]{:S(2)}) collective-permute-start(f32[2,20,3,8,128]{4,3,2,1,0:T(8,128)S(1)} %get-tuple-element.22), channel_id=1, source_target_pairs={{0,1},{1,0},{2,3},{3,2},{4,5},{5,4},{6,7},{7,6},{8,9},{9,8},{10,11... | collective-permute-start | bytes 1474568 | tf_op jit(solution)/shard_map/ppermute | solution.py:414
  4.7 3.6 %collective-permute-start = (f32[40,2,8,128]{3,2,1,0:T(8,128)S(1)}, f32[40,2,8,128]{3,2,1,0:T(8,128)S(1)}, u32[]{:S(2)}, u32[]{:S(2)}) collective-permute-start(f32[40,2,8,128]{3,2,1,0:T(8,128)S(1)} %get-tuple-element.20), channel_id=1, source_target_pairs={{0,6},{2,0},{4,2},{6,4},{8,14},{10,8},{12,10},{14,12},{16,18},{18,... | collective-permute-start | bytes 983048 | tf_op jit(solution)/shard_map/ppermute | solution.py:407
  8.3 0.0 collective-permute-start.1
  8.3 0.5 %collective-permute-start.4 = (f32[2,12,3,8,128]{4,3,2,1,0:T(8,128)S(1)}, f32[2,12,3,8,128]{4,3,2,1,0:T(8,128)S(1)}, u32[]{:S(2)}, u32[]{:S(2)}) collective-permute-start(f32[2,12,3,8,128]{4,3,2,1,0:T(8,128)S(1)} %get-tuple-element.25), channel_id=1, source_target_pairs={{0,1},{1,0},{2,3},{3,2},{4,5},{5,4},{6,7},{7,6},{8,9},{9,8},{10,11... | collective-permute-start | bytes 884744 | tf_op jit(solution)/shard_map/ppermute | solution.py:414
  8.8 3.8 %collective-permute-start.3 = (f32[24,2,8,128]{3,2,1,0:T(8,128)S(1)}, f32[24,2,8,128]{3,2,1,0:T(8,128)S(1)}, u32[]{:S(2)}, u32[]{:S(2)}) collective-permute-start(f32[24,2,8,128]{3,2,1,0:T(8,128)S(1)} %get-tuple-element.24), channel_id=1, source_target_pairs={{0,6},{2,0},{4,2},{6,4},{8,14},{10,8},{12,10},{14,12},{16,18},{18,... | collective-permute-start | bytes 589832 | tf_op jit(solution)/shard_map/ppermute | solution.py:407
  12.6 1.5 %sums.2 = f32[8,128]{1,0:T(8,128)S(1)} custom-call(f32[64,64,128]{2,1,0:T(8,128)S(1)} %get-tuple-element.19.cells.refs_0_.refs_2_), custom_call_target="tpu_custom_call" | custom-call | tf_op jit(solution)/shard_map/sums/pallas_call | solution.py:391
  14.2 5.2 %all_gather.6.refs_1_ = f32[32,128]{1,0:T(8,128)S(1)} all-gather(f32[8,128]{1,0:T(8,128)S(1)} %sums.2), channel_id=1, replica_groups=mesh['vel'=4,'sx'=4,'sy'=2] {'vel'}, dimensions={0}, use_global_device_ids=true | all-gather | bytes 20480 | tf_op jit(solution)/shard_map/all_gather | solution.py:427
  19.3 3.0 %local.2.partial = f32[64,64,128]{2,1,0:T(8,128)S(1)} custom-call(f32[64,64,128]{2,1,0:T(8,128)S(1)} %get-tuple-element.19.cells.refs_0_.refs_2_, f32[32,128]{1,0:T(8,128)S(1)} %all_gather.6.refs_1_), custom_call_target="tpu_custom_call" | custom-call | tf_op jit(solution)/shard_map/local/pallas_call | solution.py:391
  22.3 0.7 %collective-permute-done.1.from_x2 = f32[64,8,128]{2,1,0:T(8,128)S(1)} collective-permute-done((f32[64,8,128]{2,1,0:T(8,128)S(1)}, f32[64,8,128]{2,1,0:T(8,128)S(1)}, u32[]{:S(2)}, u32[]{:S(2)}) %collective-permute-start.1) | collective-permute-done | bytes 262176 | tf_op jit(solution)/shard_map/ppermute | solution.py:407
  23.0 0.0 collective-permute-done.from_x1
  23.0 0.0 collective-permute-done.2.from_y
  23.0 0.7 %correct.2 = (f32[64,64,128]{2,1,0:T(8,128)S(1)}, f32[40,2,8,128]{3,2,1,0:T(8,128)S(1)}, f32[64,8,128]{2,1,0:T(8,128)S(1)}, f32[2,20,3,8,128]{4,3,2,1,0:T(8,128)S(1)}) custom-call(f32[64,64,128]{2,1,0:T(8,128)S(1)} %local.2.partial, f32[64,64,128]{2,1,0:T(8,128)S(1)} %get-tuple-element.19.cells.refs_0_.refs_2_, ...), custom_call_target="tpu_custom_call", output_to_operand_aliasing={{0}: (0, {})} | custom-call | tf_op jit(solution)/shard_map/correct/pallas_call | solution.py:391
  23.7 0.9 %collective-permute-start.9 = (f32[2,20,3,8,128]{4,3,2,1,0:T(8,128)S(1)}, f32[2,20,3,8,128]{4,3,2,1,0:T(8,128)S(1)}, u32[]{:S(2)}, u32[]{:S(2)}) collective-permute-start(f32[2,20,3,8,128]{4,3,2,1,0:T(8,128)S(1)} %get-tuple-element.32), channel_id=1, source_target_pairs={{0,1},{1,0},{2,3},{3,2},{4,5},{5,4},{6,7},{7,6},{8,9},{9,8},{10,11... | collective-permute-start | bytes 1474568 | tf_op jit(solution)/shard_map/ppermute | solution.py:414
  24.6 0.0 collective-permute-start.8
  24.6 0.2 collective-permute-done.3.from_x1
  24.8 0.0 collective-permute-done.4.from_y
  24.8 0.4 correct.3
  25.2 1.2 %collective-permute-start.7 = (f32[2,12,3,8,128]{4,3,2,1,0:T(8,128)S(1)}, f32[2,12,3,8,128]{4,3,2,1,0:T(8,128)S(1)}, u32[]{:S(2)}, u32[]{:S(2)}) collective-permute-start(f32[2,12,3,8,128]{4,3,2,1,0:T(8,128)S(1)} %get-tuple-element.30), channel_id=1, source_target_pairs={{0,1},{1,0},{2,3},{3,2},{4,5},{5,4},{6,7},{7,6},{8,9},{9,8},{10,11... | collective-permute-start | bytes 884744 | tf_op jit(solution)/shard_map/ppermute | solution.py:414
  26.5 1.8 %collective-permute-start.6 = (f32[64,8,128]{2,1,0:T(8,128)S(1)}, f32[64,8,128]{2,1,0:T(8,128)S(1)}, u32[]{:S(2)}, u32[]{:S(2)}) collective-permute-start(f32[64,8,128]{2,1,0:T(8,128)S(1)} %get-tuple-element.29), channel_id=1, source_target_pairs={{0,2},{2,4},{4,6},{6,0},{8,10},{10,12},{12,14},{14,8},{16,22},{18,... | collective-permute-start | bytes 786440 | tf_op jit(solution)/shard_map/ppermute | solution.py:407
  28.3 2.0 %collective-permute-start.5 = (f32[24,2,8,128]{3,2,1,0:T(8,128)S(1)}, f32[24,2,8,128]{3,2,1,0:T(8,128)S(1)}, u32[]{:S(2)}, u32[]{:S(2)}) collective-permute-start(f32[24,2,8,128]{3,2,1,0:T(8,128)S(1)} %get-tuple-element.28), channel_id=1, source_target_pairs={{0,6},{2,0},{4,2},{6,4},{8,14},{10,8},{12,10},{14,12},{16,18},{18,... | collective-permute-start | bytes 589832 | tf_op jit(solution)/shard_map/ppermute | solution.py:407
  30.3 1.5 %sums.3 = f32[8,128]{1,0:T(8,128)S(1)} custom-call(f32[64,64,128]{2,1,0:T(8,128)S(1)} %get-tuple-element.27.cells.refs_0_), custom_call_target="tpu_custom_call" | custom-call | tf_op jit(solution)/shard_map/sums/pallas_call | solution.py:391
  31.8 5.2 %all_gather.7.refs_1_ = f32[32,128]{1,0:T(8,128)S(1)} all-gather(f32[8,128]{1,0:T(8,128)S(1)} %sums.3), channel_id=1, replica_groups=mesh['vel'=4,'sx'=4,'sy'=2] {'vel'}, dimensions={0}, use_global_device_ids=true | all-gather | bytes 20480 | tf_op jit(solution)/shard_map/all_gather | solution.py:427
  37.0 3.2 %local.3.partial = f32[64,64,128]{2,1,0:T(8,128)S(1)} custom-call(f32[64,64,128]{2,1,0:T(8,128)S(1)} %get-tuple-element.27.cells.refs_0_, f32[32,128]{1,0:T(8,128)S(1)} %all_gather.7.refs_1_, f32[64,64,128]{2,1,0:T(8,128)S(1)} %get-tuple-element.19.cells.refs_0_.refs_2_), custom_call_target="tpu_custom_call" | custom-call | tf_op jit(solution)/shard_map/local/pallas_call | solution.py:391
  40.2 0.0 collective-permute-done.6.from_x2
  40.2 0.5 %collective-permute-done.8.from_x1 = f32[40,2,8,128]{3,2,1,0:T(8,128)S(1)} collective-permute-done((f32[40,2,8,128]{3,2,1,0:T(8,128)S(1)}, f32[40,2,8,128]{3,2,1,0:T(8,128)S(1)}, u32[]{:S(2)}, u32[]{:S(2)}) %collective-permute-start.8) | collective-permute-done | bytes 327712 | tf_op jit(solution)/shard_map/ppermute | solution.py:407
  40.8 0.0 collective-permute-done.9.refs_0_
  40.8 1.5 %finish.2.refs_1_ = f32[8,8,8192]{2,1,0:T(8,128)} custom-call(f32[64,64,128]{2,1,0:T(8,128)S(1)} %local.3.partial, f32[64,64,128]{2,1,0:T(8,128)S(1)} %get-tuple-element.27.cells.refs_0_, f32[40,2,8,128]{3,2,1,0:T(8,128)S(1)} %collective-permute-done.8.from_x1, f32[64,8,128]{2,1,0:T(8,128)S(1)} %collective-permute-done.6.from_x2, ...), custom_call_target="tpu_custom_call" | custom-call | tf_op jit(solution)/shard_map/finish/pallas_call | solution.py:391
  42.3 1.8 %collective-permute-done.5.from_x1 = f32[24,2,8,128]{3,2,1,0:T(8,128)S(1)} collective-permute-done((f32[24,2,8,128]{3,2,1,0:T(8,128)S(1)}, f32[24,2,8,128]{3,2,1,0:T(8,128)S(1)}, u32[]{:S(2)}, u32[]{:S(2)}) %collective-permute-start.5) | collective-permute-done | bytes 196640 | tf_op jit(solution)/shard_map/ppermute | solution.py:407
  44.0 0.0 collective-permute-done.7.refs_0_
  44.0 1.2 %finish.3 = f32[8,8,8192]{2,1,0:T(8,128)} custom-call(f32[64,64,128]{2,1,0:T(8,128)S(1)} %local.3.partial, f32[64,64,128]{2,1,0:T(8,128)S(1)} %get-tuple-element.27.cells.refs_0_, f32[24,2,8,128]{3,2,1,0:T(8,128)S(1)} %collective-permute-done.5.from_x1, f32[64,8,128]{2,1,0:T(8,128)S(1)} %collective-permute-done.6.from_x2, ...), custom_call_target="tpu_custom_call", output_to_operand_aliasing={{}: (5, {})} | custom-call | tf_op jit(solution)/shard_map/finish/pallas_call | solution.py:391
Async XLA Ops:
  1.7 21.3 %collective-permute-start.2 = (f32[2,20,3,8,128]{4,3,2,1,0:T(8,128)S(1)}, f32[2,20,3,8,128]{4,3,2,1,0:T(8,128)S(1)}, u32[]{:S(2)}, u32[]{:S(2)}) collective-permute-start(f32[2,20,3,8,128]{4,3,2,1,0:T(8,128)S(1)} %get-tuple-element.22), channel_id=1, source_target_pairs={{0,1},{1,0},{2,3},{3,2},{4,5},{5,4},{6,7},{7,6},{8,9},{9,8},{10,11... | collective-permute-start | bytes 1474568 | tf_op jit(solution)/shard_map/ppermute | solution.py:414
  4.7 18.3 %collective-permute-start = (f32[40,2,8,128]{3,2,1,0:T(8,128)S(1)}, f32[40,2,8,128]{3,2,1,0:T(8,128)S(1)}, u32[]{:S(2)}, u32[]{:S(2)}) collective-permute-start(f32[40,2,8,128]{3,2,1,0:T(8,128)S(1)} %get-tuple-element.20), channel_id=1, source_target_pairs={{0,6},{2,0},{4,2},{6,4},{8,14},{10,8},{12,10},{14,12},{16,18},{18,... | collective-permute-start | bytes 983048 | tf_op jit(solution)/shard_map/ppermute | solution.py:407
  8.3 14.7 %collective-permute-start.1 = (f32[64,8,128]{2,1,0:T(8,128)S(1)}, f32[64,8,128]{2,1,0:T(8,128)S(1)}, u32[]{:S(2)}, u32[]{:S(2)}) collective-permute-start(f32[64,8,128]{2,1,0:T(8,128)S(1)} %get-tuple-element.21), channel_id=1, source_target_pairs={{0,2},{2,4},{4,6},{6,0},{8,10},{10,12},{12,14},{14,8},{16,22},{18,... | collective-permute-start | bytes 786440 | tf_op jit(solution)/shard_map/ppermute | solution.py:407
  8.3 16.6 %collective-permute-start.4 = (f32[2,12,3,8,128]{4,3,2,1,0:T(8,128)S(1)}, f32[2,12,3,8,128]{4,3,2,1,0:T(8,128)S(1)}, u32[]{:S(2)}, u32[]{:S(2)}) collective-permute-start(f32[2,12,3,8,128]{4,3,2,1,0:T(8,128)S(1)} %get-tuple-element.25), channel_id=1, source_target_pairs={{0,1},{1,0},{2,3},{3,2},{4,5},{5,4},{6,7},{7,6},{8,9},{9,8},{10,11... | collective-permute-start | bytes 884744 | tf_op jit(solution)/shard_map/ppermute | solution.py:414
  8.8 16.0 %collective-permute-start.3 = (f32[24,2,8,128]{3,2,1,0:T(8,128)S(1)}, f32[24,2,8,128]{3,2,1,0:T(8,128)S(1)}, u32[]{:S(2)}, u32[]{:S(2)}) collective-permute-start(f32[24,2,8,128]{3,2,1,0:T(8,128)S(1)} %get-tuple-element.24), channel_id=1, source_target_pairs={{0,6},{2,0},{4,2},{6,4},{8,14},{10,8},{12,10},{14,12},{16,18},{18,... | collective-permute-start | bytes 589832 | tf_op jit(solution)/shard_map/ppermute | solution.py:407
  23.7 17.1 %collective-permute-start.9 = (f32[2,20,3,8,128]{4,3,2,1,0:T(8,128)S(1)}, f32[2,20,3,8,128]{4,3,2,1,0:T(8,128)S(1)}, u32[]{:S(2)}, u32[]{:S(2)}) collective-permute-start(f32[2,20,3,8,128]{4,3,2,1,0:T(8,128)S(1)} %get-tuple-element.32), channel_id=1, source_target_pairs={{0,1},{1,0},{2,3},{3,2},{4,5},{5,4},{6,7},{7,6},{8,9},{9,8},{10,11... | collective-permute-start | bytes 1474568 | tf_op jit(solution)/shard_map/ppermute | solution.py:414
  24.6 16.2 %collective-permute-start.8 = (f32[40,2,8,128]{3,2,1,0:T(8,128)S(1)}, f32[40,2,8,128]{3,2,1,0:T(8,128)S(1)}, u32[]{:S(2)}, u32[]{:S(2)}) collective-permute-start(f32[40,2,8,128]{3,2,1,0:T(8,128)S(1)} %get-tuple-element.31), channel_id=1, source_target_pairs={{0,6},{2,0},{4,2},{6,4},{8,14},{10,8},{12,10},{14,12},{16,18},{18,... | collective-permute-start | bytes 983048 | tf_op jit(solution)/shard_map/ppermute | solution.py:407
  25.2 18.8 %collective-permute-start.7 = (f32[2,12,3,8,128]{4,3,2,1,0:T(8,128)S(1)}, f32[2,12,3,8,128]{4,3,2,1,0:T(8,128)S(1)}, u32[]{:S(2)}, u32[]{:S(2)}) collective-permute-start(f32[2,12,3,8,128]{4,3,2,1,0:T(8,128)S(1)} %get-tuple-element.30), channel_id=1, source_target_pairs={{0,1},{1,0},{2,3},{3,2},{4,5},{5,4},{6,7},{7,6},{8,9},{9,8},{10,11... | collective-permute-start | bytes 884744 | tf_op jit(solution)/shard_map/ppermute | solution.py:414
  26.5 13.7 %collective-permute-start.6 = (f32[64,8,128]{2,1,0:T(8,128)S(1)}, f32[64,8,128]{2,1,0:T(8,128)S(1)}, u32[]{:S(2)}, u32[]{:S(2)}) collective-permute-start(f32[64,8,128]{2,1,0:T(8,128)S(1)} %get-tuple-element.29), channel_id=1, source_target_pairs={{0,2},{2,4},{4,6},{6,0},{8,10},{10,12},{12,14},{14,8},{16,22},{18,... | collective-permute-start | bytes 786440 | tf_op jit(solution)/shard_map/ppermute | solution.py:407
  28.3 15.8 %collective-permute-start.5 = (f32[24,2,8,128]{3,2,1,0:T(8,128)S(1)}, f32[24,2,8,128]{3,2,1,0:T(8,128)S(1)}, u32[]{:S(2)}, u32[]{:S(2)}) collective-permute-start(f32[24,2,8,128]{3,2,1,0:T(8,128)S(1)} %get-tuple-element.28), channel_id=1, source_target_pairs={{0,6},{2,0},{4,2},{6,4},{8,14},{10,8},{12,10},{14,12},{16,18},{18,... | collective-permute-start | bytes 589832 | tf_op jit(solution)/shard_map/ppermute | solution.py:407

commit v5 on v4

--- a/solution.py
+++ b/solution.py
@@ -10,7 +10,6 @@
 
 KV = 32
 SPLIT = (5, 8)
-PARTED = ()
 LANES = 128
 ROWS = 8
 
@@ -96,7 +95,7 @@
 
 def pack_kernel(vel_size, levels, bounds, table, cells, *refs):
     chunks = len(bounds)
-    across, primary, secondary = refs[:chunks], refs[chunks : 2 * chunks], refs[2 * chunks]
+    across, primary, secondary = refs[:chunks], refs[chunks], refs[chunks + 1]
     held, sems = refs[-2], refs[-1]
     rows = [row_of(x) for x in order_of(flow_of(vel_size))]
     width = TILES * LANES
@@ -119,21 +118,34 @@
                         cells[tile, x * ROWS : (x + 1) * ROWS, :] = held[
                             level, x, :, sub * LANES : (sub + 1) * LANES
                         ]
-                    primary[c][tile - begin * TILES, 0] = cells[tile, rows[6], :]
-                    primary[c][tile - begin * TILES, 1] = cells[tile, rows[7], :]
+                    if c == 0:
+                        primary[tile, 0] = cells[tile, rows[6], :]
+                        primary[tile, 1] = cells[tile, rows[7], :]
                     secondary[tile] = cells[tile, rows[0], :]
-                send_y(cells, (level - begin) * HALF + quarter, low, high, halves(across[c : c + 1]))
+                send_y(cells, (level - begin) * HALF + quarter, low, high, halves(across[c]))
             return carry
 
         lax.fori_loop(begin, end, one, 0)
 
 
-def halves(refs):
-    return refs if len(refs) == 2 else [refs[0].at[0], refs[0].at[1]]
-
-
-def sums_kernel(levels, cells, *refs):
-    sums = refs[-1]
+def late_kernel(vel_size, begin, end, cells, after, primary):
+    rows = [row_of(x) for x in order_of(flow_of(vel_size))]
+
+    def one(level, carry):
+        for sub in range(TILES):
+            tile = level * TILES + sub
+            primary[tile - begin * TILES, 0] = cells[tile, rows[6], :]
+            primary[tile - begin * TILES, 1] = cells[tile, rows[7], :]
+        return carry
+
+    lax.fori_loop(begin, end, one, 0)
+
+
+def halves(across):
+    return across.at[0], across.at[1]
+
+
+def sums_kernel(levels, cells, sums):
     lane = lane_index()
     base = lax.axis_index("vel") * levels
     speed = [component(base + level) for level in range(levels)]
@@ -277,10 +289,9 @@
 GROUP = 1
 
 
-def correct_kernel(vel_size, levels, start, stop, parted, partial, cells, from_x1, from_x2, from_y, *refs):
-    across = halves(refs[-1 - parted :])
-    out, primary, secondary = refs[-4 - parted : -1 - parted]
-    from_y = halves([from_y])
+def correct_kernel(vel_size, levels, start, stop, partial, cells, from_x1, from_x2, from_y, *refs):
+    out, primary, secondary, across = refs[-4:]
+    across, from_y = halves(across), halves(from_y)
     base = lax.axis_index("vel") * levels
     xs = order_of(flow_of(vel_size))
     rows = [row_of(x) for x in xs]
@@ -322,8 +333,8 @@
     lax.fori_loop(start, stop, one, 0)
 
 
-def finish_kernel(vel_size, levels, start, stop, parted, partial, cells, from_x1, from_x2, *refs):
-    from_y = halves(refs[: 1 + parted])
+def finish_kernel(vel_size, levels, start, stop, partial, cells, from_x1, from_x2, from_y, *refs):
+    from_y = halves(from_y)
     result, held, side, sems = refs[-4:]
     base = lax.axis_index("vel") * levels
     xs = order_of(flow_of(vel_size))
@@ -406,34 +417,23 @@
             pairs += [(v * sx_size + i, v * sx_size + (i + way) % sx_size) for i in range(sx_size)]
         return lax.ppermute(array, ("vel", "sx"), pairs)
 
-    def along_y(arrays):
+    def along_y(array):
         ways = [[(i, (i + way) % sy_size) for i in range(sy_size)] for way in (1, -1)]
-        if len(arrays) == 2:
-            return tuple(lax.ppermute(a, "sy", way) for a, way in zip(arrays, ways))
         if sy_size == 2:
-            return (lax.ppermute(arrays[0], "sy", ways[0]),)
-        return (jnp.stack([lax.ppermute(arrays[0][i], "sy", ways[i]) for i in (0, 1)]),)
+            return lax.ppermute(array, "sy", ways[0])
+        return jnp.stack([lax.ppermute(array[i], "sy", ways[i]) for i in (0, 1)])
 
     def exchange(primary, secondary, across):
         behind = along_x(secondary, -1)
-        return [(along_x(p, 1), behind, *along_y(a)) for p, a in zip(primary, across)]
-
-    def sums_of(cells, *after):
-        return call(sums_kernel, "sums", whole, shape(ROWS, LANES), cells, *after, static=(levels,))
+        return [(along_x(p, 1), behind, along_y(a)) for p, a in zip(primary, across)]
+
+    def sums_of(cells):
+        return call(sums_kernel, "sums", whole, shape(ROWS, LANES), cells, static=(levels,))
 
     def first_sums(sums):
         if vel_size > 4:
             return lax.psum(sums, "vel")
         return lax.all_gather(sums, "vel", axis=0, tiled=True)
-
-    def second_sums(sums):
-        if vel_size & (vel_size - 1):
-            return lax.psum(sums, "vel")
-        d = 1
-        while d < vel_size:
-            sums = sums + lax.ppermute(sums, "vel", [(i, i ^ d) for i in range(vel_size)])
-            d *= 2
-        return sums
 
     table_scratch = [
         pltpu.VMEM((ROWS, TILES, 3, ROWS, LANES), f32),
@@ -444,31 +444,38 @@
     held = lambda count: pltpu.VMEM((count, ROWS, ROWS, TILES * LANES), f32)
     copies = lambda count: pltpu.SemaphoreType.DMA((count,))
 
-    cells, *messages, secondary = call(
-        pack_kernel, "pack", [whole] * (2 * chunks + 2),
-        [cells_shape] + across_shape + primary_shape + [secondary_shape],
-        pltpu.with_memory_space_constraint(table, pltpu.HBM), scratch=[held(levels), copies(levels)], static=(vel_size, levels, bounds),
+    cells, *across, primary, secondary = call(
+        pack_kernel, "pack", [whole] * (chunks + 3),
+        [cells_shape] + across_shape + [primary_shape[0], secondary_shape],
+        pltpu.with_memory_space_constraint(table, pltpu.HBM),
+        scratch=[held(levels), copies(levels)], static=(vel_size, levels, bounds),
     )
-    arrived = exchange(messages[chunks:], secondary, [(m,) for m in messages[:chunks]])
+    sums = first_sums(sums_of(cells))
+    primary = [primary]
+    for c in range(1, chunks):
+        primary.append(
+            call(
+                late_kernel, "late", whole, primary_shape[c], cells, sums,
+                static=(vel_size, *bounds[c]),
+            )
+        )
+    arrived = exchange(primary, secondary, across)
     sectioned = call(
-        local_kernel, "local", whole, cells_shape, cells, first_sums(sums_of(cells)),
+        local_kernel, "local", whole, cells_shape, cells, sums,
         scratch=table_scratch, static=(vel_size, levels, False),
     )
     primary, across, partly = [], [], ()
     for c, (begin, end) in enumerate(bounds):
-        parted = int(c in PARTED)
-        one_way = shape((end - begin) * HALF, 3, ROWS, LANES)
-        sectioned, first, secondary, *sides = call(
-            correct_kernel, "correct", [whole] * (4 + parted),
-            [cells_shape, primary_shape[c], secondary_shape]
-            + ([one_way] * 2 if parted else [across_shape[c]]),
+        sectioned, first, secondary, last = call(
+            correct_kernel, "correct", [whole] * 4,
+            [cells_shape, primary_shape[c], secondary_shape, across_shape[c]],
             sectioned, cells, *arrived[c], *partly,
-            static=(vel_size, levels, begin, end, parted),
+            static=(vel_size, levels, begin, end),
             aliases={0: 0, 5: 2} if partly else {0: 0},
         )
         partly = (secondary,)
         primary.append(first)
-        across.append(sides)
+        across.append(last)
     arrived = exchange(primary, secondary, across)
     sums = first_sums(sums_of(sectioned))
     partial = call(
@@ -486,8 +493,8 @@
                     pltpu.VMEM((TILES, ROWS * ROWS, LANES), f32),
                     copies(end - begin),
                 ],
-                static=(vel_size, levels, begin, end, int(c in PARTED)),
-                aliases={2 + len(arrived[c]): 0} if result else {},
+                static=(vel_size, levels, begin, end),
+                aliases={5: 0} if result else {},
             ),
         )
     return result[0]

time: 45.4 us -> 45.2 us (level)
    pallas_call x9 -> x10, Pallas kernels: 14.6 us -> 14.7 us  [call(): pl.pallas_call(functools.partial(kernel, *static), out_shape=outs, in_spe...]
  transfers between devices with their start and end apart: 10 -> 10, of which waited for: 4 -> 3; matrix products, arithmetic and copies ran while one was open for 0% -> 0% of each run, Pallas kernels for 26% -> 26%
where the time goes in v5:
time: 45.2 us; the launch traced here: 45 us
  starting transfers between devices  17 us (38%)
  Pallas kernels  14.7 us (33%)
  blocking collectives  10.3 us (23%)
  waiting for transfers between devices  2.94 us (7%)
    pallas_call x10, Pallas kernels, call(): pl.pallas_call(functools.partial(kernel, *static), out_shape=outs, in_spe...  14.7 us
    ppermute x6, starting transfers between devices, along_x(): return lax.ppermute(array, ('vel', 'sx'), pairs)  11.3 us
    all_gather x2, blocking collectives, first_sums(): return lax.all_gather(sums, 'vel', axis=0, tiled=True)  10.3 us
    ppermute x4, starting transfers between devices, along_y(): return lax.ppermute(array, 'sy', ways[0])  5.7 us
    ppermute x6, waiting for transfers between devices, along_x(): return lax.ppermute(array, ('vel', 'sx'), pairs)  2.93 us
  transfers between devices with their start and end apart: 10, of which 3 were waited for; matrix products, arithmetic and copies ran while one was open for 0% of the time, Pallas kernels for 26%

profile of v5, /device:TPU:0, one launch (start us, length us, event | category | flops | bytes accessed | tf_op | source)
XLA Modules:
  0.0 45.0 jit_solution(5721398299262174076)
XLA Ops:
  0.0 1.6 %pack.1 = (f32[64,64,128]{2,1,0:T(8,128)S(1)}, f32[2,20,3,8,128]{4,3,2,1,0:T(8,128)S(1)}, f32[2,12,3,8,128]{4,3,2,1,0:T(8,128)S(1)}, f32[40,2,8,128]{3,2,1,0:T(8,128)S(1)}, f32[64,8,128]{2,1,0:T(8,128)S(1)}) custom-call(f32[8,8,8192]{2,1,0:T(8,128)} %table.1), custom_call_target="tpu_custom_call" | custom-call | tf_op jit(solution)/shard_map/pack/pallas_call | solution.py:402
  1.7 3.0 %collective-permute-start.2 = (f32[2,20,3,8,128]{4,3,2,1,0:T(8,128)S(1)}, f32[2,20,3,8,128]{4,3,2,1,0:T(8,128)S(1)}, u32[]{:S(2)}, u32[]{:S(2)}) collective-permute-start(f32[2,20,3,8,128]{4,3,2,1,0:T(8,128)S(1)} %get-tuple-element.21), channel_id=1, source_target_pairs={{0,1},{1,0},{2,3},{3,2},{4,5},{5,4},{6,7},{7,6},{8,9},{9,8},{10,11... | collective-permute-start | bytes 1474568 | tf_op jit(solution)/shard_map/ppermute | solution.py:423
  4.7 3.6 %collective-permute-start = (f32[40,2,8,128]{3,2,1,0:T(8,128)S(1)}, f32[40,2,8,128]{3,2,1,0:T(8,128)S(1)}, u32[]{:S(2)}, u32[]{:S(2)}) collective-permute-start(f32[40,2,8,128]{3,2,1,0:T(8,128)S(1)} %get-tuple-element.19), channel_id=1, source_target_pairs={{0,6},{2,0},{4,2},{6,4},{8,14},{10,8},{12,10},{14,12},{16,18},{18,... | collective-permute-start | bytes 983048 | tf_op jit(solution)/shard_map/ppermute | solution.py:418
  8.3 0.0 collective-permute-start.1
  8.3 0.5 %collective-permute-start.4 = (f32[2,12,3,8,128]{4,3,2,1,0:T(8,128)S(1)}, f32[2,12,3,8,128]{4,3,2,1,0:T(8,128)S(1)}, u32[]{:S(2)}, u32[]{:S(2)}) collective-permute-start(f32[2,12,3,8,128]{4,3,2,1,0:T(8,128)S(1)} %get-tuple-element.23), channel_id=1, source_target_pairs={{0,1},{1,0},{2,3},{3,2},{4,5},{5,4},{6,7},{7,6},{8,9},{9,8},{10,11... | collective-permute-start | bytes 884744 | tf_op jit(solution)/shard_map/ppermute | solution.py:423
  8.8 1.5 %sums.2 = f32[8,128]{1,0:T(8,128)S(1)} custom-call(f32[64,64,128]{2,1,0:T(8,128)S(1)} %get-tuple-element.18.cells.refs_0_.refs_2_), custom_call_target="tpu_custom_call" | custom-call | tf_op jit(solution)/shard_map/sums/pallas_call | solution.py:402
  10.3 5.2 %all_gather.6.refs_1_.after = f32[32,128]{1,0:T(8,128)S(1)} all-gather(f32[8,128]{1,0:T(8,128)S(1)} %sums.2), channel_id=1, replica_groups=mesh['vel'=4,'sx'=4,'sy'=2] {'vel'}, dimensions={0}, use_global_device_ids=true | all-gather | bytes 20480 | tf_op jit(solution)/shard_map/all_gather | solution.py:436
  15.5 3.9 %collective-permute-start.3 = (f32[24,2,8,128]{3,2,1,0:T(8,128)S(1)}, f32[24,2,8,128]{3,2,1,0:T(8,128)S(1)}, u32[]{:S(2)}, u32[]{:S(2)}) collective-permute-start(f32[24,2,8,128]{3,2,1,0:T(8,128)S(1)} %late.1), channel_id=1, source_target_pairs={{0,6},{2,0},{4,2},{6,4},{8,14},{10,8},{12,10},{14,12},{16,18},{18,... | collective-permute-start | bytes 589832 | tf_op jit(solution)/shard_map/ppermute | solution.py:418
  19.4 3.0 %local.2.partial = f32[64,64,128]{2,1,0:T(8,128)S(1)} custom-call(f32[64,64,128]{2,1,0:T(8,128)S(1)} %get-tuple-element.18.cells.refs_0_.refs_2_, f32[32,128]{1,0:T(8,128)S(1)} %all_gather.6.refs_1_.after), custom_call_target="tpu_custom_call" | custom-call | tf_op jit(solution)/shard_map/local/pallas_call | solution.py:402
  22.4 0.0 collective-permute-done.1.from_x2
  22.4 0.0 collective-permute-done.from_x1
  22.4 0.0 collective-permute-done.2.from_y
  22.4 0.7 %correct.2 = (f32[64,64,128]{2,1,0:T(8,128)S(1)}, f32[40,2,8,128]{3,2,1,0:T(8,128)S(1)}, f32[64,8,128]{2,1,0:T(8,128)S(1)}, f32[2,20,3,8,128]{4,3,2,1,0:T(8,128)S(1)}) custom-call(f32[64,64,128]{2,1,0:T(8,128)S(1)} %local.2.partial, f32[64,64,128]{2,1,0:T(8,128)S(1)} %get-tuple-element.18.cells.refs_0_.refs_2_, ...), custom_call_target="tpu_custom_call", output_to_operand_aliasing={{0}: (0, {})} | custom-call | tf_op jit(solution)/shard_map/correct/pallas_call | solution.py:402
  23.1 1.6 %collective-permute-start.9 = (f32[2,20,3,8,128]{4,3,2,1,0:T(8,128)S(1)}, f32[2,20,3,8,128]{4,3,2,1,0:T(8,128)S(1)}, u32[]{:S(2)}, u32[]{:S(2)}) collective-permute-start(f32[2,20,3,8,128]{4,3,2,1,0:T(8,128)S(1)} %get-tuple-element.30), channel_id=1, source_target_pairs={{0,1},{1,0},{2,3},{3,2},{4,5},{5,4},{6,7},{7,6},{8,9},{9,8},{10,11... | collective-permute-start | bytes 1474568 | tf_op jit(solution)/shard_map/ppermute | solution.py:423
  24.7 0.0 collective-permute-start.8
  24.7 1.1 %collective-permute-done.3.from_x1 = f32[24,2,8,128]{3,2,1,0:T(8,128)S(1)} collective-permute-done((f32[24,2,8,128]{3,2,1,0:T(8,128)S(1)}, f32[24,2,8,128]{3,2,1,0:T(8,128)S(1)}, u32[]{:S(2)}, u32[]{:S(2)}) %collective-permute-start.3) | collective-permute-done | bytes 196640 | tf_op jit(solution)/shard_map/ppermute | solution.py:418
  25.7 0.0 collective-permute-done.4.from_y
  25.7 0.4 correct.3
  26.2 0.6 %collective-permute-start.7 = (f32[2,12,3,8,128]{4,3,2,1,0:T(8,128)S(1)}, f32[2,12,3,8,128]{4,3,2,1,0:T(8,128)S(1)}, u32[]{:S(2)}, u32[]{:S(2)}) collective-permute-start(f32[2,12,3,8,128]{4,3,2,1,0:T(8,128)S(1)} %get-tuple-element.28), channel_id=1, source_target_pairs={{0,1},{1,0},{2,3},{3,2},{4,5},{5,4},{6,7},{7,6},{8,9},{9,8},{10,11... | collective-permute-start | bytes 884744 | tf_op jit(solution)/shard_map/ppermute | solution.py:423
  26.8 1.0 %collective-permute-start.6 = (f32[64,8,128]{2,1,0:T(8,128)S(1)}, f32[64,8,128]{2,1,0:T(8,128)S(1)}, u32[]{:S(2)}, u32[]{:S(2)}) collective-permute-start(f32[64,8,128]{2,1,0:T(8,128)S(1)} %get-tuple-element.27), channel_id=1, source_target_pairs={{0,2},{2,4},{4,6},{6,0},{8,10},{10,12},{12,14},{14,8},{16,22},{18,... | collective-permute-start | bytes 786440 | tf_op jit(solution)/shard_map/ppermute | solution.py:418
  27.7 2.9 %collective-permute-start.5 = (f32[24,2,8,128]{3,2,1,0:T(8,128)S(1)}, f32[24,2,8,128]{3,2,1,0:T(8,128)S(1)}, u32[]{:S(2)}, u32[]{:S(2)}) collective-permute-start(f32[24,2,8,128]{3,2,1,0:T(8,128)S(1)} %get-tuple-element.26), channel_id=1, source_target_pairs={{0,6},{2,0},{4,2},{6,4},{8,14},{10,8},{12,10},{14,12},{16,18},{18,... | collective-permute-start | bytes 589832 | tf_op jit(solution)/shard_map/ppermute | solution.py:418
  30.6 1.5 %sums.3 = f32[8,128]{1,0:T(8,128)S(1)} custom-call(f32[64,64,128]{2,1,0:T(8,128)S(1)} %get-tuple-element.25.cells.refs_0_), custom_call_target="tpu_custom_call" | custom-call | tf_op jit(solution)/shard_map/sums/pallas_call | solution.py:402
  32.1 5.2 %all_gather.7.refs_1_ = f32[32,128]{1,0:T(8,128)S(1)} all-gather(f32[8,128]{1,0:T(8,128)S(1)} %sums.3), channel_id=1, replica_groups=mesh['vel'=4,'sx'=4,'sy'=2] {'vel'}, dimensions={0}, use_global_device_ids=true | all-gather | bytes 20480 | tf_op jit(solution)/shard_map/all_gather | solution.py:436
  37.3 3.2 %local.3.partial = f32[64,64,128]{2,1,0:T(8,128)S(1)} custom-call(f32[64,64,128]{2,1,0:T(8,128)S(1)} %get-tuple-element.25.cells.refs_0_, f32[32,128]{1,0:T(8,128)S(1)} %all_gather.7.refs_1_, f32[64,64,128]{2,1,0:T(8,128)S(1)} %get-tuple-element.18.cells.refs_0_.refs_2_), custom_call_target="tpu_custom_call" | custom-call | tf_op jit(solution)/shard_map/local/pallas_call | solution.py:402
  40.5 0.0 collective-permute-done.6.from_x2
  40.5 0.4 collective-permute-done.8.from_x1
  40.9 0.0 collective-permute-done.9.from_y
  40.9 1.5 %finish.2.refs_0_ = f32[8,8,8192]{2,1,0:T(8,128)} custom-call(f32[64,64,128]{2,1,0:T(8,128)S(1)} %local.3.partial, f32[64,64,128]{2,1,0:T(8,128)S(1)} %get-tuple-element.25.cells.refs_0_, f32[40,2,8,128]{3,2,1,0:T(8,128)S(1)} %collective-permute-done.8.from_x1, f32[64,8,128]{2,1,0:T(8,128)S(1)} %collective-permute-done.6.from_x2, ...), custom_call_target="tpu_custom_call" | custom-call | tf_op jit(solution)/shard_map/finish/pallas_call | solution.py:402
  42.4 1.5 %collective-permute-done.5.from_x1 = f32[24,2,8,128]{3,2,1,0:T(8,128)S(1)} collective-permute-done((f32[24,2,8,128]{3,2,1,0:T(8,128)S(1)}, f32[24,2,8,128]{3,2,1,0:T(8,128)S(1)}, u32[]{:S(2)}, u32[]{:S(2)}) %collective-permute-start.5) | collective-permute-done | bytes 196640 | tf_op jit(solution)/shard_map/ppermute | solution.py:418
  43.9 0.0 collective-permute-done.7.from_y
  43.9 1.2 %finish.3 = f32[8,8,8192]{2,1,0:T(8,128)} custom-call(f32[64,64,128]{2,1,0:T(8,128)S(1)} %local.3.partial, f32[64,64,128]{2,1,0:T(8,128)S(1)} %get-tuple-element.25.cells.refs_0_, f32[24,2,8,128]{3,2,1,0:T(8,128)S(1)} %collective-permute-done.5.from_x1, f32[64,8,128]{2,1,0:T(8,128)S(1)} %collective-permute-done.6.from_x2, ...), custom_call_target="tpu_custom_call", output_to_operand_aliasing={{}: (5, {})} | custom-call | tf_op jit(solution)/shard_map/finish/pallas_call | solution.py:402
  (1 shorter events, 0.0 us)
Async XLA Ops:
  1.7 20.8 %collective-permute-start.2 = (f32[2,20,3,8,128]{4,3,2,1,0:T(8,128)S(1)}, f32[2,20,3,8,128]{4,3,2,1,0:T(8,128)S(1)}, u32[]{:S(2)}, u32[]{:S(2)}) collective-permute-start(f32[2,20,3,8,128]{4,3,2,1,0:T(8,128)S(1)} %get-tuple-element.21), channel_id=1, source_target_pairs={{0,1},{1,0},{2,3},{3,2},{4,5},{5,4},{6,7},{7,6},{8,9},{9,8},{10,11... | collective-permute-start | bytes 1474568 | tf_op jit(solution)/shard_map/ppermute | solution.py:423
  4.7 17.7 %collective-permute-start = (f32[40,2,8,128]{3,2,1,0:T(8,128)S(1)}, f32[40,2,8,128]{3,2,1,0:T(8,128)S(1)}, u32[]{:S(2)}, u32[]{:S(2)}) collective-permute-start(f32[40,2,8,128]{3,2,1,0:T(8,128)S(1)} %get-tuple-element.19), channel_id=1, source_target_pairs={{0,6},{2,0},{4,2},{6,4},{8,14},{10,8},{12,10},{14,12},{16,18},{18,... | collective-permute-start | bytes 983048 | tf_op jit(solution)/shard_map/ppermute | solution.py:418
  8.3 14.1 %collective-permute-start.1 = (f32[64,8,128]{2,1,0:T(8,128)S(1)}, f32[64,8,128]{2,1,0:T(8,128)S(1)}, u32[]{:S(2)}, u32[]{:S(2)}) collective-permute-start(f32[64,8,128]{2,1,0:T(8,128)S(1)} %get-tuple-element.20), channel_id=1, source_target_pairs={{0,2},{2,4},{4,6},{6,0},{8,10},{10,12},{12,14},{14,8},{16,22},{18,... | collective-permute-start | bytes 786440 | tf_op jit(solution)/shard_map/ppermute | solution.py:418
  8.3 17.5 %collective-permute-start.4 = (f32[2,12,3,8,128]{4,3,2,1,0:T(8,128)S(1)}, f32[2,12,3,8,128]{4,3,2,1,0:T(8,128)S(1)}, u32[]{:S(2)}, u32[]{:S(2)}) collective-permute-start(f32[2,12,3,8,128]{4,3,2,1,0:T(8,128)S(1)} %get-tuple-element.23), channel_id=1, source_target_pairs={{0,1},{1,0},{2,3},{3,2},{4,5},{5,4},{6,7},{7,6},{8,9},{9,8},{10,11... | collective-permute-start | bytes 884744 | tf_op jit(solution)/shard_map/ppermute | solution.py:423
  15.5 10.2 %collective-permute-start.3 = (f32[24,2,8,128]{3,2,1,0:T(8,128)S(1)}, f32[24,2,8,128]{3,2,1,0:T(8,128)S(1)}, u32[]{:S(2)}, u32[]{:S(2)}) collective-permute-start(f32[24,2,8,128]{3,2,1,0:T(8,128)S(1)} %late.1), channel_id=1, source_target_pairs={{0,6},{2,0},{4,2},{6,4},{8,14},{10,8},{12,10},{14,12},{16,18},{18,... | collective-permute-start | bytes 589832 | tf_op jit(solution)/shard_map/ppermute | solution.py:418
  23.1 17.8 %collective-permute-start.9 = (f32[2,20,3,8,128]{4,3,2,1,0:T(8,128)S(1)}, f32[2,20,3,8,128]{4,3,2,1,0:T(8,128)S(1)}, u32[]{:S(2)}, u32[]{:S(2)}) collective-permute-start(f32[2,20,3,8,128]{4,3,2,1,0:T(8,128)S(1)} %get-tuple-element.30), channel_id=1, source_target_pairs={{0,1},{1,0},{2,3},{3,2},{4,5},{5,4},{6,7},{7,6},{8,9},{9,8},{10,11... | collective-permute-start | bytes 1474568 | tf_op jit(solution)/shard_map/ppermute | solution.py:423
  24.7 16.2 %collective-permute-start.8 = (f32[40,2,8,128]{3,2,1,0:T(8,128)S(1)}, f32[40,2,8,128]{3,2,1,0:T(8,128)S(1)}, u32[]{:S(2)}, u32[]{:S(2)}) collective-permute-start(f32[40,2,8,128]{3,2,1,0:T(8,128)S(1)} %get-tuple-element.29), channel_id=1, source_target_pairs={{0,6},{2,0},{4,2},{6,4},{8,14},{10,8},{12,10},{14,12},{16,18},{18,... | collective-permute-start | bytes 983048 | tf_op jit(solution)/shard_map/ppermute | solution.py:418
  26.2 17.7 %collective-permute-start.7 = (f32[2,12,3,8,128]{4,3,2,1,0:T(8,128)S(1)}, f32[2,12,3,8,128]{4,3,2,1,0:T(8,128)S(1)}, u32[]{:S(2)}, u32[]{:S(2)}) collective-permute-start(f32[2,12,3,8,128]{4,3,2,1,0:T(8,128)S(1)} %get-tuple-element.28), channel_id=1, source_target_pairs={{0,1},{1,0},{2,3},{3,2},{4,5},{5,4},{6,7},{7,6},{8,9},{9,8},{10,11... | collective-permute-start | bytes 884744 | tf_op jit(solution)/shard_map/ppermute | solution.py:423
  26.8 13.7 %collective-permute-start.6 = (f32[64,8,128]{2,1,0:T(8,128)S(1)}, f32[64,8,128]{2,1,0:T(8,128)S(1)}, u32[]{:S(2)}, u32[]{:S(2)}) collective-permute-start(f32[64,8,128]{2,1,0:T(8,128)S(1)} %get-tuple-element.27), channel_id=1, source_target_pairs={{0,2},{2,4},{4,6},{6,0},{8,10},{10,12},{12,14},{14,8},{16,22},{18,... | collective-permute-start | bytes 786440 | tf_op jit(solution)/shard_map/ppermute | solution.py:418
  27.7 16.1 %collective-permute-start.5 = (f32[24,2,8,128]{3,2,1,0:T(8,128)S(1)}, f32[24,2,8,128]{3,2,1,0:T(8,128)S(1)}, u32[]{:S(2)}, u32[]{:S(2)}) collective-permute-start(f32[24,2,8,128]{3,2,1,0:T(8,128)S(1)} %get-tuple-element.26), channel_id=1, source_target_pairs={{0,6},{2,0},{4,2},{6,4},{8,14},{10,8},{12,10},{14,12},{16,18},{18,... | collective-permute-start | bytes 589832 | tf_op jit(solution)/shard_map/ppermute | solution.py:418

commit v6 on v5

--- a/solution.py
+++ b/solution.py
@@ -273,16 +273,23 @@
     lax.fori_loop(0, levels * HALF, one, 0)
 
 
-def edge_changes(cells, tile, i, sign, rows, speed, from_x, from_y):
-    a_speed, b_speed = speed
+def side_changes(cells, tile, i, sign, speed, from_y):
     mine, other = 1 - sign, sign
     ys = columns_in_order(sign)
     line = [cells[tile, column_of(ys[k]), :] for k in (0, 1, 6, 7)]
-    across = outer_changes(from_y[mine][i, 0], from_y[mine][i, 1], *line, from_y[other][i, 2])
+    changes = outer_changes(from_y[mine][i, 0], from_y[mine][i, 1], *line, from_y[other][i, 2])
+    return [speed * change for change in changes]
+
+
+def flow_changes(cells, tile, rows, speed, from_x):
     line = [cells[tile, rows[k], :] for k in (0, 1, 6, 7)]
     far, near, ahead = from_x(tile)
-    along = outer_changes(far, near, *line, ahead)
-    return [a_speed * c for c in along], [b_speed * c for c in across]
+    return [speed * change for change in outer_changes(far, near, *line, ahead)]
+
+
+def edge_changes(cells, tile, i, sign, rows, speed, from_x, from_y):
+    along = flow_changes(cells, tile, rows, speed[0], from_x)
+    return along, side_changes(cells, tile, i, sign, speed[1], from_y)
 
 
 EDGE = (0, 1, ROWS - 1)
@@ -376,6 +383,93 @@
     lax.fori_loop(start, stop, one, 0)
     for level in range(start, stop):
         copy(level).wait()
+
+
+def inner_kernel(vel_size, levels, start, stop, partial, cells, from_y, before, *refs):
+    result, edges, held, side, sems = refs
+    base = lax.axis_index("vel") * levels
+    flow = flow_of(vel_size)
+    xs = order_of(flow)
+    rows = [row_of(x) for x in xs]
+    first = jnp.where(flow, 2, 1)
+    width = TILES * LANES
+    from_y = halves(from_y)
+    for sub in range(TILES):
+        side[sub] = jnp.zeros((ROWS * ROWS, LANES), f32)
+
+    def copy(level):
+        lanes = pl.ds(pl.multiple_of(level * width, width), width)
+        target = result.at[pl.ds(first, ROWS - len(EDGE)), :, lanes]
+        return pltpu.make_async_copy(held.at[level - start], target, sems.at[level - start])
+
+    def one(level, carry):
+        for quarter in range(HALF):
+            pair = (level - start) * HALF + quarter
+            for sign in (0, 1):
+                sub = quarter + sign * HALF
+                tile = level * TILES + sub
+                ys = columns_in_order(sign)
+                speed = speeds(base, level, quarter, sign, 0.5)[1]
+                changes = side_changes(cells, tile, pair, sign, speed, from_y)
+                for k, change in zip(EDGE, changes):
+                    side[sub, column_of(ys[k]), :] = change
+                for k in range(ROWS):
+                    new = partial[tile, rows[k], :] - side[sub, rows[k], :]
+                    if k in EDGE:
+                        edges[tile - start * TILES, EDGE.index(k)] = new
+                    else:
+                        lanes = slice(sub * LANES, (sub + 1) * LANES)
+                        held[level - start, xs[k] - first, :, lanes] = new
+        copy(level).start()
+        return carry
+
+    lax.fori_loop(start, stop, one, 0)
+    for level in range(start, stop):
+        copy(level).wait()
+
+
+def edge_kernel(vel_size, levels, start, stop, edges, cells, from_x1, from_x2, before, *refs):
+    result, pair, single, sems = refs
+    base = lax.axis_index("vel") * levels
+    flow = flow_of(vel_size)
+    xs = order_of(flow)
+    rows = [row_of(x) for x in xs]
+    first = jnp.where(flow, 0, 6)
+    width = TILES * LANES
+
+    def from_x(tile):
+        here = tile - start * TILES
+        return from_x1[here, 0], from_x1[here, 1], from_x2[tile]
+
+    def copies(level):
+        lanes = pl.ds(pl.multiple_of(level * width, width), width)
+        here = level - start
+        double = result.at[pl.ds(first, 2), :, lanes]
+        last = result.at[pl.ds(xs[ROWS - 1], 1), :, lanes]
+        return (
+            pltpu.make_async_copy(pair.at[here], double, sems.at[here, 0]),
+            pltpu.make_async_copy(single.at[here], last, sems.at[here, 1]),
+        )
+
+    def one(level, carry):
+        here = level - start
+        speed = speeds(base, level, 0, 0, 0.5)[0]
+        for sub in range(TILES):
+            tile = level * TILES + sub
+            lanes = slice(sub * LANES, (sub + 1) * LANES)
+            changes = flow_changes(cells, tile, rows, speed, from_x)
+            new = [edges[tile - start * TILES, i] - change for i, change in enumerate(changes)]
+            pair[here, xs[0] - first, :, lanes] = new[0]
+            pair[here, xs[1] - first, :, lanes] = new[1]
+            single[here, 0, :, lanes] = new[2]
+        for copy in copies(level):
+            copy.start()
+        return carry
+
+    lax.fori_loop(start, stop, one, 0)
+    for level in range(start, stop):
+        for copy in copies(level):
+            copy.wait()
 
 
 def local(sizes, table):
@@ -482,22 +576,39 @@
         local_kernel, "local", whole, cells_shape, sectioned, sums, cells,
         scratch=table_scratch, static=(vel_size, levels, True),
     )
-    result = ()
-    for c, (begin, end) in enumerate(bounds):
-        result = (
-            call(
-                finish_kernel, "finish", outside, shape(*table.shape),
-                partial, sectioned, *arrived[c], *result,
-                scratch=[
-                    held(end - begin),
-                    pltpu.VMEM((TILES, ROWS * ROWS, LANES), f32),
-                    copies(end - begin),
-                ],
-                static=(vel_size, levels, begin, end),
-                aliases={5: 0} if result else {},
-            ),
+    begin, end = bounds[0]
+    result = call(
+        finish_kernel, "finish", outside, shape(*table.shape), partial, sectioned, *arrived[0],
+        scratch=[held(end), pltpu.VMEM((TILES, ROWS * ROWS, LANES), f32), copies(end)],
+        static=(vel_size, levels, begin, end),
+    )
+    for c in range(1, chunks):
+        begin, end = bounds[c]
+        width = TILES * LANES
+        result, edges = call(
+            inner_kernel, "inner", [outside, whole],
+            (shape(*table.shape), shape((end - begin) * TILES, len(EDGE), ROWS, LANES)),
+            partial, sectioned, arrived[c][2], result,
+            scratch=[
+                pltpu.VMEM((end - begin, ROWS - len(EDGE), ROWS, width), f32),
+                pltpu.VMEM((TILES, ROWS * ROWS, LANES), f32),
+                copies(end - begin),
+            ],
+            static=(vel_size, levels, begin, end),
+            aliases={3: 0},
         )
-    return result[0]
+        result = call(
+            edge_kernel, "edge", outside, shape(*table.shape),
+            edges, sectioned, *arrived[c][:2], result,
+            scratch=[
+                pltpu.VMEM((end - begin, 2, ROWS, width), f32),
+                pltpu.VMEM((end - begin, 1, ROWS, width), f32),
+                pltpu.SemaphoreType.DMA((end - begin, 2)),
+            ],
+            static=(vel_size, levels, begin, end),
+            aliases={4: 0},
+        )
+    return result
 
 
 def solution(mesh):

time: 45.2 us -> 44.8 us (level)
  waiting for transfers between devices: 2.94 us -> 1.84 us
  Pallas kernels: 14.7 us -> 15.4 us
    ppermute x6, waiting for transfers between devices: 2.93 us -> 1.59 us  [along_x(): return lax.ppermute(array, ('vel', 'sx'), pairs)]
    pallas_call x10 -> x11, Pallas kernels: 14.7 us -> 15.4 us  [call(): pl.pallas_call(functools.partial(kernel, *static), out_shape=outs, in_spe...]
  transfers between devices with their start and end apart: 10 -> 10, of which waited for: 3 -> 4; matrix products, arithmetic and copies ran while one was open for 0% -> 0% of each run, Pallas kernels for 26% -> 29%
where the time goes in v6:
time: 44.8 us; the launch traced here: 44.7 us
  starting transfers between devices  17 us (38%)
  Pallas kernels  15.4 us (34%)
  blocking collectives  10.3 us (23%)
  waiting for transfers between devices  1.84 us (4%)
    pallas_call x11, Pallas kernels, call(): pl.pallas_call(functools.partial(kernel, *static), out_shape=outs, in_spe...  15.4 us
    ppermute x6, starting transfers between devices, along_x(): return lax.ppermute(array, ('vel', 'sx'), pairs)  11.3 us
    all_gather x2, blocking collectives, first_sums(): return lax.all_gather(sums, 'vel', axis=0, tiled=True)  10.3 us
    ppermute x4, starting transfers between devices, along_y(): return lax.ppermute(array, 'sy', ways[0])  5.7 us
    ppermute x6, waiting for transfers between devices, along_x(): return lax.ppermute(array, ('vel', 'sx'), pairs)  1.59 us
  transfers between devices with their start and end apart: 10, of which 4 were waited for; matrix products, arithmetic and copies ran while one was open for 0% of the time, Pallas kernels for 29%

profile of v6, /device:TPU:0, one launch (start us, length us, event | category | flops | bytes accessed | tf_op | source)
XLA Modules:
  0.0 44.7 jit_solution(5197527414269335092)
XLA Ops:
  0.0 1.6 %pack.1 = (f32[64,64,128]{2,1,0:T(8,128)S(1)}, f32[2,20,3,8,128]{4,3,2,1,0:T(8,128)S(1)}, f32[2,12,3,8,128]{4,3,2,1,0:T(8,128)S(1)}, f32[40,2,8,128]{3,2,1,0:T(8,128)S(1)}, f32[64,8,128]{2,1,0:T(8,128)S(1)}) custom-call(f32[8,8,8192]{2,1,0:T(8,128)} %table.1), custom_call_target="tpu_custom_call" | custom-call | tf_op jit(solution)/shard_map/pack/pallas_call | solution.py:496
  1.7 3.0 %collective-permute-start.2 = (f32[2,20,3,8,128]{4,3,2,1,0:T(8,128)S(1)}, f32[2,20,3,8,128]{4,3,2,1,0:T(8,128)S(1)}, u32[]{:S(2)}, u32[]{:S(2)}) collective-permute-start(f32[2,20,3,8,128]{4,3,2,1,0:T(8,128)S(1)} %get-tuple-element.23), channel_id=1, source_target_pairs={{0,1},{1,0},{2,3},{3,2},{4,5},{5,4},{6,7},{7,6},{8,9},{9,8},{10,11... | collective-permute-start | bytes 1474568 | tf_op jit(solution)/shard_map/ppermute | solution.py:517
  4.7 3.6 %collective-permute-start = (f32[40,2,8,128]{3,2,1,0:T(8,128)S(1)}, f32[40,2,8,128]{3,2,1,0:T(8,128)S(1)}, u32[]{:S(2)}, u32[]{:S(2)}) collective-permute-start(f32[40,2,8,128]{3,2,1,0:T(8,128)S(1)} %get-tuple-element.21), channel_id=1, source_target_pairs={{0,6},{2,0},{4,2},{6,4},{8,14},{10,8},{12,10},{14,12},{16,18},{18,... | collective-permute-start | bytes 983048 | tf_op jit(solution)/shard_map/ppermute | solution.py:512
  8.3 0.0 collective-permute-start.1
  8.3 0.5 %collective-permute-start.4 = (f32[2,12,3,8,128]{4,3,2,1,0:T(8,128)S(1)}, f32[2,12,3,8,128]{4,3,2,1,0:T(8,128)S(1)}, u32[]{:S(2)}, u32[]{:S(2)}) collective-permute-start(f32[2,12,3,8,128]{4,3,2,1,0:T(8,128)S(1)} %get-tuple-element.25), channel_id=1, source_target_pairs={{0,1},{1,0},{2,3},{3,2},{4,5},{5,4},{6,7},{7,6},{8,9},{9,8},{10,11... | collective-permute-start | bytes 884744 | tf_op jit(solution)/shard_map/ppermute | solution.py:517
  8.8 1.5 %sums.2 = f32[8,128]{1,0:T(8,128)S(1)} custom-call(f32[64,64,128]{2,1,0:T(8,128)S(1)} %get-tuple-element.20.cells.refs_0_.refs_2_), custom_call_target="tpu_custom_call" | custom-call | tf_op jit(solution)/shard_map/sums/pallas_call | solution.py:496
  10.3 5.2 %all_gather.6.refs_1_.after = f32[32,128]{1,0:T(8,128)S(1)} all-gather(f32[8,128]{1,0:T(8,128)S(1)} %sums.2), channel_id=1, replica_groups=mesh['vel'=4,'sx'=4,'sy'=2] {'vel'}, dimensions={0}, use_global_device_ids=true | all-gather | bytes 20480 | tf_op jit(solution)/shard_map/all_gather | solution.py:530
  15.5 3.9 %collective-permute-start.3 = (f32[24,2,8,128]{3,2,1,0:T(8,128)S(1)}, f32[24,2,8,128]{3,2,1,0:T(8,128)S(1)}, u32[]{:S(2)}, u32[]{:S(2)}) collective-permute-start(f32[24,2,8,128]{3,2,1,0:T(8,128)S(1)} %late.1), channel_id=1, source_target_pairs={{0,6},{2,0},{4,2},{6,4},{8,14},{10,8},{12,10},{14,12},{16,18},{18,... | collective-permute-start | bytes 589832 | tf_op jit(solution)/shard_map/ppermute | solution.py:512
  19.4 3.0 %local.2.partial = f32[64,64,128]{2,1,0:T(8,128)S(1)} custom-call(f32[64,64,128]{2,1,0:T(8,128)S(1)} %get-tuple-element.20.cells.refs_0_.refs_2_, f32[32,128]{1,0:T(8,128)S(1)} %all_gather.6.refs_1_.after), custom_call_target="tpu_custom_call" | custom-call | tf_op jit(solution)/shard_map/local/pallas_call | solution.py:496
  22.4 0.0 collective-permute-done.1.from_x2
  22.4 0.0 collective-permute-done.from_x1
  22.4 0.0 collective-permute-done.2.from_y
  22.4 0.7 %correct.2 = (f32[64,64,128]{2,1,0:T(8,128)S(1)}, f32[40,2,8,128]{3,2,1,0:T(8,128)S(1)}, f32[64,8,128]{2,1,0:T(8,128)S(1)}, f32[2,20,3,8,128]{4,3,2,1,0:T(8,128)S(1)}) custom-call(f32[64,64,128]{2,1,0:T(8,128)S(1)} %local.2.partial, f32[64,64,128]{2,1,0:T(8,128)S(1)} %get-tuple-element.20.cells.refs_0_.refs_2_, ...), custom_call_target="tpu_custom_call", output_to_operand_aliasing={{0}: (0, {})} | custom-call | tf_op jit(solution)/shard_map/correct/pallas_call | solution.py:496
  23.1 1.6 %collective-permute-start.8 = (f32[2,20,3,8,128]{4,3,2,1,0:T(8,128)S(1)}, f32[2,20,3,8,128]{4,3,2,1,0:T(8,128)S(1)}, u32[]{:S(2)}, u32[]{:S(2)}) collective-permute-start(f32[2,20,3,8,128]{4,3,2,1,0:T(8,128)S(1)} %get-tuple-element.31), channel_id=1, source_target_pairs={{0,1},{1,0},{2,3},{3,2},{4,5},{5,4},{6,7},{7,6},{8,9},{9,8},{10,11... | collective-permute-start | bytes 1474568 | tf_op jit(solution)/shard_map/ppermute | solution.py:517
  24.7 0.0 collective-permute-start.6
  24.7 1.0 %collective-permute-done.3.from_x1 = f32[24,2,8,128]{3,2,1,0:T(8,128)S(1)} collective-permute-done((f32[24,2,8,128]{3,2,1,0:T(8,128)S(1)}, f32[24,2,8,128]{3,2,1,0:T(8,128)S(1)}, u32[]{:S(2)}, u32[]{:S(2)}) %collective-permute-start.3) | collective-permute-done | bytes 196640 | tf_op jit(solution)/shard_map/ppermute | solution.py:512
  25.7 0.0 collective-permute-done.4.from_y
  25.7 0.4 correct.3
  26.2 0.6 %collective-permute-start.5 = (f32[2,12,3,8,128]{4,3,2,1,0:T(8,128)S(1)}, f32[2,12,3,8,128]{4,3,2,1,0:T(8,128)S(1)}, u32[]{:S(2)}, u32[]{:S(2)}) collective-permute-start(f32[2,12,3,8,128]{4,3,2,1,0:T(8,128)S(1)} %get-tuple-element.28), channel_id=1, source_target_pairs={{0,1},{1,0},{2,3},{3,2},{4,5},{5,4},{6,7},{7,6},{8,9},{9,8},{10,11... | collective-permute-start | bytes 884744 | tf_op jit(solution)/shard_map/ppermute | solution.py:517
  26.8 1.0 %collective-permute-start.7 = (f32[64,8,128]{2,1,0:T(8,128)S(1)}, f32[64,8,128]{2,1,0:T(8,128)S(1)}, u32[]{:S(2)}, u32[]{:S(2)}) collective-permute-start(f32[64,8,128]{2,1,0:T(8,128)S(1)} %get-tuple-element.30), channel_id=1, source_target_pairs={{0,2},{2,4},{4,6},{6,0},{8,10},{10,12},{12,14},{14,8},{16,22},{18,... | collective-permute-start | bytes 786440 | tf_op jit(solution)/shard_map/ppermute | solution.py:512
  27.7 2.8 %collective-permute-start.9 = (f32[24,2,8,128]{3,2,1,0:T(8,128)S(1)}, f32[24,2,8,128]{3,2,1,0:T(8,128)S(1)}, u32[]{:S(2)}, u32[]{:S(2)}) collective-permute-start(f32[24,2,8,128]{3,2,1,0:T(8,128)S(1)} %get-tuple-element.33), channel_id=1, source_target_pairs={{0,6},{2,0},{4,2},{6,4},{8,14},{10,8},{12,10},{14,12},{16,18},{18,... | collective-permute-start | bytes 589832 | tf_op jit(solution)/shard_map/ppermute | solution.py:512
  30.6 1.5 %sums.3 = f32[8,128]{1,0:T(8,128)S(1)} custom-call(f32[64,64,128]{2,1,0:T(8,128)S(1)} %get-tuple-element.27.cells.refs_0_), custom_call_target="tpu_custom_call" | custom-call | tf_op jit(solution)/shard_map/sums/pallas_call | solution.py:496
  32.1 5.2 %all_gather.7.refs_1_ = f32[32,128]{1,0:T(8,128)S(1)} all-gather(f32[8,128]{1,0:T(8,128)S(1)} %sums.3), channel_id=1, replica_groups=mesh['vel'=4,'sx'=4,'sy'=2] {'vel'}, dimensions={0}, use_global_device_ids=true | all-gather | bytes 20480 | tf_op jit(solution)/shard_map/all_gather | solution.py:530
  37.3 3.2 %local.3.partial = f32[64,64,128]{2,1,0:T(8,128)S(1)} custom-call(f32[64,64,128]{2,1,0:T(8,128)S(1)} %get-tuple-element.27.cells.refs_0_, f32[32,128]{1,0:T(8,128)S(1)} %all_gather.7.refs_1_, f32[64,64,128]{2,1,0:T(8,128)S(1)} %get-tuple-element.20.cells.refs_0_.refs_2_), custom_call_target="tpu_custom_call" | custom-call | tf_op jit(solution)/shard_map/local/pallas_call | solution.py:496
  40.5 0.0 collective-permute-done.7.from_x2
  40.5 0.4 collective-permute-done.6.from_x1
  40.9 0.0 collective-permute-done.8.from_y
  40.9 1.5 %finish.1.before = f32[8,8,8192]{2,1,0:T(8,128)} custom-call(f32[64,64,128]{2,1,0:T(8,128)S(1)} %local.3.partial, f32[64,64,128]{2,1,0:T(8,128)S(1)} %get-tuple-element.27.cells.refs_0_, f32[40,2,8,128]{3,2,1,0:T(8,128)S(1)} %collective-permute-done.6.from_x1, f32[64,8,128]{2,1,0:T(8,128)S(1)} %collective-permute-done.7.from_x2, ...), custom_call_target="tpu_custom_call" | custom-call | tf_op jit(solution)/shard_map/finish/pallas_call | solution.py:496
  42.4 0.2 collective-permute-done.5.from_y
  42.7 1.1 %inner.1 = (f32[8,8,8192]{2,1,0:T(8,128)}, f32[24,3,8,128]{3,2,1,0:T(8,128)S(1)}) custom-call(f32[64,64,128]{2,1,0:T(8,128)S(1)} %local.3.partial, f32[64,64,128]{2,1,0:T(8,128)S(1)} %get-tuple-element.27.cells.refs_0_, f32[2,12,3,8,128]{4,3,2,1,0:T(8,128)S(1)} %collective-permute-done.5.from_y, ...), custom_call_target="tpu_custom_call", output_to_operand_aliasing={{0}: (3, {})} | custom-call | tf_op jit(solution)/shard_map/inner/pallas_call | solution.py:496
  43.7 0.1 collective-permute-done.9.from_x1
  43.9 0.8 %edge.1 = f32[8,8,8192]{2,1,0:T(8,128)} custom-call(f32[24,3,8,128]{3,2,1,0:T(8,128)S(1)} %get-tuple-element.32.edges, f32[64,64,128]{2,1,0:T(8,128)S(1)} %get-tuple-element.27.cells.refs_0_, f32[24,2,8,128]{3,2,1,0:T(8,128)S(1)} %collective-permute-done.9.from_x1, f32[64,8,128]{2,1,0:T(8,128)S(1)} %collective-permute-done.7.from_x2, ...), custom_call_target="tpu_custom_call", output_to_operand_aliasing={{}: (4, {})} | custom-call | tf_op jit(solution)/shard_map/edge/pallas_call | solution.py:496
  (1 shorter events, 0.0 us)
Async XLA Ops:
  1.7 20.8 %collective-permute-start.2 = (f32[2,20,3,8,128]{4,3,2,1,0:T(8,128)S(1)}, f32[2,20,3,8,128]{4,3,2,1,0:T(8,128)S(1)}, u32[]{:S(2)}, u32[]{:S(2)}) collective-permute-start(f32[2,20,3,8,128]{4,3,2,1,0:T(8,128)S(1)} %get-tuple-element.23), channel_id=1, source_target_pairs={{0,1},{1,0},{2,3},{3,2},{4,5},{5,4},{6,7},{7,6},{8,9},{9,8},{10,11... | collective-permute-start | bytes 1474568 | tf_op jit(solution)/shard_map/ppermute | solution.py:517
  4.7 17.7 %collective-permute-start = (f32[40,2,8,128]{3,2,1,0:T(8,128)S(1)}, f32[40,2,8,128]{3,2,1,0:T(8,128)S(1)}, u32[]{:S(2)}, u32[]{:S(2)}) collective-permute-start(f32[40,2,8,128]{3,2,1,0:T(8,128)S(1)} %get-tuple-element.21), channel_id=1, source_target_pairs={{0,6},{2,0},{4,2},{6,4},{8,14},{10,8},{12,10},{14,12},{16,18},{18,... | collective-permute-start | bytes 983048 | tf_op jit(solution)/shard_map/ppermute | solution.py:512
  8.3 14.1 %collective-permute-start.1 = (f32[64,8,128]{2,1,0:T(8,128)S(1)}, f32[64,8,128]{2,1,0:T(8,128)S(1)}, u32[]{:S(2)}, u32[]{:S(2)}) collective-permute-start(f32[64,8,128]{2,1,0:T(8,128)S(1)} %get-tuple-element.22), channel_id=1, source_target_pairs={{0,2},{2,4},{4,6},{6,0},{8,10},{10,12},{12,14},{14,8},{16,22},{18,... | collective-permute-start | bytes 786440 | tf_op jit(solution)/shard_map/ppermute | solution.py:512
  8.3 17.5 %collective-permute-start.4 = (f32[2,12,3,8,128]{4,3,2,1,0:T(8,128)S(1)}, f32[2,12,3,8,128]{4,3,2,1,0:T(8,128)S(1)}, u32[]{:S(2)}, u32[]{:S(2)}) collective-permute-start(f32[2,12,3,8,128]{4,3,2,1,0:T(8,128)S(1)} %get-tuple-element.25), channel_id=1, source_target_pairs={{0,1},{1,0},{2,3},{3,2},{4,5},{5,4},{6,7},{7,6},{8,9},{9,8},{10,11... | collective-permute-start | bytes 884744 | tf_op jit(solution)/shard_map/ppermute | solution.py:517
  15.5 10.2 %collective-permute-start.3 = (f32[24,2,8,128]{3,2,1,0:T(8,128)S(1)}, f32[24,2,8,128]{3,2,1,0:T(8,128)S(1)}, u32[]{:S(2)}, u32[]{:S(2)}) collective-permute-start(f32[24,2,8,128]{3,2,1,0:T(8,128)S(1)} %late.1), channel_id=1, source_target_pairs={{0,6},{2,0},{4,2},{6,4},{8,14},{10,8},{12,10},{14,12},{16,18},{18,... | collective-permute-start | bytes 589832 | tf_op jit(solution)/shard_map/ppermute | solution.py:512
  23.1 17.8 %collective-permute-start.8 = (f32[2,20,3,8,128]{4,3,2,1,0:T(8,128)S(1)}, f32[2,20,3,8,128]{4,3,2,1,0:T(8,128)S(1)}, u32[]{:S(2)}, u32[]{:S(2)}) collective-permute-start(f32[2,20,3,8,128]{4,3,2,1,0:T(8,128)S(1)} %get-tuple-element.31), channel_id=1, source_target_pairs={{0,1},{1,0},{2,3},{3,2},{4,5},{5,4},{6,7},{7,6},{8,9},{9,8},{10,11... | collective-permute-start | bytes 1474568 | tf_op jit(solution)/shard_map/ppermute | solution.py:517
  24.7 16.2 %collective-permute-start.6 = (f32[40,2,8,128]{3,2,1,0:T(8,128)S(1)}, f32[40,2,8,128]{3,2,1,0:T(8,128)S(1)}, u32[]{:S(2)}, u32[]{:S(2)}) collective-permute-start(f32[40,2,8,128]{3,2,1,0:T(8,128)S(1)} %get-tuple-element.29), channel_id=1, source_target_pairs={{0,6},{2,0},{4,2},{6,4},{8,14},{10,8},{12,10},{14,12},{16,18},{18,... | collective-permute-start | bytes 983048 | tf_op jit(solution)/shard_map/ppermute | solution.py:512
  26.2 16.5 %collective-permute-start.5 = (f32[2,12,3,8,128]{4,3,2,1,0:T(8,128)S(1)}, f32[2,12,3,8,128]{4,3,2,1,0:T(8,128)S(1)}, u32[]{:S(2)}, u32[]{:S(2)}) collective-permute-start(f32[2,12,3,8,128]{4,3,2,1,0:T(8,128)S(1)} %get-tuple-element.28), channel_id=1, source_target_pairs={{0,1},{1,0},{2,3},{3,2},{4,5},{5,4},{6,7},{7,6},{8,9},{9,8},{10,11... | collective-permute-start | bytes 884744 | tf_op jit(solution)/shard_map/ppermute | solution.py:517
  26.8 13.7 %collective-permute-start.7 = (f32[64,8,128]{2,1,0:T(8,128)S(1)}, f32[64,8,128]{2,1,0:T(8,128)S(1)}, u32[]{:S(2)}, u32[]{:S(2)}) collective-permute-start(f32[64,8,128]{2,1,0:T(8,128)S(1)} %get-tuple-element.30), channel_id=1, source_target_pairs={{0,2},{2,4},{4,6},{6,0},{8,10},{10,12},{12,14},{14,8},{16,22},{18,... | collective-permute-start | bytes 786440 | tf_op jit(solution)/shard_map/ppermute | solution.py:512
  27.7 16.1 %collective-permute-start.9 = (f32[24,2,8,128]{3,2,1,0:T(8,128)S(1)}, f32[24,2,8,128]{3,2,1,0:T(8,128)S(1)}, u32[]{:S(2)}, u32[]{:S(2)}) collective-permute-start(f32[24,2,8,128]{3,2,1,0:T(8,128)S(1)} %get-tuple-element.33), channel_id=1, source_target_pairs={{0,6},{2,0},{4,2},{6,4},{8,14},{10,8},{12,10},{14,12},{16,18},{18,... | collective-permute-start | bytes 589832 | tf_op jit(solution)/shard_map/ppermute | solution.py:512

commit v7 on v6

--- a/solution.py
+++ b/solution.py
@@ -145,10 +145,11 @@
     return across.at[0], across.at[1]
 
 
-def sums_kernel(levels, cells, sums):
+def sums_kernel(levels, start, stop, cells, *refs):
+    earlier, sums = refs[:-1], refs[-1]
     lane = lane_index()
     base = lax.axis_index("vel") * levels
-    speed = [component(base + level) for level in range(levels)]
+    speed = {level: component(base + level) for level in range(start, stop)}
 
     def one(x, total):
         acc = [jnp.zeros((ROWS, LANES), f32) for _ in range(13)]
@@ -156,12 +157,12 @@
         for tile in range(TILES):
             cb, ce = lane_components(tile)
             m0 = m1 = m2 = m3 = None
-            for level in range(levels):
+            for level in range(start, stop):
                 g = cells[level * TILES + tile, row, :]
                 g1 = g * speed[level]
                 g2 = g1 * speed[level]
                 g3 = g2 * speed[level]
-                if level == 0:
+                if level == start:
                     m0, m1, m2, m3 = g, g1, g2, g3
                 else:
                     m0, m1, m2, m3 = m0 + g, m1 + g1, m2 + g2, m3 + g3
@@ -177,7 +178,10 @@
             total = jnp.where(lane == x * SLOTS + m, jnp.sum(acc[m], axis=1, keepdims=True), total)
         return total
 
-    sums[...] = lax.fori_loop(0, ROWS, one, jnp.zeros((ROWS, LANES), f32))
+    total = lax.fori_loop(0, ROWS, one, jnp.zeros((ROWS, LANES), f32))
+    for part in earlier:
+        total = total + part[...]
+    sums[...] = total
 
 
 def tables(parts, levels, base, scale, tab_b, tab_a, keep):
@@ -521,8 +525,9 @@
         behind = along_x(secondary, -1)
         return [(along_x(p, 1), behind, along_y(a)) for p, a in zip(primary, across)]
 
-    def sums_of(cells):
-        return call(sums_kernel, "sums", whole, shape(ROWS, LANES), cells, static=(levels,))
+    def sums_of(cells, begin=0, end=levels, *earlier):
+        static = (levels, begin, end)
+        return call(sums_kernel, "sums", whole, shape(ROWS, LANES), cells, *earlier, static=static)
 
     def first_sums(sums):
         if vel_size > 4:
@@ -558,20 +563,21 @@
         local_kernel, "local", whole, cells_shape, cells, sums,
         scratch=table_scratch, static=(vel_size, levels, False),
     )
-    primary, across, partly = [], [], ()
+    primary, across, partly, earlier = [], [], (), ()
     for c, (begin, end) in enumerate(bounds):
         sectioned, first, secondary, last = call(
             correct_kernel, "correct", [whole] * 4,
             [cells_shape, primary_shape[c], secondary_shape, across_shape[c]],
-            sectioned, cells, *arrived[c], *partly,
+            sectioned, cells, *arrived[c], *partly, *earlier,
             static=(vel_size, levels, begin, end),
             aliases={0: 0, 5: 2} if partly else {0: 0},
         )
         partly = (secondary,)
+        earlier = (sums_of(sectioned, begin, end, *earlier),)
         primary.append(first)
         across.append(last)
     arrived = exchange(primary, secondary, across)
-    sums = first_sums(sums_of(sectioned))
+    sums = first_sums(*earlier)
     partial = call(
         local_kernel, "local", whole, cells_shape, sectioned, sums, cells,
         scratch=table_scratch, static=(vel_size, levels, True),

time: 44.8 us -> 44.8 us (level)
  waiting for transfers between devices: 1.84 us -> 0.08 us
  Pallas kernels: 15.4 us -> 16.3 us
  starting transfers between devices: 17 us -> 17.8 us
    ppermute x6, waiting for transfers between devices: 1.59 us -> 0.07 us  [along_x(): return lax.ppermute(array, ('vel', 'sx'), pairs)]
    pallas_call x11 -> x12, Pallas kernels: 15.4 us -> 16.3 us  [call(): pl.pallas_call(functools.partial(kernel, *static), out_shape=outs, in_spe...]
    ppermute x4, starting transfers between devices: 5.7 us -> 6.48 us  [along_y(): return lax.ppermute(array, 'sy', ways[0])]
  transfers between devices with their start and end apart: 10 -> 10, of which waited for: 4 -> 0; matrix products, arithmetic and copies ran while one was open for 0% -> 0% of each run, Pallas kernels for 29% -> 31%
where the time goes in v7:
time: 44.8 us; the launch traced here: 44.7 us
  starting transfers between devices  17.8 us (40%)
  Pallas kernels  16.3 us (36%)
  blocking collectives  10.4 us (23%)
    pallas_call x12, Pallas kernels, call(): pl.pallas_call(functools.partial(kernel, *static), out_shape=outs, in_spe...  16.3 us
    ppermute x6, starting transfers between devices, along_x(): return lax.ppermute(array, ('vel', 'sx'), pairs)  11.3 us
    all_gather x2, blocking collectives, first_sums(): return lax.all_gather(sums, 'vel', axis=0, tiled=True)  10.4 us
    ppermute x4, starting transfers between devices, along_y(): return lax.ppermute(array, 'sy', ways[0])  6.48 us
  transfers between devices with their start and end apart: 10, of which 0 were waited for; matrix products, arithmetic and copies ran while one was open for 0% of the time, Pallas kernels for 31%

profile of v7, /device:TPU:0, one launch (start us, length us, event | category | flops | bytes accessed | tf_op | source)
XLA Modules:
  0.0 44.7 jit_solution(11093806091103768220)
XLA Ops:
  0.0 1.6 %pack.1 = (f32[64,64,128]{2,1,0:T(8,128)S(1)}, f32[2,20,3,8,128]{4,3,2,1,0:T(8,128)S(1)}, f32[2,12,3,8,128]{4,3,2,1,0:T(8,128)S(1)}, f32[40,2,8,128]{3,2,1,0:T(8,128)S(1)}, f32[64,8,128]{2,1,0:T(8,128)S(1)}) custom-call(f32[8,8,8192]{2,1,0:T(8,128)} %table.1), custom_call_target="tpu_custom_call" | custom-call | tf_op jit(solution)/shard_map/pack/pallas_call | solution.py:500
  1.7 3.0 %collective-permute-start.2 = (f32[2,20,3,8,128]{4,3,2,1,0:T(8,128)S(1)}, f32[2,20,3,8,128]{4,3,2,1,0:T(8,128)S(1)}, u32[]{:S(2)}, u32[]{:S(2)}) collective-permute-start(f32[2,20,3,8,128]{4,3,2,1,0:T(8,128)S(1)} %get-tuple-element.23), channel_id=1, source_target_pairs={{0,1},{1,0},{2,3},{3,2},{4,5},{5,4},{6,7},{7,6},{8,9},{9,8},{10,11... | collective-permute-start | bytes 1474568 | tf_op jit(solution)/shard_map/ppermute | solution.py:521
  4.7 3.6 %collective-permute-start = (f32[40,2,8,128]{3,2,1,0:T(8,128)S(1)}, f32[40,2,8,128]{3,2,1,0:T(8,128)S(1)}, u32[]{:S(2)}, u32[]{:S(2)}) collective-permute-start(f32[40,2,8,128]{3,2,1,0:T(8,128)S(1)} %get-tuple-element.21), channel_id=1, source_target_pairs={{0,6},{2,0},{4,2},{6,4},{8,14},{10,8},{12,10},{14,12},{16,18},{18,... | collective-permute-start | bytes 983048 | tf_op jit(solution)/shard_map/ppermute | solution.py:516
  8.3 0.0 collective-permute-start.1
  8.3 0.5 %collective-permute-start.4 = (f32[2,12,3,8,128]{4,3,2,1,0:T(8,128)S(1)}, f32[2,12,3,8,128]{4,3,2,1,0:T(8,128)S(1)}, u32[]{:S(2)}, u32[]{:S(2)}) collective-permute-start(f32[2,12,3,8,128]{4,3,2,1,0:T(8,128)S(1)} %get-tuple-element.25), channel_id=1, source_target_pairs={{0,1},{1,0},{2,3},{3,2},{4,5},{5,4},{6,7},{7,6},{8,9},{9,8},{10,11... | collective-permute-start | bytes 884744 | tf_op jit(solution)/shard_map/ppermute | solution.py:521
  8.8 1.5 %sums.3 = f32[8,128]{1,0:T(8,128)S(1)} custom-call(f32[64,64,128]{2,1,0:T(8,128)S(1)} %get-tuple-element.20.cells.refs_0_.refs_2_), custom_call_target="tpu_custom_call" | custom-call | tf_op jit(solution)/shard_map/sums/pallas_call | solution.py:500
  10.3 5.2 %all_gather.6.refs_1_.after = f32[32,128]{1,0:T(8,128)S(1)} all-gather(f32[8,128]{1,0:T(8,128)S(1)} %sums.3), channel_id=1, replica_groups=mesh['vel'=4,'sx'=4,'sy'=2] {'vel'}, dimensions={0}, use_global_device_ids=true | all-gather | bytes 20480 | tf_op jit(solution)/shard_map/all_gather | solution.py:535
  15.5 3.9 %collective-permute-start.3 = (f32[24,2,8,128]{3,2,1,0:T(8,128)S(1)}, f32[24,2,8,128]{3,2,1,0:T(8,128)S(1)}, u32[]{:S(2)}, u32[]{:S(2)}) collective-permute-start(f32[24,2,8,128]{3,2,1,0:T(8,128)S(1)} %late.1), channel_id=1, source_target_pairs={{0,6},{2,0},{4,2},{6,4},{8,14},{10,8},{12,10},{14,12},{16,18},{18,... | collective-permute-start | bytes 589832 | tf_op jit(solution)/shard_map/ppermute | solution.py:516
  19.4 3.0 %local.2.partial = f32[64,64,128]{2,1,0:T(8,128)S(1)} custom-call(f32[64,64,128]{2,1,0:T(8,128)S(1)} %get-tuple-element.20.cells.refs_0_.refs_2_, f32[32,128]{1,0:T(8,128)S(1)} %all_gather.6.refs_1_.after), custom_call_target="tpu_custom_call" | custom-call | tf_op jit(solution)/shard_map/local/pallas_call | solution.py:500
  22.4 0.0 collective-permute-done.1.from_x2
  22.4 0.0 collective-permute-done.from_x1
  22.4 0.0 collective-permute-done.2.from_y
  22.4 0.7 %correct.2 = (f32[64,64,128]{2,1,0:T(8,128)S(1)}, f32[40,2,8,128]{3,2,1,0:T(8,128)S(1)}, f32[64,8,128]{2,1,0:T(8,128)S(1)}, f32[2,20,3,8,128]{4,3,2,1,0:T(8,128)S(1)}) custom-call(f32[64,64,128]{2,1,0:T(8,128)S(1)} %local.2.partial, f32[64,64,128]{2,1,0:T(8,128)S(1)} %get-tuple-element.20.cells.refs_0_.refs_2_, ...), custom_call_target="tpu_custom_call", output_to_operand_aliasing={{0}: (0, {})} | custom-call | tf_op jit(solution)/shard_map/correct/pallas_call | solution.py:500
  23.1 1.6 %collective-permute-start.8 = (f32[2,20,3,8,128]{4,3,2,1,0:T(8,128)S(1)}, f32[2,20,3,8,128]{4,3,2,1,0:T(8,128)S(1)}, u32[]{:S(2)}, u32[]{:S(2)}) collective-permute-start(f32[2,20,3,8,128]{4,3,2,1,0:T(8,128)S(1)} %get-tuple-element.31), channel_id=1, source_target_pairs={{0,1},{1,0},{2,3},{3,2},{4,5},{5,4},{6,7},{7,6},{8,9},{9,8},{10,11... | collective-permute-start | bytes 1474568 | tf_op jit(solution)/shard_map/ppermute | solution.py:521
  24.7 0.0 collective-permute-start.6
  24.7 1.3 %sums.4.refs_1_.refs_0_ = f32[8,128]{1,0:T(8,128)S(1)} custom-call(f32[64,64,128]{2,1,0:T(8,128)S(1)} %get-tuple-element.24.cells.partial), custom_call_target="tpu_custom_call" | custom-call | tf_op jit(solution)/shard_map/sums/pallas_call | solution.py:500
  26.0 0.0 collective-permute-done.3.from_x1
  26.0 0.0 collective-permute-done.4.from_y
  26.0 0.4 correct.3
  26.5 1.4 %collective-permute-start.5 = (f32[2,12,3,8,128]{4,3,2,1,0:T(8,128)S(1)}, f32[2,12,3,8,128]{4,3,2,1,0:T(8,128)S(1)}, u32[]{:S(2)}, u32[]{:S(2)}) collective-permute-start(f32[2,12,3,8,128]{4,3,2,1,0:T(8,128)S(1)} %get-tuple-element.28), channel_id=1, source_target_pairs={{0,1},{1,0},{2,3},{3,2},{4,5},{5,4},{6,7},{7,6},{8,9},{9,8},{10,11... | collective-permute-start | bytes 884744 | tf_op jit(solution)/shard_map/ppermute | solution.py:521
  27.8 1.2 %collective-permute-start.7 = (f32[64,8,128]{2,1,0:T(8,128)S(1)}, f32[64,8,128]{2,1,0:T(8,128)S(1)}, u32[]{:S(2)}, u32[]{:S(2)}) collective-permute-start(f32[64,8,128]{2,1,0:T(8,128)S(1)} %get-tuple-element.30), channel_id=1, source_target_pairs={{0,2},{2,4},{4,6},{6,0},{8,10},{10,12},{12,14},{14,8},{16,22},{18,... | collective-permute-start | bytes 786440 | tf_op jit(solution)/shard_map/ppermute | solution.py:516
  29.1 2.6 %collective-permute-start.9 = (f32[24,2,8,128]{3,2,1,0:T(8,128)S(1)}, f32[24,2,8,128]{3,2,1,0:T(8,128)S(1)}, u32[]{:S(2)}, u32[]{:S(2)}) collective-permute-start(f32[24,2,8,128]{3,2,1,0:T(8,128)S(1)} %get-tuple-element.33), channel_id=1, source_target_pairs={{0,6},{2,0},{4,2},{6,4},{8,14},{10,8},{12,10},{14,12},{16,18},{18,... | collective-permute-start | bytes 589832 | tf_op jit(solution)/shard_map/ppermute | solution.py:516
  31.7 1.1 %sums.5 = f32[8,128]{1,0:T(8,128)S(1)} custom-call(f32[64,64,128]{2,1,0:T(8,128)S(1)} %get-tuple-element.27.cells.refs_0_, f32[8,128]{1,0:T(8,128)S(1)} %sums.4.refs_1_.refs_0_), custom_call_target="tpu_custom_call" | custom-call | tf_op jit(solution)/shard_map/sums/pallas_call | solution.py:500
  32.8 5.2 %all_gather.7.refs_1_ = f32[32,128]{1,0:T(8,128)S(1)} all-gather(f32[8,128]{1,0:T(8,128)S(1)} %sums.5), channel_id=1, replica_groups=mesh['vel'=4,'sx'=4,'sy'=2] {'vel'}, dimensions={0}, use_global_device_ids=true | all-gather | bytes 20480 | tf_op jit(solution)/shard_map/all_gather | solution.py:535
  38.0 3.2 %local.3.partial = f32[64,64,128]{2,1,0:T(8,128)S(1)} custom-call(f32[64,64,128]{2,1,0:T(8,128)S(1)} %get-tuple-element.27.cells.refs_0_, f32[32,128]{1,0:T(8,128)S(1)} %all_gather.7.refs_1_, f32[64,64,128]{2,1,0:T(8,128)S(1)} %get-tuple-element.20.cells.refs_0_.refs_2_), custom_call_target="tpu_custom_call" | custom-call | tf_op jit(solution)/shard_map/local/pallas_call | solution.py:500
  41.2 0.0 collective-permute-done.7.from_x2
  41.2 0.0 collective-permute-done.6.from_x1
  41.2 0.0 collective-permute-done.8.from_y
  41.2 1.5 %finish.1.before = f32[8,8,8192]{2,1,0:T(8,128)} custom-call(f32[64,64,128]{2,1,0:T(8,128)S(1)} %local.3.partial, f32[64,64,128]{2,1,0:T(8,128)S(1)} %get-tuple-element.27.cells.refs_0_, f32[40,2,8,128]{3,2,1,0:T(8,128)S(1)} %collective-permute-done.6.from_x1, f32[64,8,128]{2,1,0:T(8,128)S(1)} %collective-permute-done.7.from_x2, ...), custom_call_target="tpu_custom_call" | custom-call | tf_op jit(solution)/shard_map/finish/pallas_call | solution.py:500
  42.7 1.1 %inner.1 = (f32[8,8,8192]{2,1,0:T(8,128)}, f32[24,3,8,128]{3,2,1,0:T(8,128)S(1)}) custom-call(f32[64,64,128]{2,1,0:T(8,128)S(1)} %local.3.partial, f32[64,64,128]{2,1,0:T(8,128)S(1)} %get-tuple-element.27.cells.refs_0_, f32[2,12,3,8,128]{4,3,2,1,0:T(8,128)S(1)} %collective-permute-done.5.from_y, ...), custom_call_target="tpu_custom_call", output_to_operand_aliasing={{0}: (3, {})} | custom-call | tf_op jit(solution)/shard_map/inner/pallas_call | solution.py:500
  43.8 0.0 collective-permute-done.9.from_x1
  43.9 0.8 %edge.1 = f32[8,8,8192]{2,1,0:T(8,128)} custom-call(f32[24,3,8,128]{3,2,1,0:T(8,128)S(1)} %get-tuple-element.32.edges, f32[64,64,128]{2,1,0:T(8,128)S(1)} %get-tuple-element.27.cells.refs_0_, f32[24,2,8,128]{3,2,1,0:T(8,128)S(1)} %collective-permute-done.9.from_x1, f32[64,8,128]{2,1,0:T(8,128)S(1)} %collective-permute-done.7.from_x2, ...), custom_call_target="tpu_custom_call", output_to_operand_aliasing={{}: (4, {})} | custom-call | tf_op jit(solution)/shard_map/edge/pallas_call | solution.py:500
  (2 shorter events, 0.0 us)
Async XLA Ops:
  1.7 20.7 %collective-permute-start.2 = (f32[2,20,3,8,128]{4,3,2,1,0:T(8,128)S(1)}, f32[2,20,3,8,128]{4,3,2,1,0:T(8,128)S(1)}, u32[]{:S(2)}, u32[]{:S(2)}) collective-permute-start(f32[2,20,3,8,128]{4,3,2,1,0:T(8,128)S(1)} %get-tuple-element.23), channel_id=1, source_target_pairs={{0,1},{1,0},{2,3},{3,2},{4,5},{5,4},{6,7},{7,6},{8,9},{9,8},{10,11... | collective-permute-start | bytes 1474568 | tf_op jit(solution)/shard_map/ppermute | solution.py:521
  4.7 17.7 %collective-permute-start = (f32[40,2,8,128]{3,2,1,0:T(8,128)S(1)}, f32[40,2,8,128]{3,2,1,0:T(8,128)S(1)}, u32[]{:S(2)}, u32[]{:S(2)}) collective-permute-start(f32[40,2,8,128]{3,2,1,0:T(8,128)S(1)} %get-tuple-element.21), channel_id=1, source_target_pairs={{0,6},{2,0},{4,2},{6,4},{8,14},{10,8},{12,10},{14,12},{16,18},{18,... | collective-permute-start | bytes 983048 | tf_op jit(solution)/shard_map/ppermute | solution.py:516
  8.3 14.1 %collective-permute-start.1 = (f32[64,8,128]{2,1,0:T(8,128)S(1)}, f32[64,8,128]{2,1,0:T(8,128)S(1)}, u32[]{:S(2)}, u32[]{:S(2)}) collective-permute-start(f32[64,8,128]{2,1,0:T(8,128)S(1)} %get-tuple-element.22), channel_id=1, source_target_pairs={{0,2},{2,4},{4,6},{6,0},{8,10},{10,12},{12,14},{14,8},{16,22},{18,... | collective-permute-start | bytes 786440 | tf_op jit(solution)/shard_map/ppermute | solution.py:516
  8.3 17.7 %collective-permute-start.4 = (f32[2,12,3,8,128]{4,3,2,1,0:T(8,128)S(1)}, f32[2,12,3,8,128]{4,3,2,1,0:T(8,128)S(1)}, u32[]{:S(2)}, u32[]{:S(2)}) collective-permute-start(f32[2,12,3,8,128]{4,3,2,1,0:T(8,128)S(1)} %get-tuple-element.25), channel_id=1, source_target_pairs={{0,1},{1,0},{2,3},{3,2},{4,5},{5,4},{6,7},{7,6},{8,9},{9,8},{10,11... | collective-permute-start | bytes 884744 | tf_op jit(solution)/shard_map/ppermute | solution.py:521
  15.5 10.5 %collective-permute-start.3 = (f32[24,2,8,128]{3,2,1,0:T(8,128)S(1)}, f32[24,2,8,128]{3,2,1,0:T(8,128)S(1)}, u32[]{:S(2)}, u32[]{:S(2)}) collective-permute-start(f32[24,2,8,128]{3,2,1,0:T(8,128)S(1)} %late.1), channel_id=1, source_target_pairs={{0,6},{2,0},{4,2},{6,4},{8,14},{10,8},{12,10},{14,12},{16,18},{18,... | collective-permute-start | bytes 589832 | tf_op jit(solution)/shard_map/ppermute | solution.py:516
  23.1 18.1 %collective-permute-start.8 = (f32[2,20,3,8,128]{4,3,2,1,0:T(8,128)S(1)}, f32[2,20,3,8,128]{4,3,2,1,0:T(8,128)S(1)}, u32[]{:S(2)}, u32[]{:S(2)}) collective-permute-start(f32[2,20,3,8,128]{4,3,2,1,0:T(8,128)S(1)} %get-tuple-element.31), channel_id=1, source_target_pairs={{0,1},{1,0},{2,3},{3,2},{4,5},{5,4},{6,7},{7,6},{8,9},{9,8},{10,11... | collective-permute-start | bytes 1474568 | tf_op jit(solution)/shard_map/ppermute | solution.py:521
  24.7 16.5 %collective-permute-start.6 = (f32[40,2,8,128]{3,2,1,0:T(8,128)S(1)}, f32[40,2,8,128]{3,2,1,0:T(8,128)S(1)}, u32[]{:S(2)}, u32[]{:S(2)}) collective-permute-start(f32[40,2,8,128]{3,2,1,0:T(8,128)S(1)} %get-tuple-element.29), channel_id=1, source_target_pairs={{0,6},{2,0},{4,2},{6,4},{8,14},{10,8},{12,10},{14,12},{16,18},{18,... | collective-permute-start | bytes 983048 | tf_op jit(solution)/shard_map/ppermute | solution.py:516
  26.5 16.3 %collective-permute-start.5 = (f32[2,12,3,8,128]{4,3,2,1,0:T(8,128)S(1)}, f32[2,12,3,8,128]{4,3,2,1,0:T(8,128)S(1)}, u32[]{:S(2)}, u32[]{:S(2)}) collective-permute-start(f32[2,12,3,8,128]{4,3,2,1,0:T(8,128)S(1)} %get-tuple-element.28), channel_id=1, source_target_pairs={{0,1},{1,0},{2,3},{3,2},{4,5},{5,4},{6,7},{7,6},{8,9},{9,8},{10,11... | collective-permute-start | bytes 884744 | tf_op jit(solution)/shard_map/ppermute | solution.py:521
  27.8 13.4 %collective-permute-start.7 = (f32[64,8,128]{2,1,0:T(8,128)S(1)}, f32[64,8,128]{2,1,0:T(8,128)S(1)}, u32[]{:S(2)}, u32[]{:S(2)}) collective-permute-start(f32[64,8,128]{2,1,0:T(8,128)S(1)} %get-tuple-element.30), channel_id=1, source_target_pairs={{0,2},{2,4},{4,6},{6,0},{8,10},{10,12},{12,14},{14,8},{16,22},{18,... | collective-permute-start | bytes 786440 | tf_op jit(solution)/shard_map/ppermute | solution.py:516
  29.1 14.8 %collective-permute-start.9 = (f32[24,2,8,128]{3,2,1,0:T(8,128)S(1)}, f32[24,2,8,128]{3,2,1,0:T(8,128)S(1)}, u32[]{:S(2)}, u32[]{:S(2)}) collective-permute-start(f32[24,2,8,128]{3,2,1,0:T(8,128)S(1)} %get-tuple-element.33), channel_id=1, source_target_pairs={{0,6},{2,0},{4,2},{6,4},{8,14},{10,8},{12,10},{14,12},{16,18},{18,... | collective-permute-start | bytes 589832 | tf_op jit(solution)/shard_map/ppermute | solution.py:516

commit v8 on v7

--- a/solution.py
+++ b/solution.py
@@ -97,7 +97,7 @@
     chunks = len(bounds)
     across, primary, secondary = refs[:chunks], refs[chunks], refs[chunks + 1]
     held, sems = refs[-2], refs[-1]
-    rows = [row_of(x) for x in order_of(flow_of(vel_size))]
+    xs = order_of(flow_of(vel_size))
     width = TILES * LANES
 
     def copy(level):
@@ -119,9 +119,9 @@
                             level, x, :, sub * LANES : (sub + 1) * LANES
                         ]
                     if c == 0:
-                        primary[tile, 0] = cells[tile, rows[6], :]
-                        primary[tile, 1] = cells[tile, rows[7], :]
-                    secondary[tile] = cells[tile, rows[0], :]
+                        primary[tile, 0] = held[level, xs[6], :, sub * LANES : (sub + 1) * LANES]
+                        primary[tile, 1] = held[level, xs[7], :, sub * LANES : (sub + 1) * LANES]
+                    secondary[tile] = held[level, xs[0], :, sub * LANES : (sub + 1) * LANES]
                 send_y(cells, (level - begin) * HALF + quarter, low, high, halves(across[c]))
             return carry
 

time: 44.8 us -> 44.8 us (level)
  no operation moved by 1% of the time
where the time goes in v8:
time: 44.8 us; the launch traced here: 44.7 us
  starting transfers between devices  17.8 us (40%)
  Pallas kernels  16.3 us (36%)
  blocking collectives  10.4 us (23%)
    pallas_call x12, Pallas kernels, call(): pl.pallas_call(functools.partial(kernel, *static), out_shape=outs, in_spe...  16.3 us
    ppermute x6, starting transfers between devices, along_x(): return lax.ppermute(array, ('vel', 'sx'), pairs)  11.3 us
    all_gather x2, blocking collectives, first_sums(): return lax.all_gather(sums, 'vel', axis=0, tiled=True)  10.4 us
    ppermute x4, starting transfers between devices, along_y(): return lax.ppermute(array, 'sy', ways[0])  6.48 us
  transfers between devices with their start and end apart: 10, of which 0 were waited for; matrix products, arithmetic and copies ran while one was open for 0% of the time, Pallas kernels for 31%

profile of v8, /device:TPU:0, one launch (start us, length us, event | category | flops | bytes accessed | tf_op | source)
XLA Modules:
  0.0 44.7 jit_solution(6846367786330437201)
XLA Ops:
  0.0 1.6 %pack.1 = (f32[64,64,128]{2,1,0:T(8,128)S(1)}, f32[2,20,3,8,128]{4,3,2,1,0:T(8,128)S(1)}, f32[2,12,3,8,128]{4,3,2,1,0:T(8,128)S(1)}, f32[40,2,8,128]{3,2,1,0:T(8,128)S(1)}, f32[64,8,128]{2,1,0:T(8,128)S(1)}) custom-call(f32[8,8,8192]{2,1,0:T(8,128)} %table.1), custom_call_target="tpu_custom_call" | custom-call | tf_op jit(solution)/shard_map/pack/pallas_call | solution.py:500
  1.6 3.0 %collective-permute-start.2 = (f32[2,20,3,8,128]{4,3,2,1,0:T(8,128)S(1)}, f32[2,20,3,8,128]{4,3,2,1,0:T(8,128)S(1)}, u32[]{:S(2)}, u32[]{:S(2)}) collective-permute-start(f32[2,20,3,8,128]{4,3,2,1,0:T(8,128)S(1)} %get-tuple-element.23), channel_id=1, source_target_pairs={{0,1},{1,0},{2,3},{3,2},{4,5},{5,4},{6,7},{7,6},{8,9},{9,8},{10,11... | collective-permute-start | bytes 1474568 | tf_op jit(solution)/shard_map/ppermute | solution.py:521
  4.6 3.6 %collective-permute-start = (f32[40,2,8,128]{3,2,1,0:T(8,128)S(1)}, f32[40,2,8,128]{3,2,1,0:T(8,128)S(1)}, u32[]{:S(2)}, u32[]{:S(2)}) collective-permute-start(f32[40,2,8,128]{3,2,1,0:T(8,128)S(1)} %get-tuple-element.21), channel_id=1, source_target_pairs={{0,6},{2,0},{4,2},{6,4},{8,14},{10,8},{12,10},{14,12},{16,18},{18,... | collective-permute-start | bytes 983048 | tf_op jit(solution)/shard_map/ppermute | solution.py:516
  8.2 0.0 collective-permute-start.1
  8.2 0.5 %collective-permute-start.4 = (f32[2,12,3,8,128]{4,3,2,1,0:T(8,128)S(1)}, f32[2,12,3,8,128]{4,3,2,1,0:T(8,128)S(1)}, u32[]{:S(2)}, u32[]{:S(2)}) collective-permute-start(f32[2,12,3,8,128]{4,3,2,1,0:T(8,128)S(1)} %get-tuple-element.25), channel_id=1, source_target_pairs={{0,1},{1,0},{2,3},{3,2},{4,5},{5,4},{6,7},{7,6},{8,9},{9,8},{10,11... | collective-permute-start | bytes 884744 | tf_op jit(solution)/shard_map/ppermute | solution.py:521
  8.8 1.5 %sums.3 = f32[8,128]{1,0:T(8,128)S(1)} custom-call(f32[64,64,128]{2,1,0:T(8,128)S(1)} %get-tuple-element.20.cells.refs_0_.refs_2_), custom_call_target="tpu_custom_call" | custom-call | tf_op jit(solution)/shard_map/sums/pallas_call | solution.py:500
  10.3 5.2 %all_gather.6.refs_1_.after = f32[32,128]{1,0:T(8,128)S(1)} all-gather(f32[8,128]{1,0:T(8,128)S(1)} %sums.3), channel_id=1, replica_groups=mesh['vel'=4,'sx'=4,'sy'=2] {'vel'}, dimensions={0}, use_global_device_ids=true | all-gather | bytes 20480 | tf_op jit(solution)/shard_map/all_gather | solution.py:535
  15.5 3.9 %collective-permute-start.3 = (f32[24,2,8,128]{3,2,1,0:T(8,128)S(1)}, f32[24,2,8,128]{3,2,1,0:T(8,128)S(1)}, u32[]{:S(2)}, u32[]{:S(2)}) collective-permute-start(f32[24,2,8,128]{3,2,1,0:T(8,128)S(1)} %late.1), channel_id=1, source_target_pairs={{0,6},{2,0},{4,2},{6,4},{8,14},{10,8},{12,10},{14,12},{16,18},{18,... | collective-permute-start | bytes 589832 | tf_op jit(solution)/shard_map/ppermute | solution.py:516
  19.4 3.0 %local.2.partial = f32[64,64,128]{2,1,0:T(8,128)S(1)} custom-call(f32[64,64,128]{2,1,0:T(8,128)S(1)} %get-tuple-element.20.cells.refs_0_.refs_2_, f32[32,128]{1,0:T(8,128)S(1)} %all_gather.6.refs_1_.after), custom_call_target="tpu_custom_call" | custom-call | tf_op jit(solution)/shard_map/local/pallas_call | solution.py:500
  22.3 0.0 collective-permute-done.1.from_x2
  22.4 0.0 collective-permute-done.from_x1
  22.4 0.0 collective-permute-done.2.from_y
  22.4 0.7 %correct.2 = (f32[64,64,128]{2,1,0:T(8,128)S(1)}, f32[40,2,8,128]{3,2,1,0:T(8,128)S(1)}, f32[64,8,128]{2,1,0:T(8,128)S(1)}, f32[2,20,3,8,128]{4,3,2,1,0:T(8,128)S(1)}) custom-call(f32[64,64,128]{2,1,0:T(8,128)S(1)} %local.2.partial, f32[64,64,128]{2,1,0:T(8,128)S(1)} %get-tuple-element.20.cells.refs_0_.refs_2_, ...), custom_call_target="tpu_custom_call", output_to_operand_aliasing={{0}: (0, {})} | custom-call | tf_op jit(solution)/shard_map/correct/pallas_call | solution.py:500
  23.1 1.6 %collective-permute-start.8 = (f32[2,20,3,8,128]{4,3,2,1,0:T(8,128)S(1)}, f32[2,20,3,8,128]{4,3,2,1,0:T(8,128)S(1)}, u32[]{:S(2)}, u32[]{:S(2)}) collective-permute-start(f32[2,20,3,8,128]{4,3,2,1,0:T(8,128)S(1)} %get-tuple-element.31), channel_id=1, source_target_pairs={{0,1},{1,0},{2,3},{3,2},{4,5},{5,4},{6,7},{7,6},{8,9},{9,8},{10,11... | collective-permute-start | bytes 1474568 | tf_op jit(solution)/shard_map/ppermute | solution.py:521
  24.7 0.0 collective-permute-start.6
  24.7 1.3 %sums.4.refs_1_.refs_0_ = f32[8,128]{1,0:T(8,128)S(1)} custom-call(f32[64,64,128]{2,1,0:T(8,128)S(1)} %get-tuple-element.24.cells.partial), custom_call_target="tpu_custom_call" | custom-call | tf_op jit(solution)/shard_map/sums/pallas_call | solution.py:500
  26.0 0.0 collective-permute-done.3.from_x1
  26.0 0.0 collective-permute-done.4.from_y
  26.0 0.4 correct.3
  26.4 1.4 %collective-permute-start.5 = (f32[2,12,3,8,128]{4,3,2,1,0:T(8,128)S(1)}, f32[2,12,3,8,128]{4,3,2,1,0:T(8,128)S(1)}, u32[]{:S(2)}, u32[]{:S(2)}) collective-permute-start(f32[2,12,3,8,128]{4,3,2,1,0:T(8,128)S(1)} %get-tuple-element.28), channel_id=1, source_target_pairs={{0,1},{1,0},{2,3},{3,2},{4,5},{5,4},{6,7},{7,6},{8,9},{9,8},{10,11... | collective-permute-start | bytes 884744 | tf_op jit(solution)/shard_map/ppermute | solution.py:521
  27.8 1.2 %collective-permute-start.7 = (f32[64,8,128]{2,1,0:T(8,128)S(1)}, f32[64,8,128]{2,1,0:T(8,128)S(1)}, u32[]{:S(2)}, u32[]{:S(2)}) collective-permute-start(f32[64,8,128]{2,1,0:T(8,128)S(1)} %get-tuple-element.30), channel_id=1, source_target_pairs={{0,2},{2,4},{4,6},{6,0},{8,10},{10,12},{12,14},{14,8},{16,22},{18,... | collective-permute-start | bytes 786440 | tf_op jit(solution)/shard_map/ppermute | solution.py:516
  29.0 2.6 %collective-permute-start.9 = (f32[24,2,8,128]{3,2,1,0:T(8,128)S(1)}, f32[24,2,8,128]{3,2,1,0:T(8,128)S(1)}, u32[]{:S(2)}, u32[]{:S(2)}) collective-permute-start(f32[24,2,8,128]{3,2,1,0:T(8,128)S(1)} %get-tuple-element.33), channel_id=1, source_target_pairs={{0,6},{2,0},{4,2},{6,4},{8,14},{10,8},{12,10},{14,12},{16,18},{18,... | collective-permute-start | bytes 589832 | tf_op jit(solution)/shard_map/ppermute | solution.py:516
  31.6 1.1 %sums.5 = f32[8,128]{1,0:T(8,128)S(1)} custom-call(f32[64,64,128]{2,1,0:T(8,128)S(1)} %get-tuple-element.27.cells.refs_0_, f32[8,128]{1,0:T(8,128)S(1)} %sums.4.refs_1_.refs_0_), custom_call_target="tpu_custom_call" | custom-call | tf_op jit(solution)/shard_map/sums/pallas_call | solution.py:500
  32.8 5.2 %all_gather.7.refs_1_ = f32[32,128]{1,0:T(8,128)S(1)} all-gather(f32[8,128]{1,0:T(8,128)S(1)} %sums.5), channel_id=1, replica_groups=mesh['vel'=4,'sx'=4,'sy'=2] {'vel'}, dimensions={0}, use_global_device_ids=true | all-gather | bytes 20480 | tf_op jit(solution)/shard_map/all_gather | solution.py:535
  38.0 3.2 %local.3.partial = f32[64,64,128]{2,1,0:T(8,128)S(1)} custom-call(f32[64,64,128]{2,1,0:T(8,128)S(1)} %get-tuple-element.27.cells.refs_0_, f32[32,128]{1,0:T(8,128)S(1)} %all_gather.7.refs_1_, f32[64,64,128]{2,1,0:T(8,128)S(1)} %get-tuple-element.20.cells.refs_0_.refs_2_), custom_call_target="tpu_custom_call" | custom-call | tf_op jit(solution)/shard_map/local/pallas_call | solution.py:500
  41.2 0.0 collective-permute-done.7.from_x2
  41.2 0.0 collective-permute-done.6.from_x1
  41.2 0.0 collective-permute-done.8.from_y
  41.2 1.5 %finish.1.before = f32[8,8,8192]{2,1,0:T(8,128)} custom-call(f32[64,64,128]{2,1,0:T(8,128)S(1)} %local.3.partial, f32[64,64,128]{2,1,0:T(8,128)S(1)} %get-tuple-element.27.cells.refs_0_, f32[40,2,8,128]{3,2,1,0:T(8,128)S(1)} %collective-permute-done.6.from_x1, f32[64,8,128]{2,1,0:T(8,128)S(1)} %collective-permute-done.7.from_x2, ...), custom_call_target="tpu_custom_call" | custom-call | tf_op jit(solution)/shard_map/finish/pallas_call | solution.py:500
  42.7 1.1 %inner.1 = (f32[8,8,8192]{2,1,0:T(8,128)}, f32[24,3,8,128]{3,2,1,0:T(8,128)S(1)}) custom-call(f32[64,64,128]{2,1,0:T(8,128)S(1)} %local.3.partial, f32[64,64,128]{2,1,0:T(8,128)S(1)} %get-tuple-element.27.cells.refs_0_, f32[2,12,3,8,128]{4,3,2,1,0:T(8,128)S(1)} %collective-permute-done.5.from_y, ...), custom_call_target="tpu_custom_call", output_to_operand_aliasing={{0}: (3, {})} | custom-call | tf_op jit(solution)/shard_map/inner/pallas_call | solution.py:500
  43.8 0.0 collective-permute-done.9.from_x1
  43.9 0.8 %edge.1 = f32[8,8,8192]{2,1,0:T(8,128)} custom-call(f32[24,3,8,128]{3,2,1,0:T(8,128)S(1)} %get-tuple-element.32.edges, f32[64,64,128]{2,1,0:T(8,128)S(1)} %get-tuple-element.27.cells.refs_0_, f32[24,2,8,128]{3,2,1,0:T(8,128)S(1)} %collective-permute-done.9.from_x1, f32[64,8,128]{2,1,0:T(8,128)S(1)} %collective-permute-done.7.from_x2, ...), custom_call_target="tpu_custom_call", output_to_operand_aliasing={{}: (4, {})} | custom-call | tf_op jit(solution)/shard_map/edge/pallas_call | solution.py:500
  (2 shorter events, 0.0 us)
Async XLA Ops:
  1.6 20.7 %collective-permute-start.2 = (f32[2,20,3,8,128]{4,3,2,1,0:T(8,128)S(1)}, f32[2,20,3,8,128]{4,3,2,1,0:T(8,128)S(1)}, u32[]{:S(2)}, u32[]{:S(2)}) collective-permute-start(f32[2,20,3,8,128]{4,3,2,1,0:T(8,128)S(1)} %get-tuple-element.23), channel_id=1, source_target_pairs={{0,1},{1,0},{2,3},{3,2},{4,5},{5,4},{6,7},{7,6},{8,9},{9,8},{10,11... | collective-permute-start | bytes 1474568 | tf_op jit(solution)/shard_map/ppermute | solution.py:521
  4.6 17.7 %collective-permute-start = (f32[40,2,8,128]{3,2,1,0:T(8,128)S(1)}, f32[40,2,8,128]{3,2,1,0:T(8,128)S(1)}, u32[]{:S(2)}, u32[]{:S(2)}) collective-permute-start(f32[40,2,8,128]{3,2,1,0:T(8,128)S(1)} %get-tuple-element.21), channel_id=1, source_target_pairs={{0,6},{2,0},{4,2},{6,4},{8,14},{10,8},{12,10},{14,12},{16,18},{18,... | collective-permute-start | bytes 983048 | tf_op jit(solution)/shard_map/ppermute | solution.py:516
  8.2 14.1 %collective-permute-start.1 = (f32[64,8,128]{2,1,0:T(8,128)S(1)}, f32[64,8,128]{2,1,0:T(8,128)S(1)}, u32[]{:S(2)}, u32[]{:S(2)}) collective-permute-start(f32[64,8,128]{2,1,0:T(8,128)S(1)} %get-tuple-element.22), channel_id=1, source_target_pairs={{0,2},{2,4},{4,6},{6,0},{8,10},{10,12},{12,14},{14,8},{16,22},{18,... | collective-permute-start | bytes 786440 | tf_op jit(solution)/shard_map/ppermute | solution.py:516
  8.2 17.7 %collective-permute-start.4 = (f32[2,12,3,8,128]{4,3,2,1,0:T(8,128)S(1)}, f32[2,12,3,8,128]{4,3,2,1,0:T(8,128)S(1)}, u32[]{:S(2)}, u32[]{:S(2)}) collective-permute-start(f32[2,12,3,8,128]{4,3,2,1,0:T(8,128)S(1)} %get-tuple-element.25), channel_id=1, source_target_pairs={{0,1},{1,0},{2,3},{3,2},{4,5},{5,4},{6,7},{7,6},{8,9},{9,8},{10,11... | collective-permute-start | bytes 884744 | tf_op jit(solution)/shard_map/ppermute | solution.py:521
  15.5 10.5 %collective-permute-start.3 = (f32[24,2,8,128]{3,2,1,0:T(8,128)S(1)}, f32[24,2,8,128]{3,2,1,0:T(8,128)S(1)}, u32[]{:S(2)}, u32[]{:S(2)}) collective-permute-start(f32[24,2,8,128]{3,2,1,0:T(8,128)S(1)} %late.1), channel_id=1, source_target_pairs={{0,6},{2,0},{4,2},{6,4},{8,14},{10,8},{12,10},{14,12},{16,18},{18,... | collective-permute-start | bytes 589832 | tf_op jit(solution)/shard_map/ppermute | solution.py:516
  23.1 18.1 %collective-permute-start.8 = (f32[2,20,3,8,128]{4,3,2,1,0:T(8,128)S(1)}, f32[2,20,3,8,128]{4,3,2,1,0:T(8,128)S(1)}, u32[]{:S(2)}, u32[]{:S(2)}) collective-permute-start(f32[2,20,3,8,128]{4,3,2,1,0:T(8,128)S(1)} %get-tuple-element.31), channel_id=1, source_target_pairs={{0,1},{1,0},{2,3},{3,2},{4,5},{5,4},{6,7},{7,6},{8,9},{9,8},{10,11... | collective-permute-start | bytes 1474568 | tf_op jit(solution)/shard_map/ppermute | solution.py:521
  24.7 16.5 %collective-permute-start.6 = (f32[40,2,8,128]{3,2,1,0:T(8,128)S(1)}, f32[40,2,8,128]{3,2,1,0:T(8,128)S(1)}, u32[]{:S(2)}, u32[]{:S(2)}) collective-permute-start(f32[40,2,8,128]{3,2,1,0:T(8,128)S(1)} %get-tuple-element.29), channel_id=1, source_target_pairs={{0,6},{2,0},{4,2},{6,4},{8,14},{10,8},{12,10},{14,12},{16,18},{18,... | collective-permute-start | bytes 983048 | tf_op jit(solution)/shard_map/ppermute | solution.py:516
  26.4 16.3 %collective-permute-start.5 = (f32[2,12,3,8,128]{4,3,2,1,0:T(8,128)S(1)}, f32[2,12,3,8,128]{4,3,2,1,0:T(8,128)S(1)}, u32[]{:S(2)}, u32[]{:S(2)}) collective-permute-start(f32[2,12,3,8,128]{4,3,2,1,0:T(8,128)S(1)} %get-tuple-element.28), channel_id=1, source_target_pairs={{0,1},{1,0},{2,3},{3,2},{4,5},{5,4},{6,7},{7,6},{8,9},{9,8},{10,11... | collective-permute-start | bytes 884744 | tf_op jit(solution)/shard_map/ppermute | solution.py:521
  27.8 13.4 %collective-permute-start.7 = (f32[64,8,128]{2,1,0:T(8,128)S(1)}, f32[64,8,128]{2,1,0:T(8,128)S(1)}, u32[]{:S(2)}, u32[]{:S(2)}) collective-permute-start(f32[64,8,128]{2,1,0:T(8,128)S(1)} %get-tuple-element.30), channel_id=1, source_target_pairs={{0,2},{2,4},{4,6},{6,0},{8,10},{10,12},{12,14},{14,8},{16,22},{18,... | collective-permute-start | bytes 786440 | tf_op jit(solution)/shard_map/ppermute | solution.py:516
  29.0 14.8 %collective-permute-start.9 = (f32[24,2,8,128]{3,2,1,0:T(8,128)S(1)}, f32[24,2,8,128]{3,2,1,0:T(8,128)S(1)}, u32[]{:S(2)}, u32[]{:S(2)}) collective-permute-start(f32[24,2,8,128]{3,2,1,0:T(8,128)S(1)} %get-tuple-element.33), channel_id=1, source_target_pairs={{0,6},{2,0},{4,2},{6,4},{8,14},{10,8},{12,10},{14,12},{16,18},{18,... | collective-permute-start | bytes 589832 | tf_op jit(solution)/shard_map/ppermute | solution.py:516
